TPU v7x, 32 devices: a whole 2x2x4 slice. The times are simulated.
32 devices in a mesh: dp: 8 (over y, x, core), fsdp: 4 (over z).
Axes of the slice: x: 2, y: 2, z: 4, core: 2. Of those that a mesh axis runs over, the one named last changes fastest.
Arguments:
- tokens: bfloat16 [32, 1024, 512], P('dp', 'fsdp'), may hold values from -6 to 6
- out_grad: bfloat16 [32, 1024, 512], P('dp', 'fsdp'), may hold values from -6 to 6
- segment_ids: int32 [32, 1024], P('dp', 'fsdp'), may hold values from 0 to 7, as said below
- key_mask: int32 [32, 1024], P('dp', 'fsdp'), may hold values from 0 to 1, as said below
- sent_task: int32 [32, 8], P('dp'), may hold values from 0 to 31, as said below
- task_experts: int32 [32, 2], replicated, may hold values from 0 to 7, all different within a row
- ln1_gain: bfloat16 [512], P(('dp', 'fsdp')), may hold values from 0.5 to 1.5
- ln1_bias: bfloat16 [512], P(('dp', 'fsdp')), may hold values from -1.1953125 to 1.1953125
- w_qkv: bfloat16 [512, 1536], P(('dp', 'fsdp')), may hold values from -0.25 to 0.25
- w_proj: bfloat16 [512, 512], P(('dp', 'fsdp')), may hold values from -1 to 1
- ln2_gain: bfloat16 [512], P(('dp', 'fsdp')), may hold values from 0.5 to 1.5
- ln2_bias: bfloat16 [512], P(('dp', 'fsdp')), may hold values from -1.1953125 to 1.1953125
- task_embed: bfloat16 [32, 512], P(None, ('dp', 'fsdp')), may hold values from -6 to 6
- w_gate: bfloat16 [512, 8], P(('dp', 'fsdp')), may hold values from -0.125 to 0.125
- w_up: bfloat16 [8, 512, 2048], P('dp', 'fsdp'), may hold values from -0.25 to 0.25
- b_up: bfloat16 [8, 2048], P('dp', 'fsdp'), may hold values from -0.59765625 to 0.59765625
- w_down: bfloat16 [8, 2048, 512], P('dp', 'fsdp'), may hold values from -0.125 to 0.125
- b_down: bfloat16 [8, 512], P('dp', 'fsdp'), may hold values from -0.59765625 to 0.59765625
Outputs:
- output: bfloat16 [32, 1024, 512], P('dp', 'fsdp')
- d_tokens: float32 [32, 1024, 512], P('dp', 'fsdp')
- d_ln1_gain: float32 [512], P(('dp', 'fsdp'))
- d_ln1_bias: float32 [512], P(('dp', 'fsdp'))
- d_w_qkv: float32 [512, 1536], P(('dp', 'fsdp'))
- d_w_proj: float32 [512, 512], P(('dp', 'fsdp'))
- d_ln2_gain: float32 [512], P(('dp', 'fsdp'))
- d_ln2_bias: float32 [512], P(('dp', 'fsdp'))
- d_task_embed: float32 [32, 512], P(None, ('dp', 'fsdp'))
- d_w_gate: float32 [512, 8], P(('dp', 'fsdp'))
- d_w_up: float32 [8, 512, 2048], P('dp', 'fsdp')
- d_b_up: float32 [8, 2048], P('dp', 'fsdp')
- d_w_down: float32 [8, 2048, 512], P('dp', 'fsdp')
- d_b_down: float32 [8, 512], P('dp', 'fsdp')
Inputs may be any that keep to these rules, and one draw needn't show every extreme that they name: `segment_ids`: never falling along a row. In each group of 4 rows that share an index of dp, one row holds a single sentence. `key_mask`: the first position of every sentence is 1. `sent_task`: entries past a row's last sentence are unused. The single-sentence rows all have the same task. `task_experts`: two different experts per task; every expert belongs to some task.
All inputs are finite; a program needn't handle non-finite values.
Results may differ from a plain program's by a relative error of at most 0.012.
Values may be sent and summed in bfloat16 or wider, within the bound.
A program may use at most 192 MiB of HBM per device.

v0:
```python
import jax
import jax.numpy as jnp
from jax import lax
from jax.sharding import PartitionSpec as P

HEADS = 8
HD = 64


exact = lax.Precision.HIGHEST


def layer_norm(values_in, gain_vec, shift_vec):
    centre = values_in - jnp.mean(values_in, axis=-1, keepdims=True)
    spread = jnp.mean(centre * centre, axis=-1, keepdims=True)
    return centre * lax.rsqrt(spread + 1e-05) * gain_vec + shift_vec


def allow_table(query_codes, key_codes):
    query_int = query_codes.astype(jnp.int32)
    key_int = key_codes.astype(jnp.int32)
    same_sentence = (query_int // 2)[:, :, None] == (key_int // 2)[:, None, :]
    return same_sentence & ((key_int % 2)[:, None, :] == 1)


def row_scores(query_row, key_row, allow_row):
    scores = (
        jnp.einsum("qhd,khd->hqk", query_row, key_row, preferred_element_type=jnp.float32) * 0.125
    )
    return jnp.where(allow_row[None], scores, -1000000000.0)


def attend_forward(queries, key_heads, value_heads, allowed):

    def one_row(parts):
        query_row, key_row, value_row, allow_row = parts
        scores = row_scores(query_row, key_row, allow_row)
        biggest = jnp.max(scores, axis=-1, keepdims=True)
        weights = jnp.exp(scores - biggest)
        row_total = jnp.sum(weights, axis=-1, keepdims=True)
        weights_low = (weights / row_total).astype(jnp.bfloat16)
        mixed_row = jnp.einsum(
            "hqk,khd->qhd", weights_low, value_row, preferred_element_type=jnp.float32
        )
        return (mixed_row.astype(jnp.bfloat16), (biggest + jnp.log(row_total))[..., 0])

    return lax.map(one_row, (queries, key_heads, value_heads, allowed))


def attend_backward(queries, key_heads, value_heads, allowed, logsum, grad_out):

    def one_row(parts):
        query_row, key_row, value_row, allow_row, logsum_row, grad_row = parts
        scores = row_scores(query_row, key_row, allow_row)
        weights = jnp.exp(scores - logsum_row[..., None])
        grad_weights = jnp.einsum(
            "qhd,khd->hqk", grad_row, value_row, preferred_element_type=jnp.float32
        )
        inner = jnp.sum(weights * grad_weights, axis=-1, keepdims=True)
        grad_scores = (weights * (grad_weights - inner)).astype(jnp.bfloat16)
        grad_query = (
            jnp.einsum("hqk,khd->qhd", grad_scores, key_row, preferred_element_type=jnp.float32)
            * 0.125
        )
        grad_key = (
            jnp.einsum("hqk,qhd->khd", grad_scores, query_row, preferred_element_type=jnp.float32)
            * 0.125
        )
        grad_value = jnp.einsum(
            "hqk,qhd->khd",
            weights.astype(jnp.bfloat16),
            grad_row,
            preferred_element_type=jnp.float32,
        )
        return (grad_query, grad_key, grad_value)

    return lax.map(one_row, (queries, key_heads, value_heads, allowed, logsum, grad_out))


def shards(
    tokens,
    out_grad,
    segment_ids,
    key_mask,
    sent_task,
    task_experts,
    ln1_gain,
    ln1_bias,
    w_qkv,
    w_proj,
    ln2_gain,
    ln2_bias,
    task_embed,
    w_gate,
    w_up,
    b_up,
    w_down,
    b_down,
):
    row_count, piece_len, model_width = tokens.shape
    tok_count = row_count * piece_len
    gain_one, bias_one, qkv_full, proj_full, gain_two, bias_two, embed_full, router_full = (
        lax.all_gather(ln1_gain, ("dp", "fsdp"), axis=0, tiled=True),
        lax.all_gather(ln1_bias, ("dp", "fsdp"), axis=0, tiled=True),
        lax.all_gather(w_qkv, ("dp", "fsdp"), axis=0, tiled=True),
        lax.all_gather(w_proj, ("dp", "fsdp"), axis=0, tiled=True),
        lax.all_gather(ln2_gain, ("dp", "fsdp"), axis=0, tiled=True),
        lax.all_gather(ln2_bias, ("dp", "fsdp"), axis=0, tiled=True),
        lax.all_gather(task_embed, ("dp", "fsdp"), axis=1, tiled=True),
        lax.all_gather(w_gate, ("dp", "fsdp"), axis=0, tiled=True),
    )
    up_full, up_bias, down_full, down_bias = (
        lax.all_gather(w_up, "fsdp", axis=1, tiled=True),
        lax.all_gather(b_up, "fsdp", axis=1, tiled=True),
        lax.all_gather(w_down, "fsdp", axis=1, tiled=True),
        lax.all_gather(b_down, "fsdp", axis=1, tiled=True),
    )
    up_full = up_full[0]
    down_full = down_full[0]
    up_bias_f = up_bias[0].astype(jnp.float32)
    down_bias_f = down_bias[0].astype(jnp.float32)
    experts_count = router_full.shape[1]
    task_count = embed_full.shape[0]
    capacity = 4 * tok_count // experts_count
    inputs = tokens.astype(jnp.float32).reshape(tok_count, model_width)
    normed, norm_back = jax.vjp(
        layer_norm, inputs, gain_one.astype(jnp.float32), bias_one.astype(jnp.float32)
    )
    normed_low = normed.astype(jnp.bfloat16)
    projected = jnp.dot(normed_low, qkv_full, preferred_element_type=jnp.float32).astype(
        jnp.bfloat16
    )
    projected = projected.reshape(row_count, piece_len, 3, HEADS, HD)
    queries = projected[:, :, 0]
    key_heads = projected[:, :, 1]
    value_heads = projected[:, :, 2]
    row_codes = (2 * segment_ids + key_mask).astype(jnp.bfloat16)
    keys_all, values_all, codes_all = (
        lax.all_gather(key_heads, "fsdp", axis=1, tiled=True),
        lax.all_gather(value_heads, "fsdp", axis=1, tiled=True),
        lax.all_gather(row_codes, "fsdp", axis=1, tiled=True),
    )
    allowed = allow_table(row_codes, codes_all)
    attended, logsum = attend_forward(queries, keys_all, values_all, allowed)
    attended_flat = attended.reshape(tok_count, model_width)
    hidden = inputs + jnp.dot(attended_flat, proj_full, preferred_element_type=jnp.float32)
    normed_two, norm_two_back = jax.vjp(
        layer_norm, hidden, gain_two.astype(jnp.float32), bias_two.astype(jnp.float32)
    )
    normed_two_low = normed_two.astype(jnp.bfloat16)
    choose = (task_experts[:, :, None] == jnp.arange(experts_count)[None, None, :]).astype(
        jnp.float32
    )

    def gate_values(embed_in, router_in):
        logits = jnp.einsum(
            "te,tke->tk", jnp.dot(embed_in, router_in, precision=exact), choose, precision=exact
        )
        return jax.nn.softmax(logits, axis=-1)

    gate_probs, gate_back = jax.vjp(
        gate_values, embed_full.astype(jnp.float32), router_full.astype(jnp.float32)
    )
    segment_hot = (segment_ids[:, :, None] == jnp.arange(sent_task.shape[1])[None, None, :]).astype(
        jnp.int32
    )
    task_tok = jnp.sum(segment_hot * sent_task[:, None, :], axis=-1).reshape(tok_count)
    task_hot = (task_tok[:, None] == jnp.arange(task_count)[None, :]).astype(jnp.float32)
    gate_tok = jnp.dot(task_hot, gate_probs, precision=exact)
    expert_tok = jnp.sum(task_hot.astype(jnp.int32)[:, :, None] * task_experts[None], axis=1)
    copy_expert = expert_tok.T.reshape(-1)
    one_hot = (copy_expert[:, None] == jnp.arange(experts_count)[None, :]).astype(jnp.int32)
    rank = jnp.sum((jnp.cumsum(one_hot, axis=0) - one_hot) * one_hot, axis=-1)
    kept_copy = rank < capacity
    slot_index = jnp.where(kept_copy, copy_expert * capacity + rank, experts_count * capacity)
    send_rows = (
        jnp.zeros((experts_count * capacity + 1, model_width), jnp.bfloat16)
        .at[slot_index]
        .set(jnp.tile(normed_two_low, (2, 1)))
    )
    send_rows = send_rows[:-1].reshape(experts_count, capacity, model_width)
    received = lax.all_to_all(send_rows, "dp", split_axis=0, concat_axis=0, tiled=True)
    slot_total = received.shape[0] * received.shape[1]
    block_rows = min(512, slot_total)
    block_count = slot_total // block_rows
    slot_blocks = received.reshape(block_count, block_rows, model_width)

    def expert_forward(slot_rows):
        pre_act = jnp.dot(slot_rows, up_full, preferred_element_type=jnp.float32) + up_bias_f
        activated = jax.nn.gelu(pre_act, approximate=True).astype(jnp.bfloat16)
        return (
            jnp.dot(activated, down_full, preferred_element_type=jnp.float32) + down_bias_f
        ).astype(jnp.bfloat16)

    produced = lax.map(expert_forward, slot_blocks).reshape(received.shape)
    returned = lax.all_to_all(produced, "dp", split_axis=0, concat_axis=0, tiled=True)
    return_pad = jnp.concatenate(
        [returned.reshape(-1, model_width), jnp.zeros((1, model_width), jnp.bfloat16)], axis=0
    )
    copies = jnp.take(return_pad, slot_index, axis=0).reshape(2, tok_count, model_width)
    kept_float = kept_copy.reshape(2, tok_count).astype(jnp.float32)
    copy_weight = gate_tok.T * kept_float
    mixed_rows = (
        hidden
        + copy_weight[0][:, None] * copies[0].astype(jnp.float32)
        + copy_weight[1][:, None] * copies[1].astype(jnp.float32)
    )
    output = mixed_rows.astype(jnp.bfloat16).reshape(tokens.shape)
    grad_mixed = out_grad.astype(jnp.float32).reshape(tok_count, model_width)
    grad_copies = (copy_weight[:, :, None] * grad_mixed[None]).astype(jnp.bfloat16)
    grad_gate_copy = jnp.sum(copies.astype(jnp.float32) * grad_mixed[None], axis=-1) * kept_float
    grad_send = (
        jnp.zeros((experts_count * capacity + 1, model_width), jnp.bfloat16)
        .at[slot_index]
        .set(grad_copies.reshape(-1, model_width))
    )
    grad_send = grad_send[:-1].reshape(experts_count, capacity, model_width)
    grad_received = lax.all_to_all(grad_send, "dp", split_axis=0, concat_axis=0, tiled=True)

    def expert_backward(totals, parts):
        slot_rows, grad_rows = parts
        pre_act = jnp.dot(slot_rows, up_full, preferred_element_type=jnp.float32) + up_bias_f
        activated, gelu_back = jax.vjp(
            lambda values_in: jax.nn.gelu(values_in, approximate=True), pre_act
        )
        activated_low = activated.astype(jnp.bfloat16)
        grad_act = jnp.dot(grad_rows, down_full.T, preferred_element_type=jnp.float32)
        grad_pre = gelu_back(grad_act)[0].astype(jnp.bfloat16)
        grad_inputs_slot = jnp.dot(grad_pre, up_full.T, preferred_element_type=jnp.float32).astype(
            jnp.bfloat16
        )
        totals = (
            totals[0] + jnp.dot(slot_rows.T, grad_pre, preferred_element_type=jnp.float32),
            totals[1] + jnp.sum(grad_pre.astype(jnp.float32), axis=0),
            totals[2] + jnp.dot(activated_low.T, grad_rows, preferred_element_type=jnp.float32),
            totals[3] + jnp.sum(grad_rows.astype(jnp.float32), axis=0),
        )
        return (totals, grad_inputs_slot)

    start_totals = (
        jnp.zeros(up_full.shape, jnp.float32),
        jnp.zeros(up_bias_f.shape, jnp.float32),
        jnp.zeros(down_full.shape, jnp.float32),
        jnp.zeros(down_bias_f.shape, jnp.float32),
    )
    totals, grad_slots = lax.scan(
        expert_backward,
        start_totals,
        (slot_blocks, grad_received.reshape(block_count, block_rows, model_width)),
    )
    grad_back = lax.all_to_all(
        grad_slots.reshape(received.shape), "dp", split_axis=0, concat_axis=0, tiled=True
    )
    grad_pad = jnp.concatenate(
        [grad_back.reshape(-1, model_width), jnp.zeros((1, model_width), jnp.bfloat16)], axis=0
    )
    grad_taken = (
        jnp.take(grad_pad, slot_index, axis=0)
        .reshape(2, tok_count, model_width)
        .astype(jnp.float32)
    )
    grad_normed_two = grad_taken[0] + grad_taken[1]
    grad_up, grad_up_bias, grad_down, grad_down_bias = (
        lax.psum_scatter(
            totals[0][None].astype(jnp.bfloat16), "fsdp", scatter_dimension=1, tiled=True
        ).astype(jnp.float32),
        lax.psum_scatter(
            totals[1][None].astype(jnp.bfloat16), "fsdp", scatter_dimension=1, tiled=True
        ).astype(jnp.float32),
        lax.psum_scatter(
            totals[2][None].astype(jnp.bfloat16), "fsdp", scatter_dimension=1, tiled=True
        ).astype(jnp.float32),
        lax.psum_scatter(
            totals[3][None].astype(jnp.bfloat16), "fsdp", scatter_dimension=1, tiled=True
        ).astype(jnp.float32),
    )
    grad_hidden_part, grad_gain_two, grad_bias_two = norm_two_back(grad_normed_two)
    grad_hidden = grad_mixed + grad_hidden_part
    grad_branch = grad_hidden.astype(jnp.bfloat16)
    grad_proj = jnp.dot(attended_flat.T, grad_branch, preferred_element_type=jnp.float32)
    grad_attended = jnp.dot(grad_branch, proj_full.T, preferred_element_type=jnp.float32).astype(
        jnp.bfloat16
    )
    grad_attended = grad_attended.reshape(row_count, piece_len, HEADS, HD)
    part_query, part_key, part_value = attend_backward(
        queries, keys_all, values_all, allowed, logsum, grad_attended
    )
    summed_key, summed_value = (
        lax.psum_scatter(
            part_key.astype(jnp.bfloat16), "fsdp", scatter_dimension=1, tiled=True
        ).astype(jnp.float32),
        lax.psum_scatter(
            part_value.astype(jnp.bfloat16), "fsdp", scatter_dimension=1, tiled=True
        ).astype(jnp.float32),
    )
    grad_query = part_query.astype(jnp.bfloat16)
    grad_key = summed_key.astype(jnp.bfloat16)
    grad_value = summed_value.astype(jnp.bfloat16)
    grad_projected = jnp.stack([grad_query, grad_key, grad_value], axis=2).reshape(
        tok_count, 3 * model_width
    )
    grad_qkv_weight = jnp.dot(normed_low.T, grad_projected, preferred_element_type=jnp.float32)
    grad_normed = jnp.dot(grad_projected, qkv_full.T, preferred_element_type=jnp.float32)
    grad_inputs, grad_gain_one, grad_bias_one = norm_back(grad_normed)
    grad_tokens = (grad_hidden + grad_inputs).reshape(tokens.shape)
    grad_gate_task = jnp.dot(task_hot.T, grad_gate_copy.T, precision=exact)
    grad_embed, grad_router = gate_back(grad_gate_task)
    reduced = (
        lax.psum_scatter(grad_gain_one, ("dp", "fsdp"), scatter_dimension=0, tiled=True),
        lax.psum_scatter(grad_bias_one, ("dp", "fsdp"), scatter_dimension=0, tiled=True),
        lax.psum_scatter(grad_qkv_weight, ("dp", "fsdp"), scatter_dimension=0, tiled=True),
        lax.psum_scatter(grad_proj, ("dp", "fsdp"), scatter_dimension=0, tiled=True),
        lax.psum_scatter(grad_gain_two, ("dp", "fsdp"), scatter_dimension=0, tiled=True),
        lax.psum_scatter(grad_bias_two, ("dp", "fsdp"), scatter_dimension=0, tiled=True),
        lax.psum_scatter(grad_embed, ("dp", "fsdp"), scatter_dimension=1, tiled=True),
        lax.psum_scatter(grad_router, ("dp", "fsdp"), scatter_dimension=0, tiled=True),
    )
    return (
        output,
        grad_tokens,
        reduced[0],
        reduced[1],
        reduced[2],
        reduced[3],
        reduced[4],
        reduced[5],
        reduced[6],
        reduced[7],
        grad_up,
        grad_up_bias,
        grad_down,
        grad_down_bias,
    )


def solution(mesh):
    placed = (
        P("dp", "fsdp", None),
        P("dp", "fsdp", None),
        P("dp", "fsdp"),
        P("dp", "fsdp"),
        P("dp", None),
        P(),
        P(("dp", "fsdp")),
        P(("dp", "fsdp")),
        P(("dp", "fsdp"), None),
        P(("dp", "fsdp"), None),
        P(("dp", "fsdp")),
        P(("dp", "fsdp")),
        P(None, ("dp", "fsdp")),
        P(("dp", "fsdp"), None),
        P("dp", "fsdp", None),
        P("dp", "fsdp"),
        P("dp", "fsdp", None),
        P("dp", "fsdp"),
    )
    return jax.shard_map(
        shards,
        mesh=mesh,
        in_specs=placed,
        out_specs=(
            P("dp", "fsdp", None),
            P("dp", "fsdp", None),
            P(("dp", "fsdp")),
            P(("dp", "fsdp")),
            P(("dp", "fsdp"), None),
            P(("dp", "fsdp"), None),
            P(("dp", "fsdp")),
            P(("dp", "fsdp")),
            P(None, ("dp", "fsdp")),
            P(("dp", "fsdp"), None),
            P("dp", "fsdp", None),
            P("dp", "fsdp"),
            P("dp", "fsdp", None),
            P("dp", "fsdp"),
        ),
        check_vma=False,
    )
```

profile of v0, /device:TPU:25, one launch (start us, length us, event | category | flops | bytes accessed | tf_op | source)
XLA Modules:
  0.0 1822.8 jit_solution(15222776655426489141)
XLA Ops:
  11.4 38.4 %all-reduce.11 = (bf16[512]{0:T(512)(128)(2,1)S(1)}, bf16[512]{0:T(512)(128)(2,1)S(1)}, bf16[512]{0:T(512)(128)(2,1)S(1)}, bf16[512]{0:T(512)(128)(2,1)S(1)}) all-reduce(bf16[512]{0:T(512)(128)(2,1)S(1)} %dynamic-update-slice.1, bf16[512]{0:T(512)(128)(2,1)S(1)} %dynamic-update-slice, ...), channel_id=1, replica_groups=mesh['dp'=8,'fsdp'=4] {'dp','fsdp'}, use_global_device_ids=true, to_apply=%add.3 | all-reduce | flops 2048 | bytes 8192
  57.4 8.9 all-gather.9.cloned.1.call-done
  81.5 8.3 all_gather.49
  89.9 113.6 %all_gather.51 = bf16[512,512]{1,0:T(8,128)(2,1)} all-gather(bf16[16,512]{1,0:T(8,128)(2,1)S(1)} %copy-done.56), channel_id=1, replica_groups=mesh['dp'=8,'fsdp'=4] {'dp','fsdp'}, dimensions={0}, use_global_device_ids=true | all-gather | bytes 540672 | tf_op jit(solution)/shard_map/all_gather | solution.py:106
  213.5 34.8 %all-gather.17.cloned.1.call-done = bf16[4,1024,1,8,64]{1,0,4,3,2:T(4,128)(2,1)} async-done(((bf16[4,256,1,8,64]{1,0,4,3,2:T(4,128)(2,1)}), bf16[4,1024,1,8,64]{1,0,4,3,2:T(4,128)(2,1)}) %all-gather.17.cloned.1.call-update) | async-done | bytes 4194320 | tf_op jit(solution)/shard_map/all_gather | solution.py:139
  253.9 37.2 %while.57 = (s32[]{:T(128)}, bf16[4,256,8,64]{1,3,2,0:T(8,128)(2,1)S(1)}, f32[4,8,256]{2,1,0:T(8,128)}, bf16[4,1024,8,64]{1,3,2,0:T(8,128)(2,1)}, pred[4,256,102...) while((s32[]{:T(128)}, ...), condition=%wide.region_5.6_spmd, body=%wide.region_2.5_spmd.sunk | while | flops 562165760 | bytes 29166168 | solution.py:47
  296.3 12.4 scatter_custom_fusion
  319.3 9.8 all_gather.57
  329.1 9.0 all_gather.59
  338.1 28.8 %all-gather.13.cloned.1.call-done = bf16[1,2048,512]{2,1,0:T(8,128)(2,1)} async-done(((bf16[1,512,512]{2,1,0:T(8,128)(2,1)}), bf16[1,2048,512]{2,1,0:T(8,128)(2,1)}) %all-gather.13.cloned.1.call-update) | async-done | bytes 2097168 | tf_op jit(solution)/shard_map/all_gather | solution.py:115
  369.2 42.5 %while.58 = (s32[]{:T(128)}, bf16[8,512,512]{2,1,0:T(8,128)(2,1)}, bf16[8,512,512]{2,1,0:T(8,128)(2,1)}, bf16[512,2048]{1,0:T(8,128)(2,1)S(1)}, f32[2048]{0:T(10...) while((s32[]{:T(128)}, bf16[8,512,512]{2,1,0:T(8,128)(2,1)}, ...), condition=%wide.region_17.18_spmd, body=%wide.region_16.17_spmd.sunk | while | flops 2158493696 | bytes 5254229 | solution.py:195
  417.5 59.1 %all-gather.2 = bf16[32,16,8]{1,2,0:T(8,128)(2,1)S(1)} all-gather(bf16[1,16,8]{1,2,0:T(8,128)(2,1)S(1)} %bitcast.381), channel_id=1, replica_groups=mesh['dp'=8,'fsdp'=4] {'dp','fsdp'}, dimensions={0}, use_global_device_ids=true | all-gather | bytes 8448 | tf_op jit(solution)/shard_map/all_gather | solution.py:110
  476.8 64.9 %all_gather.52 = bf16[32,512]{0,1:T(8,128)(2,1)S(1)} all-gather(bf16[32,16]{0,1:T(8,128)(2,1)S(1)} %copy-done.66), channel_id=1, replica_groups=mesh['dp'=8,'fsdp'=4] {'dp','fsdp'}, dimensions={1}, use_global_device_ids=true | all-gather | bytes 33792 | tf_op jit(solution)/shard_map/all_gather | solution.py:109
  549.3 12.4 gather_fusion
  567.5 12.6 scatter_custom_fusion.1
  584.5 12.6 all-to-all-start.2
  597.1 45.5 %all-to-all-done.2 = bf16[8,512,512]{2,1,0:T(8,128)(2,1)} async-done(((bf16[8,512,512]{2,1,0:T(8,128)(2,1)}), bf16[8,512,512]{2,1,0:T(8,128)(2,1)}, u32[]{:S(2)}, u32[]{:S(2)}) %all-to-all-start.2) | async-done | bytes 4194336 | tf_op jit(solution)/shard_map/all_to_all | solution.py:218
  645.0 208.5 %while.60 = (s32[]{:T(128)}, f32[512,2048]{1,0:T(8,128)}, f32[2048]{0:T(1024)S(1)}, f32[2048,512]{1,0:T(8,128)}, f32[512]{0:T(512)S(1)}, /*index=5*/bf16[8,512,5...) while((s32[]{:T(128)}, f32[512,2048]{1,0:T(8,128)}, ...), condition=%wide.region_22.24_spmd.clone, body=%wide.region_19.23_spmd.clone.sunk | while | flops 5408295424 | bytes 129035064 | solution.py:246
  861.6 45.6 %all-to-all-done.3 = bf16[8,512,512]{2,1,0:T(8,128)(2,1)} async-done(((bf16[8,512,512]{2,1,0:T(8,128)(2,1)}), bf16[8,512,512]{2,1,0:T(8,128)(2,1)}, u32[]{:S(2)}, u32[]{:S(2)}) %all-to-all-start.3) | async-done | bytes 4194336 | tf_op jit(solution)/shard_map/all_to_all | solution.py:251
  911.6 10.5 gather_fusion.1
  937.4 79.8 %while.59 = (s32[]{:T(128)}, bf16[4,256,8,64]{1,3,2,0:T(8,128)(2,1)}, bf16[4,1024,8,64]{1,3,2,0:T(8,128)(2,1)}, bf16[4,1024,8,64]{1,3,2,0:T(8,128)(2,1)}, bf16[4...) while((s32[]{:T(128)}, ...), condition=%wide.region_27.29_spmd, body=%wide.region_25.28_spmd.sunk | while | flops 1374287872 | bytes 85783752 | solution.py:77
  1036.4 61.1 %reduce-scatter.17.cloned.1.call-done = bf16[4,256,8,64]{1,3,2,0:T(8,128)(2,1)} async-done(((bf16[4,1024,8,64]{1,3,2,0:T(8,128)(2,1)}), bf16[4,256,8,64]{1,3,2,0:T(8,128)(2,1)}) %reduce-scatter.17.cloned.1.call-update) | async-done | bytes 1048592 | tf_op jit(solution)/shard_map/reduce_scatter | solution.py:289
  1097.5 79.7 %reduce-scatter.19.cloned.1.call-done = bf16[4,256,8,64]{1,3,2,0:T(8,128)(2,1)} async-done(((bf16[4,1024,8,64]{1,3,2,0:T(8,128)(2,1)}), bf16[4,256,8,64]{1,3,2,0:T(8,128)(2,1)}) %reduce-scatter.19.cloned.1.call-update) | async-done | bytes 1048592 | tf_op jit(solution)/shard_map/reduce_scatter | solution.py:292
  1188.3 111.3 %reduce-scatter.31.cloned.1.call-done = f32[16,8]{1,0:T(8,128)} async-done(((f32[512,8]{1,0:T(8,128)}), f32[16,8]{1,0:T(8,128)}) %reduce-scatter.31.cloned.1.call-update) | async-done | bytes 528
  1300.9 26.4 %reduce-scatter.35.cloned.1.call-done = bf16[128,1]{1,0:T(8,128)(2,1)} async-done(((bf16[512,1]{1,0:T(8,128)(2,1)}), bf16[128,1]{1,0:T(8,128)(2,1)}) %reduce-scatter.35.cloned.1.call-update) | async-done | bytes 272
  1328.7 21.5 %reduce-scatter.33.cloned.1.call-done = bf16[512,1]{1,0:T(8,128)(2,1)} async-done(((bf16[2048,1]{1,0:T(8,128)(2,1)}), bf16[512,1]{1,0:T(8,128)(2,1)}) %reduce-scatter.33.cloned.1.call-update) | async-done | bytes 1040
  1351.8 45.4 %reduce-scatter.27.cloned.1.call-done = bf16[1,128,2048]{2,1,0:T(8,128)(2,1)} async-done(((bf16[1,512,2048]{2,1,0:T(8,128)(2,1)}), bf16[1,128,2048]{2,1,0:T(8,128)(2,1)}) %reduce-scatter.27.cloned.1.call-update) | async-done | bytes 524304 | tf_op jit(solution)/shard_map/reduce_scatter | solution.py:264
  1399.3 43.3 %reduce-scatter.29.cloned.1.call-done = bf16[1,512,512]{2,1,0:T(8,128)(2,1)} async-done(((bf16[1,2048,512]{2,1,0:T(8,128)(2,1)}), bf16[1,512,512]{2,1,0:T(8,128)(2,1)}) %reduce-scatter.29.cloned.1.call-update) | async-done | bytes 524304 | tf_op jit(solution)/shard_map/reduce_scatter | solution.py:270
  1452.0 39.9 %all-reduce.10 = (f32[512]{0:T(512)S(1)}, f32[512]{0:T(512)S(1)}, f32[512]{0:T(512)S(1)}, f32[512]{0:T(512)S(1)}) all-reduce(f32[512]{0:T(512)S(1)} %get-tuple-element.395, f32[512]{0:T(512)S(1)} %get-tuple-element.398, f32[512]{0:T(512)S(1)} %get-tuple-element.393, ...), channel_id=6, replica_groups=mesh['dp'=8,'fsdp'=4] {'dp','fsdp'}, use_global_device_ids=true, to_apply=%region_33.35.clone | all-reduce | flops 2048 | bytes 16384
  1497.6 68.0 %reduce-scatter.25.cloned.1.call-done = f32[32,16]{0,1:T(8,128)} async-done(((f32[32,512]{0,1:T(8,128)}), f32[32,16]{0,1:T(8,128)}) %reduce-scatter.25.cloned.1.call-update) | async-done | bytes 2064 | tf_op jit(solution)/shard_map/reduce_scatter | solution.py:315
  1565.6 134.8 %reduce-scatter.23.cloned.1.call-done = f32[16,512]{1,0:T(8,128)} async-done(((f32[512,512]{1,0:T(8,128)}), f32[16,512]{1,0:T(8,128)}) %reduce-scatter.23.cloned.1.call-update) | async-done | bytes 32784 | tf_op jit(solution)/shard_map/reduce_scatter | solution.py:312
  1700.5 115.4 %reduce-scatter.21.cloned.1.call-done = f32[16,1536]{1,0:T(8,128)} async-done(((f32[512,1536]{1,0:T(8,128)}), f32[16,1536]{1,0:T(8,128)}) %reduce-scatter.21.cloned.1.call-update) | async-done | bytes 98320 | tf_op jit(solution)/shard_map/reduce_scatter | solution.py:311
  (549 shorter events, 532.5 us)
Async XLA Ops:
  7.2 59.1 %all-gather.9.cloned.1.call-start = ((), (), s32[]{:S(2)}) async-start(), calls=%async_computation.14 | async-start | bytes 1622016 | tf_op jit(solution)/shard_map/all_gather | solution.py:105
  7.9 199.9 %all-gather.15.cloned.1.call-start = ((), (), s32[]{:S(2)}) async-start(), calls=%async_computation.24 | async-start | bytes 5242880 | tf_op jit(solution)/shard_map/all_gather | solution.py:140
  77.6 125.9 %copy-start.69 = (s32[4,8]{1,0:T(4,128)S(1)}, s32[4,8]{1,0:T(4,128)}, u32[]{:S(2)}) copy-start(s32[4,8]{1,0:T(4,128)} %param.32) | copy-start | bytes 388
  77.6 126.1 %copy-start.64 = (s32[32,2]{0,1:T(2,128)S(1)}, s32[32,2]{0,1:T(2,128)}, u32[]{:S(2)}) copy-start(s32[32,2]{0,1:T(2,128)} %param.33) | copy-start | bytes 772
  80.1 127.5 %copy-start.19 = (bf16[4,256,8,64]{1,0,3,2:T(4,128)(2,1)S(1)}, bf16[4,256,8,64]{1,0,3,2:T(4,128)(2,1)}, u32[]{:S(2)}) copy-start(bf16[4,256,8,64]{1,0,3,2:T(4,128)(2,1)} %get-tuple-element.492) | copy-start | bytes 3145732
  80.2 168.1 %all-gather.17.cloned.1.call-start = ((), (), s32[]{:S(2)}) async-start(), calls=%async_computation.25 | async-start | bytes 5242880 | tf_op jit(solution)/shard_map/all_gather | solution.py:139
  80.9 257.2 %all-gather.11.cloned.1.call-start = ((), (), s32[]{:S(2)}) async-start(), calls=%async_computation.15 | async-start | bytes 2621440 | tf_op jit(solution)/shard_map/all_gather | solution.py:113
  203.5 91.4 %copy-start.50 = (f32[512]{0:T(512)}, f32[512]{0:T(512)S(1)}, u32[]{:S(2)}) copy-start(f32[512]{0:T(512)S(1)} %convert_element_type.216) | copy-start | bytes 6148
  203.6 339.3 %copy-start.58 = (s32[1,2,4,128]{3,1,2,0:T(2,128)}, s32[1,2,4,128]{3,1,2,0:T(2,128)S(1)}, u32[]{:S(2)}) copy-start(s32[1,2,4,128]{3,1,2,0:T(2,128)S(1)} %copy.99) | copy-start | bytes 12292
  313.1 15.9 copy-start.74
  313.1 53.7 %all-to-all-start = ((bf16[8,512,512]{2,1,0:T(8,128)(2,1)}), bf16[8,512,512]{2,1,0:T(8,128)(2,1)}, u32[]{:S(2)}, u32[]{:S(2)}) async-start(bf16[8,512,512]{2,1,0:T(8,128)(2,1)} %bitcast.334), calls=%async_computation | async-start | bytes 8388608 | tf_op jit(solution)/shard_map/all_to_all | solution.py:182
  318.7 48.1 %all-gather.13.cloned.1.call-start = ((), (), s32[]{:S(2)}) async-start(), calls=%async_computation.16 | async-start | bytes 2621440 | tf_op jit(solution)/shard_map/all_gather | solution.py:115
  338.1 31.1 %copy-start.2 = (bf16[1,512,2048]{2,1,0:T(8,128)(2,1)S(1)}, bf16[1,512,2048]{2,1,0:T(8,128)(2,1)}, u32[]{:S(2)}) copy-start(bf16[1,512,2048]{2,1,0:T(8,128)(2,1)} %all-gather.11.cloned.1.call-done) | copy-start | bytes 6291460
  411.7 65.1 %copy-start.66 = (bf16[32,16]{0,1:T(8,128)(2,1)S(1)}, bf16[32,16]{0,1:T(8,128)(2,1)}, u32[]{:S(2)}) copy-start(bf16[32,16]{0,1:T(8,128)(2,1)} %param.40) | copy-start | bytes 3076
  411.7 131.4 %copy-start.11 = (bf16[4,256,512]{2,1,0:T(8,128)(2,1)S(1)}, bf16[4,256,512]{2,1,0:T(8,128)(2,1)}, u32[]{:S(2)}) copy-start(bf16[4,256,512]{2,1,0:T(8,128)(2,1)} %param.29) | copy-start | bytes 3145732
  411.7 133.1 %all-to-all-start.1 = ((bf16[8,512,512]{2,1,0:T(8,128)(2,1)}), bf16[8,512,512]{2,1,0:T(8,128)(2,1)}, u32[]{:S(2)}, u32[]{:S(2)}) async-start(bf16[8,512,512]{2,1,0:T(8,128)(2,1)} %get-tuple-element.286), calls=%async_computation.1 | async-start | bytes 8388608 | tf_op jit(solution)/shard_map/all_to_all | solution.py:196
  417.5 131.8 %copy-start.40 = (s32[32,2]{1,0:T(8,128)}, s32[32,2]{1,0:T(8,128)S(1)}, u32[]{:S(2)}) copy-start(s32[32,2]{1,0:T(8,128)S(1)} %copy.72) | copy-start | bytes 772
  417.5 131.7 %copy-start.67 = (pred[2,1024]{1,0:T(4,128)(4,1)}, pred[2,1024]{1,0:T(4,128)(4,1)S(1)}, u32[]{:S(2)}) copy-start(pred[2,1024]{1,0:T(4,128)(4,1)S(1)} %lt.55) | copy-start | bytes 6148
  476.8 72.4 %copy-start.32 = (bf16[512,8]{0,1:T(8,128)(2,1)}, bf16[512,8]{0,1:T(8,128)(2,1)S(1)}, u32[]{:S(2)}) copy-start(bf16[512,8]{0,1:T(8,128)(2,1)S(1)} %reshape.402) | copy-start | bytes 24580
  584.5 58.2 %all-to-all-start.2 = ((bf16[8,512,512]{2,1,0:T(8,128)(2,1)}), bf16[8,512,512]{2,1,0:T(8,128)(2,1)}, u32[]{:S(2)}, u32[]{:S(2)}) async-start(bf16[8,512,512]{2,1,0:T(8,128)(2,1)} %bitcast.335), calls=%async_computation.2 | async-start | bytes 8388608 | tf_op jit(solution)/shard_map/all_to_all | solution.py:218
  853.5 53.7 %all-to-all-start.3 = ((bf16[8,512,512]{2,1,0:T(8,128)(2,1)}), bf16[8,512,512]{2,1,0:T(8,128)(2,1)}, u32[]{:S(2)}, u32[]{:S(2)}) async-start(bf16[8,512,512]{2,1,0:T(8,128)(2,1)} %get-tuple-element.287), calls=%async_computation.3 | async-start | bytes 8388608 | tf_op jit(solution)/shard_map/all_to_all | solution.py:251
  861.6 236.0 %reduce-scatter.17.cloned.1.call-start = ((), (), s32[]{:S(2)}) async-start(), calls=%async_computation.17 | async-start | bytes 5242880 | tf_op jit(solution)/shard_map/reduce_scatter | solution.py:289
  1017.2 160.1 %reduce-scatter.19.cloned.1.call-start = ((), (), s32[]{:S(2)}) async-start(), calls=%async_computation.18 | async-start | bytes 5242880 | tf_op jit(solution)/shard_map/reduce_scatter | solution.py:292
  1018.0 281.6 %reduce-scatter.31.cloned.1.call-start = ((), (), s32[]{:S(2)}) async-start(), calls=%async_computation.26 | async-start | bytes 270336
  1019.9 307.5 %reduce-scatter.35.cloned.1.call-start = ((), (), s32[]{:S(2)}) async-start(), calls=%async_computation.28 | async-start | bytes 163840
  1020.7 329.5 %reduce-scatter.33.cloned.1.call-start = ((), (), s32[]{:S(2)}) async-start(), calls=%async_computation.27 | async-start | bytes 655360
  1022.0 375.2 %reduce-scatter.27.cloned.1.call-start = ((), (), s32[]{:S(2)}) async-start(), calls=%async_computation.22 | async-start | bytes 2621440 | tf_op jit(solution)/shard_map/reduce_scatter | solution.py:264
  1025.9 416.8 %reduce-scatter.29.cloned.1.call-start = ((), (), s32[]{:S(2)}) async-start(), calls=%async_computation.23 | async-start | bytes 2621440 | tf_op jit(solution)/shard_map/reduce_scatter | solution.py:270
  1030.5 535.2 %reduce-scatter.25.cloned.1.call-start = ((), (), s32[]{:S(2)}) async-start(), calls=%async_computation.21 | async-start | bytes 270336 | tf_op jit(solution)/shard_map/reduce_scatter | solution.py:315
  1031.6 668.8 %reduce-scatter.23.cloned.1.call-start = ((), (), s32[]{:S(2)}) async-start(), calls=%async_computation.20 | async-start | bytes 1081344 | tf_op jit(solution)/shard_map/reduce_scatter | solution.py:312
  1034.9 780.9 %reduce-scatter.21.cloned.1.call-start = ((), (), s32[]{:S(2)}) async-start(), calls=%async_computation.19 | async-start | bytes 3244032 | tf_op jit(solution)/shard_map/reduce_scatter | solution.py:311
  1188.3 256.6 %copy-start.37 = (f32[1,2,4,128]{3,1,2,0:T(2,128)S(1)}, f32[1,2,4,128]{3,1,2,0:T(2,128)}, u32[]{:S(2)}) copy-start(f32[1,2,4,128]{3,1,2,0:T(2,128)} %copy-done.36) | copy-start | bytes 12292
  (114 other events, 399.1 us)
Sparse Core Ops, SparseCore 0:
  10.9 55.3 all-gather.8
  80.3 83.5 all-gather.14
  166.0 82.2 all-gather.16
  249.7 46.0 all-gather.10
  320.8 46.0 all-gather.12
  1017.3 80.1 reduce-scatter.16
  1099.9 77.2 reduce-scatter.18
  1179.5 120.0 reduce-scatter.30
  1301.9 25.4 reduce-scatter.34
  1329.5 20.6 reduce-scatter.32
  1353.1 44.0 reduce-scatter.26
  1399.5 43.1 reduce-scatter.28
  1445.5 120.0 reduce-scatter.24
  1568.4 132.0 reduce-scatter.22
  1706.3 109.4 reduce-scatter.20
where the time goes:
time: 1840 us; the launch traced here: 1820 us
  waiting for transfers between devices  874 us (48%)
  blocking collectives  343 us (19%)
  matrix products  318 us (17%)
  local copies, waits for them, and re-layouts  165 us (9%)
  other arithmetic  74.1 us (4%)
  starting transfers between devices  32.7 us (2%)
    unnamed x18, waiting for transfers between devices  163 us
    reduce_scatter x1, waiting for transfers between devices, shards(): lax.psum_scatter(grad_proj, ('dp', 'fsdp'), scatter_dimension=0, tiled=True)  135 us
    reduce_scatter x1, waiting for transfers between devices, shards(): lax.psum_scatter(grad_qkv_weight, ('dp', 'fsdp'), scatter_dimension=0, ti...  115 us
    all_gather x1, blocking collectives, shards(): lax.all_gather(w_proj, ('dp', 'fsdp'), axis=0, tiled=True)  114 us
    reduce_scatter x1, waiting for transfers between devices, shards(): lax.psum_scatter(part_value.astype(jnp.bfloat16), 'fsdp', scatter_dimensi...  79.7 us
    unnamed x2, blocking collectives  78.3 us
    reduce_scatter x1, waiting for transfers between devices, shards(): lax.psum_scatter(grad_embed, ('dp', 'fsdp'), scatter_dimension=1, tiled=T...  68 us
    all_gather x1, blocking collectives, shards(): lax.all_gather(task_embed, ('dp', 'fsdp'), axis=1, tiled=True)  64.9 us
  transfers between devices with their start and end apart: 19, of which 15 were waited for; matrix products, arithmetic and copies ran while one was open for 7% of the time, Pallas kernels for 0%

commit v1 on v0

--- a/solution.py
+++ b/solution.py
@@ -1,6 +1,10 @@
+import functools
+
 import jax
 import jax.numpy as jnp
 from jax import lax
+from jax.experimental import pallas as pl
+from jax.experimental.pallas import tpu as pltpu
 from jax.sharding import PartitionSpec as P
 
 HEADS = 8
@@ -333,6 +337,1213 @@
     )
 
 
+MESH_ID = pl.DeviceIdType.MESH
+VMEM_MAX = 60 * 1024 * 1024
+TILE = 16
+BLOCK = 512
+FCHUNK = 512
+QCHUNK = 256
+FAR = -float(2**30)
+F32 = jnp.float32
+BF16 = jnp.bfloat16
+
+
+def dot_nn(lhs, rhs):
+    return lax.dot_general(lhs, rhs, (((1,), (0,)), ((), ())), preferred_element_type=F32)
+
+
+def dot_nt(lhs, rhs):
+    return lax.dot_general(lhs, rhs, (((1,), (1,)), ((), ())), preferred_element_type=F32)
+
+
+def dot_tn(lhs, rhs):
+    return lax.dot_general(lhs, rhs, (((0,), (0,)), ((), ())), preferred_element_type=F32)
+
+
+def vmem_spec():
+    return pl.BlockSpec(memory_space=pltpu.VMEM)
+
+
+def any_spec():
+    return pl.BlockSpec(memory_space=pl.ANY)
+
+
+def smem_spec():
+    return pl.BlockSpec(memory_space=pltpu.SMEM)
+
+
+def norm_parts(values):
+    centre = values - jnp.mean(values, axis=-1, keepdims=True)
+    spread = jnp.mean(centre * centre, axis=-1, keepdims=True)
+    scale = lax.rsqrt(spread + 1e-05)
+    return centre * scale, scale
+
+
+def norm_back_parts(grad, normal, scale):
+    mean_grad = jnp.mean(grad, axis=-1, keepdims=True)
+    mean_prod = jnp.mean(grad * normal, axis=-1, keepdims=True)
+    return (grad - mean_grad - normal * mean_prod) * scale
+
+
+def fold_rows(values):
+    rows, width = values.shape
+    return jnp.sum(values.reshape(rows // 8, 8, width), axis=0)
+
+
+def plane_ids():
+    me = lax.axis_index("dp")
+    core, xpos, ypos = lax.rem(me, 2), lax.rem(me // 2, 2), me // 4
+
+    def at(ypos, xpos, core):
+        return (ypos * 2 + xpos) * 2 + core
+
+    return me, core, xpos, ypos, at
+
+
+def greet(peers):
+    barrier = pltpu.get_barrier_semaphore()
+    for peer in peers:
+        pl.semaphore_signal(barrier, inc=1, device_id=peer, device_id_type=MESH_ID)
+    pl.semaphore_wait(barrier, len(peers))
+
+
+class Sender:
+    def __init__(self, send_sems, recv_sems):
+        self.send_sems, self.recv_sems, self.count, self.all = send_sems, recv_sems, 0, []
+
+    def start(self, src, dst, peer):
+        copy = pltpu.make_async_remote_copy(
+            src_ref=src,
+            dst_ref=dst,
+            send_sem=self.send_sems.at[self.count],
+            recv_sem=self.recv_sems.at[self.count],
+            device_id=peer,
+            device_id_type=MESH_ID,
+        )
+        copy.start()
+        self.count += 1
+        self.all.append(copy)
+        return copy
+
+    def drain(self):
+        for copy in self.all:
+            copy.wait_send()
+
+
+def plane_gather_steps(block, own, rows, sender, z):
+    me, core, xpos, ypos, at = plane_ids()
+    sib, xn, yn = at(ypos, xpos, 1 - core), at(ypos, 1 - xpos, core), at(1 - ypos, xpos, core)
+    diag = at(1 - ypos, 1 - xpos, core)
+    half = rows // 2
+
+    def part(i, k):
+        return block(i).at[pl.ds(k * half, half)]
+
+    def send(i, k, peer):
+        src = own.at[pl.ds(k * half, half)] if i is me else part(i, k)
+        return sender.start(src, part(i, k), (peer, z))
+
+    x_own = [send(me, 0, xn)]
+    y_own = [send(me, 1, yn)]
+    x_own.append(send(me, 1, xn))
+    y_own.insert(0, send(me, 0, yn))
+    last = [send(me, 0, sib), send(me, 1, sib)]
+    x_own[0].wait_recv()
+    to_y = send(xn, 0, yn)
+    y_own[1].wait_recv()
+    to_x = send(yn, 1, xn)
+    last.append(send(xn, 0, sib))
+    last.append(send(yn, 1, sib))
+    x_own[1].wait_recv()
+    last.append(send(xn, 1, sib))
+    y_own[0].wait_recv()
+    last.append(send(yn, 0, sib))
+    to_y.wait_recv()
+    last.append(send(diag, 0, sib))
+    to_x.wait_recv()
+    last.append(send(diag, 1, sib))
+    for copy in last:
+        copy.wait_recv()
+
+
+PLANE_GATHER_COPIES = 14
+
+
+def plane_peers(z):
+    me, core, xpos, ypos, at = plane_ids()
+    return [
+        (at(ypos, xpos, 1 - core), z),
+        (at(ypos, 1 - xpos, core), z),
+        (at(1 - ypos, xpos, core), z),
+    ]
+
+
+def small_gather_kernel(planes, groups, in_ref, out_ref, send_sems, recv_sems):
+    me, z = lax.axis_index("dp"), lax.axis_index("fsdp")
+    z_peers = [(me, lax.rem(z + k, planes)) for k in range(1, planes)]
+    d_peers = [(lax.rem(me + k, groups), z) for k in range(1, groups)]
+    greet(z_peers + d_peers)
+    sender = Sender(send_sems, recv_sems)
+    out_ref[me, z] = in_ref[...]
+    first = [sender.start(in_ref, out_ref.at[me, z], peer) for peer in z_peers]
+    for copy in first:
+        copy.wait_recv()
+    second = [sender.start(out_ref.at[me], out_ref.at[me], peer) for peer in d_peers]
+    for copy in second:
+        copy.wait_recv()
+    sender.drain()
+
+
+def small_gather(payload, planes, groups):
+    return pl.pallas_call(
+        functools.partial(small_gather_kernel, planes, groups),
+        out_shape=jax.ShapeDtypeStruct((groups, planes) + payload.shape, payload.dtype),
+        in_specs=[vmem_spec()],
+        out_specs=vmem_spec(),
+        scratch_shapes=[
+            pltpu.SemaphoreType.DMA((planes + groups,)),
+            pltpu.SemaphoreType.DMA((planes + groups,)),
+        ],
+        compiler_params=pltpu.CompilerParams(collective_id=1, has_side_effects=True),
+        name="routing_gather",
+    )(payload)
+
+
+def enter_kernel(planes, tok_ref, w_ref, row_ref, full_ref, send_sems, recv_sems, loc_sems):
+    me, z = lax.axis_index("dp"), lax.axis_index("fsdp")
+    z_peers = [(me, lax.rem(z + k, planes)) for k in range(1, planes)]
+    greet(z_peers + plane_peers(z))
+    shard = w_ref.shape[0]
+    sender = Sender(send_sems, recv_sems)
+    mine = pltpu.make_async_copy(w_ref, full_ref.at[me, pl.ds(z * shard, shard)], loc_sems.at[0])
+    mine.start()
+    held = pltpu.make_async_copy(tok_ref.at[z], row_ref.at[z], loc_sems.at[1])
+    held.start()
+    first = [
+        sender.start(w_ref, full_ref.at[me, pl.ds(z * shard, shard)], peer) for peer in z_peers
+    ]
+    rows = [sender.start(tok_ref.at[peer[1]], row_ref.at[z], peer) for peer in z_peers]
+    mine.wait()
+    for copy in first:
+        copy.wait_recv()
+    plane_gather_steps(lambda i: full_ref.at[i], full_ref.at[me], planes * shard, sender, z)
+    for copy in rows:
+        copy.wait_recv()
+    held.wait()
+    sender.drain()
+
+
+def enter(tokens, weights, planes, groups):
+    copies = 2 * (planes - 1) + PLANE_GATHER_COPIES
+    return pl.pallas_call(
+        functools.partial(enter_kernel, planes),
+        out_shape=(
+            jax.ShapeDtypeStruct(tokens.shape, tokens.dtype),
+            jax.ShapeDtypeStruct(
+                (groups, planes * weights.shape[0], weights.shape[1]), weights.dtype
+            ),
+        ),
+        in_specs=[any_spec(), any_spec()],
+        out_specs=(any_spec(), any_spec()),
+        scratch_shapes=[
+            pltpu.SemaphoreType.DMA((copies,)),
+            pltpu.SemaphoreType.DMA((copies,)),
+            pltpu.SemaphoreType.DMA((2,)),
+        ],
+        compiler_params=pltpu.CompilerParams(collective_id=2, has_side_effects=True),
+        name="rows_and_dense_weights",
+    )(tokens, weights)
+
+
+def plane_gather_kernel(in_ref, out_ref, send_sems, recv_sems):
+    z = lax.axis_index("fsdp")
+    greet(plane_peers(z))
+    sender = Sender(send_sems, recv_sems)
+    plane_gather_steps(lambda i: out_ref.at[i], in_ref, in_ref.shape[0], sender, z)
+    sender.drain()
+
+
+def plane_gather(block, groups):
+    return pl.pallas_call(
+        plane_gather_kernel,
+        out_shape=jax.ShapeDtypeStruct((groups,) + block.shape, block.dtype),
+        in_specs=[any_spec()],
+        out_specs=any_spec(),
+        scratch_shapes=[
+            pltpu.SemaphoreType.DMA((PLANE_GATHER_COPIES,)),
+            pltpu.SemaphoreType.DMA((PLANE_GATHER_COPIES,)),
+        ],
+        compiler_params=pltpu.CompilerParams(collective_id=3, has_side_effects=True),
+        name="expert_rows_gather",
+    )(block)
+
+
+def plane_scatter_steps(z_ref, out_ref, own, theirs, deep, near_x, near_y, sender, loc_sems, z):
+    me, core, xpos, ypos, at = plane_ids()
+    sib, xn, yn = at(ypos, xpos, 1 - core), at(ypos, 1 - xpos, core), at(1 - ypos, xpos, core)
+    chips = [(ypos, xpos), (ypos, 1 - xpos), (1 - ypos, xpos), (1 - ypos, 1 - xpos)]
+    rows = z_ref.shape[1]
+    half = rows // 2
+    first, second = pl.ds(0, half), pl.ds(half, half)
+    loads, trades = {}, {}
+    for slot in (3, 1, 2, 0):
+        pos = chips[slot]
+        loads[slot] = pltpu.make_async_copy(
+            z_ref.at[at(pos[0], pos[1], core)], own.at[slot], loc_sems.at[slot]
+        )
+        loads[slot].start()
+        trades[slot] = sender.start(
+            z_ref.at[at(pos[0], pos[1], 1 - core)], theirs.at[slot], (sib, z)
+        )
+
+    def add(slot, part):
+        own[slot, part] = (
+            own[slot, part].astype(F32) + theirs[slot, part].astype(F32)
+        ).astype(own.dtype)
+
+    loads[3].wait()
+    trades[3].wait_recv()
+    add(3, first)
+    deep_x = sender.start(own.at[3, first], deep.at[0], (xn, z))
+    add(3, second)
+    deep_y = sender.start(own.at[3, second], deep.at[1], (yn, z))
+    loads[1].wait()
+    trades[1].wait_recv()
+    add(1, first)
+    x_first = sender.start(own.at[1, first], near_x.at[first], (xn, z))
+    loads[2].wait()
+    trades[2].wait_recv()
+    add(2, second)
+    y_second = sender.start(own.at[2, second], near_y.at[second], (yn, z))
+    add(1, second)
+    add(2, first)
+    deep_y.wait_recv()
+    own[1, second] = (own[1, second].astype(F32) + deep[1].astype(F32)).astype(own.dtype)
+    x_second = sender.start(own.at[1, second], near_x.at[second], (xn, z))
+    deep_x.wait_recv()
+    own[2, first] = (own[2, first].astype(F32) + deep[0].astype(F32)).astype(own.dtype)
+    y_first = sender.start(own.at[2, first], near_y.at[first], (yn, z))
+    loads[0].wait()
+    trades[0].wait_recv()
+    mine = own[0].astype(F32) + theirs[0].astype(F32)
+    x_first.wait_recv()
+    y_second.wait_recv()
+    x_second.wait_recv()
+    y_first.wait_recv()
+    out_ref[...] = (mine + near_x[...].astype(F32) + near_y[...].astype(F32)).astype(out_ref.dtype)
+
+
+PLANE_SCATTER_COPIES = 10
+
+
+def plane_scatter_scratch(rows, width):
+    return [
+        pltpu.VMEM((4, rows, width), BF16),
+        pltpu.VMEM((4, rows, width), BF16),
+        pltpu.VMEM((2, rows // 2, width), BF16),
+        pltpu.VMEM((rows, width), BF16),
+        pltpu.VMEM((rows, width), BF16),
+    ]
+
+
+def plane_scatter_kernel(
+    planes,
+    groups,
+    z_ref,
+    small_ref,
+    out_ref,
+    small_out,
+    own,
+    theirs,
+    deep,
+    near_x,
+    near_y,
+    small_in,
+    send_sems,
+    recv_sems,
+    loc_sems,
+):
+    me, z = lax.axis_index("dp"), lax.axis_index("fsdp")
+    z_peers = [(me, lax.rem(z + k, planes)) for k in range(1, planes)]
+    d_peers = [(lax.rem(me + k, groups), z) for k in range(1, groups)]
+    greet(z_peers + d_peers)
+    sender = Sender(send_sems, recv_sems)
+    first = [sender.start(small_ref, small_in.at[k], peer) for k, peer in enumerate(z_peers)]
+    for copy in first:
+        copy.wait_recv()
+    small_out[me] = small_ref[...] + jnp.sum(small_in[...], axis=0)
+    second = [sender.start(small_out.at[me], small_out.at[me], peer) for peer in d_peers]
+    plane_scatter_steps(
+        z_ref, out_ref, own, theirs, deep, near_x, near_y, sender, loc_sems, z
+    )
+    for copy in second:
+        copy.wait_recv()
+    sender.drain()
+
+
+def plane_scatter(terms, small, planes, groups):
+    rows, width = terms.shape[1:]
+    copies = PLANE_SCATTER_COPIES + planes + groups
+    return pl.pallas_call(
+        functools.partial(plane_scatter_kernel, planes, groups),
+        out_shape=(
+            jax.ShapeDtypeStruct((rows, width), F32),
+            jax.ShapeDtypeStruct((groups,) + small.shape, F32),
+        ),
+        in_specs=[any_spec(), vmem_spec()],
+        out_specs=(vmem_spec(), vmem_spec()),
+        scratch_shapes=plane_scatter_scratch(rows, width)
+        + [
+            pltpu.VMEM((planes - 1,) + small.shape, F32),
+            pltpu.SemaphoreType.DMA((copies,)),
+            pltpu.SemaphoreType.DMA((copies,)),
+            pltpu.SemaphoreType.DMA((4,)),
+        ],
+        compiler_params=pltpu.CompilerParams(
+            collective_id=4, has_side_effects=True, vmem_limit_bytes=VMEM_MAX
+        ),
+        name="expert_grads_scatter",
+    )(terms, small)
+
+
+def leave_kernel(
+    planes,
+    tok_ref,
+    w_ref,
+    piece_ref,
+    shard_ref,
+    own,
+    theirs,
+    deep,
+    near_x,
+    near_y,
+    plane_sum,
+    plane_in,
+    send_sems,
+    recv_sems,
+    loc_sems,
+):
+    me, z = lax.axis_index("dp"), lax.axis_index("fsdp")
+    z_peers = [(me, lax.rem(z + k, planes)) for k in range(1, planes)]
+    greet(z_peers + plane_peers(z))
+    sender = Sender(send_sems, recv_sems)
+    held = pltpu.make_async_copy(tok_ref.at[z], piece_ref.at[z], loc_sems.at[4])
+    held.start()
+    rows = [sender.start(tok_ref.at[peer[1]], piece_ref.at[z], peer) for peer in z_peers]
+    plane_scatter_steps(
+        w_ref, plane_sum, own, theirs, deep, near_x, near_y, sender, loc_sems, z
+    )
+    shard = shard_ref.shape[0]
+    last = [
+        sender.start(plane_sum.at[pl.ds(peer[1] * shard, shard)], plane_in.at[k], peer)
+        for k, peer in enumerate(z_peers)
+    ]
+    total = plane_sum[pl.ds(z * shard, shard)].astype(F32)
+    for k, copy in enumerate(last):
+        copy.wait_recv()
+        total = total + plane_in[k].astype(F32)
+    shard_ref[...] = total
+    for copy in rows:
+        copy.wait_recv()
+    held.wait()
+    sender.drain()
+
+
+def leave(tokens, terms, planes, groups):
+    rows, width = terms.shape[1:]
+    copies = PLANE_SCATTER_COPIES + 2 * planes
+    return pl.pallas_call(
+        functools.partial(leave_kernel, planes),
+        out_shape=(
+            jax.ShapeDtypeStruct(tokens.shape, tokens.dtype),
+            jax.ShapeDtypeStruct((rows // planes, width), F32),
+        ),
+        in_specs=[any_spec(), any_spec()],
+        out_specs=(any_spec(), vmem_spec()),
+        scratch_shapes=plane_scatter_scratch(rows, width)
+        + [
+            pltpu.VMEM((rows, width), BF16),
+            pltpu.VMEM((planes - 1, rows // planes, width), BF16),
+            pltpu.SemaphoreType.DMA((copies,)),
+            pltpu.SemaphoreType.DMA((copies,)),
+            pltpu.SemaphoreType.DMA((5,)),
+        ],
+        compiler_params=pltpu.CompilerParams(
+            collective_id=5, has_side_effects=True, vmem_limit_bytes=VMEM_MAX
+        ),
+        name="grads_and_rows_back",
+    )(tokens, terms)
+
+
+def pick_rows_kernel(order_ref, *refs):
+    count = len(refs) // 2
+    for a in range(count):
+        refs[count + a][...] = refs[a][...].astype(refs[count + a].dtype)
+
+
+def pick_rows(order, arrays, kinds):
+    def block(array):
+        return (1,) + array.shape[1:]
+
+    return pl.pallas_call(
+        pick_rows_kernel,
+        out_shape=tuple(
+            jax.ShapeDtypeStruct(array.shape, kind) for array, kind in zip(arrays, kinds)
+        ),
+        grid_spec=pltpu.PrefetchScalarGridSpec(
+            num_scalar_prefetch=1,
+            grid=(arrays[0].shape[0],),
+            in_specs=[
+                pl.BlockSpec(block(array), lambda r, order_ref: (order_ref[r], 0, 0))
+                for array in arrays
+            ],
+            out_specs=tuple(
+                pl.BlockSpec(block(array), lambda r, order_ref: (r, 0, 0)) for array in arrays
+            ),
+        ),
+        name="row_order",
+    )(order, *arrays)
+
+
+def forward_kernel(
+    heads,
+    tok_ref,
+    norm_ref,
+    w_ref,
+    qf_ref,
+    kf_ref,
+    qkv_ref,
+    o_ref,
+    lse_ref,
+    hres_ref,
+    xn2_ref,
+    kaug,
+    vaug,
+):
+    rows, width = tok_ref.shape
+    chunk = QCHUNK
+    pair = 2 * (width // heads)
+    lane = lax.broadcasted_iota(jnp.int32, (rows, pair), 1)
+    lane_c = lax.broadcasted_iota(jnp.int32, (chunk, pair), 1)
+
+    def project(c, carry):
+        part = pl.ds(pl.multiple_of(c * chunk, chunk), chunk)
+        normal, _ = norm_parts(tok_ref[part, :].astype(F32))
+        xn1 = (normal * norm_ref[0:1, :] + norm_ref[1:2, :]).astype(BF16)
+        out = dot_nn(xn1, w_ref[:, : 3 * width])
+        qkv_ref[part, :width] = (out[:, :width] * 0.125).astype(BF16)
+        qkv_ref[part, width:] = out[:, width:].astype(BF16)
+        return carry
+
+    lax.fori_loop(0, rows // chunk, project, 0)
+
+    for side in range(2):
+        kaug[side, :, pair:] = kf_ref[...]
+        vaug[side, :, pair:] = jnp.where((lane // (pair // 2)) == side, 1.0, 0.0).astype(BF16)
+
+    def one_pair(g, carry):
+        cols = pl.ds(pl.multiple_of(g * pair, pair), pair)
+        k_pair = qkv_ref[:, pl.ds(pl.multiple_of(width + g * pair, pair), pair)]
+        v_pair = qkv_ref[:, pl.ds(pl.multiple_of(2 * width + g * pair, pair), pair)]
+        zero = jnp.zeros_like(k_pair)
+        for side in range(2):
+            mine = (lane // (pair // 2)) == side
+            kaug[side, :, :pair] = jnp.where(mine, k_pair, zero)
+            vaug[side, :, :pair] = jnp.where(mine, v_pair, zero)
+
+        def one_chunk(c, inner):
+            part = pl.ds(pl.multiple_of(c * chunk, chunk), chunk)
+            qa = jnp.concatenate([qkv_ref[part, cols], qf_ref[part, :]], axis=1)
+            acc = jnp.zeros((chunk, 2 * pair), F32)
+            tops = []
+            for side in range(2):
+                s = dot_nt(qa, kaug[side])
+                top = jnp.max(s, axis=-1, keepdims=True)
+                acc = acc + dot_nn(jnp.exp(s - top).astype(BF16), vaug[side])
+                tops.append(top)
+            total = acc[:, pair:]
+            o_ref[part, cols] = (acc[:, :pair] / total).astype(BF16)
+            top = jnp.where(lane_c < pair // 2, tops[0], tops[1])
+            lse_ref[part, cols] = top + jnp.log(total)
+            return inner
+
+        lax.fori_loop(0, rows // chunk, one_chunk, 0)
+        return carry
+
+    lax.fori_loop(0, heads // 2, one_pair, 0)
+
+    def finish(c, carry):
+        part = pl.ds(pl.multiple_of(c * chunk, chunk), chunk)
+        hres = tok_ref[part, :].astype(F32) + dot_nn(o_ref[part, :], w_ref[:, 3 * width :])
+        hres_ref[part, :] = hres
+        normal, _ = norm_parts(hres)
+        xn2_ref[part, :] = (normal * norm_ref[2:3, :] + norm_ref[3:4, :]).astype(BF16)
+        return carry
+
+    lax.fori_loop(0, rows // chunk, finish, 0)
+
+
+def forward(row, norms, weights, qf, kf, heads):
+    rows, width = row.shape
+    pair = 2 * (width // heads)
+    return pl.pallas_call(
+        functools.partial(forward_kernel, heads),
+        out_shape=(
+            jax.ShapeDtypeStruct((rows, 3 * width), BF16),
+            jax.ShapeDtypeStruct((rows, width), BF16),
+            jax.ShapeDtypeStruct((rows, width), F32),
+            jax.ShapeDtypeStruct((rows, width), F32),
+            jax.ShapeDtypeStruct((rows, width), BF16),
+        ),
+        in_specs=[vmem_spec()] * 5,
+        out_specs=tuple([vmem_spec()] * 5),
+        scratch_shapes=[
+            pltpu.VMEM((2, rows, 2 * pair), BF16),
+            pltpu.VMEM((2, rows, 2 * pair), BF16),
+        ],
+        compiler_params=pltpu.CompilerParams(vmem_limit_bytes=VMEM_MAX),
+        cost_estimate=pl.CostEstimate(
+            flops=40_000_000_000, bytes_accessed=10_000_000, transcendentals=8_000_000
+        ),
+        name="attention_forward",
+    )(row, norms, weights, qf, kf)
+
+
+def split3(values):
+    high = values.astype(BF16)
+    rest = values - high.astype(F32)
+    middle = rest.astype(BF16)
+    low = (rest - middle.astype(F32)).astype(BF16)
+    return high, middle, low
+
+
+def backward_kernel(
+    heads,
+    tok_ref,
+    norm_ref,
+    w_ref,
+    qf_ref,
+    kf_ref,
+    qkv_ref,
+    o_ref,
+    lse_ref,
+    hres_ref,
+    dxn2_ref,
+    gm_ref,
+    dtok_ref,
+    dw_ref,
+    dnorm_ref,
+    kaug,
+    vaug,
+    dh,
+    db,
+    do,
+    delta,
+    qt,
+    dot_t,
+    dkt,
+    dvt,
+    dq,
+    dqkv,
+    xn1,
+):
+    rows, width = tok_ref.shape
+    chunk = QCHUNK
+    head = width // heads
+    pair = 2 * head
+    lane = lax.broadcasted_iota(jnp.int32, (rows, pair), 1)
+    lane_c = lax.broadcasted_iota(jnp.int32, (chunk, pair), 1)
+    same = (
+        lax.broadcasted_iota(jnp.int32, (pair, pair), 0) // head
+        == lax.broadcasted_iota(jnp.int32, (pair, pair), 1) // head
+    )
+    ones = jnp.where(same, 1.0, 0.0).astype(BF16)
+    dnorm_ref[...] = jnp.zeros_like(dnorm_ref)
+
+    def begin(c, carry):
+        part = pl.ds(pl.multiple_of(c * chunk, chunk), chunk)
+        normal, scale = norm_parts(hres_ref[part, :])
+        grad = dxn2_ref[part, :]
+        dnorm_ref[2] += fold_rows(grad * normal)
+        dnorm_ref[3] += fold_rows(grad)
+        dh_part = gm_ref[part, :].astype(F32) + norm_back_parts(
+            grad * norm_ref[2:3, :], normal, scale
+        )
+        dh[part, :] = dh_part
+        low = dh_part.astype(BF16)
+        db[part, :] = low
+        do_part = dot_nt(low, w_ref[:, 3 * width :]).astype(BF16)
+        do[part, :] = do_part
+        prod = do_part.astype(F32) * o_ref[part, :].astype(F32)
+        high = prod.astype(BF16)
+        rest = (prod - high.astype(F32)).astype(BF16)
+        for g in range(heads // 2):
+            cols = slice(g * pair, (g + 1) * pair)
+            delta[part, cols] = dot_nn(high[:, cols], ones) + dot_nn(rest[:, cols], ones)
+        qt[:, part] = qkv_ref[part, :width].T
+        dot_t[:, part] = do_part.T
+        normal, _ = norm_parts(tok_ref[part, :].astype(F32))
+        xn1[part, :] = (normal * norm_ref[0:1, :] + norm_ref[1:2, :]).astype(BF16)
+        return carry
+
+    lax.fori_loop(0, rows // chunk, begin, 0)
+    dw_ref[:, 3 * width :] = dot_tn(o_ref[...], db[...]).astype(BF16)
+
+    mark = (lane >= heads) & (lane < heads + 3)
+    for side in range(2):
+        kaug[side, :, pair:] = jnp.where(mark, 1.0, kf_ref[...].astype(F32)).astype(BF16)
+        vaug[side, :, pair:] = jnp.where(mark, 1.0, 0.0).astype(BF16)
+
+    def put_parts(base, values):
+        high, middle, low = split3(-values)
+        out = jnp.where(lane_c == heads, high.astype(F32), base)
+        out = jnp.where(lane_c == heads + 1, middle.astype(F32), out)
+        return jnp.where(lane_c == heads + 2, low.astype(F32), out).astype(BF16)
+
+    def one_pair(g, carry):
+        cols = pl.ds(pl.multiple_of(g * pair, pair), pair)
+        k_pair = qkv_ref[:, pl.ds(pl.multiple_of(width + g * pair, pair), pair)]
+        v_pair = qkv_ref[:, pl.ds(pl.multiple_of(2 * width + g * pair, pair), pair)]
+        zero = jnp.zeros_like(k_pair)
+        for side in range(2):
+            mine = (lane // head) == side
+            kaug[side, :, :pair] = jnp.where(mine, k_pair, zero)
+            vaug[side, :, :pair] = jnp.where(mine, v_pair, zero)
+
+        def one_chunk(c, inner):
+            part = pl.ds(pl.multiple_of(c * chunk, chunk), chunk)
+            q_pair, do_pair = qkv_ref[part, cols], do[part, cols]
+            lse_pair, delta_pair = lse_ref[part, cols], delta[part, cols]
+            base = qf_ref[part, :].astype(F32)
+            acc = jnp.zeros((chunk, pair), F32)
+            for side in range(2):
+                lse = lse_pair[:, side * head : side * head + 1]
+                qa = jnp.concatenate([q_pair, put_parts(base, lse)], axis=1)
+                pr = jnp.exp(dot_nt(qa, kaug[side]))
+                dlt = delta_pair[:, side * head : side * head + 1]
+                da = jnp.concatenate([do_pair, put_parts(jnp.zeros_like(base), dlt)], axis=1)
+                ds = (pr * dot_nt(da, vaug[side])).astype(BF16)
+                acc = acc + dot_nn(ds, kaug[side, :, :pair])
+                spot = pl.ds(pl.multiple_of(g * pair + side * head, head), head)
+                dk_new = dot_nn(qt[spot, part], ds)
+                dv_new = dot_nn(dot_t[spot, part], pr.astype(BF16))
+
+                @pl.when(c == 0)
+                def _():
+                    dkt[spot, :] = dk_new
+                    dvt[spot, :] = dv_new
+
+                @pl.when(c > 0)
+                def _():
+                    dkt[spot, :] += dk_new
+                    dvt[spot, :] += dv_new
+
+            dq[part, cols] = (acc * 0.125).astype(BF16)
+            return inner
+
+        lax.fori_loop(0, rows // chunk, one_chunk, 0)
+        return carry
+
+    lax.fori_loop(0, heads // 2, one_pair, 0)
+
+    def finish(c, carry):
+        part = pl.ds(pl.multiple_of(c * chunk, chunk), chunk)
+        dqkv[part, :width] = dq[part, :]
+        dqkv[part, width : 2 * width] = dkt[:, part].T.astype(BF16)
+        dqkv[part, 2 * width :] = dvt[:, part].T.astype(BF16)
+        grad = dot_nt(dqkv[part, :], w_ref[:, : 3 * width])
+        normal, scale = norm_parts(tok_ref[part, :].astype(F32))
+        dnorm_ref[0] += fold_rows(grad * normal)
+        dnorm_ref[1] += fold_rows(grad)
+        dtok_ref[part, :] = (
+            dh[part, :] + norm_back_parts(grad * norm_ref[0:1, :], normal, scale)
+        ).astype(BF16)
+        return carry
+
+    lax.fori_loop(0, rows // chunk, finish, 0)
+    for c in range(3):
+        cols = slice(c * width, (c + 1) * width)
+        dw_ref[:, cols] = dot_tn(xn1[...], dqkv[:, cols]).astype(BF16)
+
+
+def backward(row, norms, weights, qf, kf, qkv, o, lse, hres, dxn2, gm, heads):
+    rows, width = row.shape
+    pair = 2 * (width // heads)
+    return pl.pallas_call(
+        functools.partial(backward_kernel, heads),
+        out_shape=(
+            jax.ShapeDtypeStruct((rows, width), BF16),
+            jax.ShapeDtypeStruct((width, 4 * width), BF16),
+            jax.ShapeDtypeStruct((4, 8, width), F32),
+        ),
+        in_specs=[vmem_spec()] * 11,
+        out_specs=tuple([vmem_spec()] * 3),
+        scratch_shapes=[
+            pltpu.VMEM((2, rows, 2 * pair), BF16),
+            pltpu.VMEM((2, rows, 2 * pair), BF16),
+            pltpu.VMEM((rows, width), F32),
+            pltpu.VMEM((rows, width), BF16),
+            pltpu.VMEM((rows, width), BF16),
+            pltpu.VMEM((rows, width), F32),
+            pltpu.VMEM((width, rows), BF16),
+            pltpu.VMEM((width, rows), BF16),
+            pltpu.VMEM((width, rows), F32),
+            pltpu.VMEM((width, rows), F32),
+            pltpu.VMEM((rows, width), BF16),
+            pltpu.VMEM((rows, 3 * width), BF16),
+            pltpu.VMEM((rows, width), BF16),
+        ],
+        compiler_params=pltpu.CompilerParams(vmem_limit_bytes=VMEM_MAX),
+        cost_estimate=pl.CostEstimate(
+            flops=80_000_000_000, bytes_accessed=20_000_000, transcendentals=8_000_000
+        ),
+        name="attention_backward",
+    )(row, norms, weights, qf, kf, qkv, o, lse, hres, dxn2, gm)
+
+
+def expert_kernel(planes, groups, *refs):
+    refs = list(refs)
+
+    def take(count):
+        out = refs[:count]
+        del refs[:count]
+        return out
+
+    list_ref, meta_ref, own_ref, x_ref = take(4)
+    g_refs, up_refs, down_refs = take(groups), take(planes), take(planes)
+    bup_ref, bdown_ref = take(2)
+    (zd_ref,) = take(1)
+    zy_refs, dup_refs, ddown_refs = take(groups), take(planes), take(planes)
+    dbup_ref, dbdown_ref, dgate_ref = take(3)
+    xs, gs, up, down, acc_up, acc_down, xb, gb, mb, dyb, xt, dyt, yacc, xacc, cast, sems = refs
+    me, z = lax.axis_index("dp"), lax.axis_index("fsdp")
+    width, hidden = up.shape
+    rows = x_ref.shape[1]
+    up_rows, down_rows = width // planes, hidden // planes
+    tiles = BLOCK // TILE
+    copies = []
+
+    def load(src, dst):
+        copy = pltpu.make_async_copy(src, dst, sems.at[len(copies)])
+        copy.start()
+        copies.append(copy)
+
+    for k in range(planes):
+        owner = lax.rem(z + k, planes)
+        load(up_refs[k], up.at[pl.ds(pl.multiple_of(owner * up_rows, up_rows), up_rows)])
+        load(down_refs[k], down.at[pl.ds(pl.multiple_of(owner * down_rows, down_rows), down_rows)])
+    for k in range(groups):
+        owner = me ^ k
+        load(g_refs[k], gs.at[pl.ds(pl.multiple_of(owner * rows, rows), rows)])
+        load(
+            x_ref.at[owner] if k else own_ref,
+            xs.at[pl.ds(pl.multiple_of(owner * rows, rows), rows)],
+        )
+    acc_up[...] = jnp.zeros_like(acc_up)
+    acc_down[...] = jnp.zeros_like(acc_down)
+    dbup_ref[...] = jnp.zeros_like(dbup_ref)
+    dbdown_ref[...] = jnp.zeros_like(dbdown_ref)
+    dgate_ref[...] = jnp.zeros_like(dgate_ref)
+    for copy in copies:
+        copy.wait()
+    n_tiles = list_ref[0]
+    n_blocks = lax.div(n_tiles + (tiles - 1), tiles)
+
+    def spot(index):
+        return pl.ds(pl.multiple_of(index * TILE, TILE), TILE)
+
+    def one_block(b, carry):
+        def fetch(k, inner):
+            src = spot(list_ref[1 + b * tiles + k])
+            dst = spot(k)
+            xb[dst, :] = xs[src, :]
+            gb[dst, :] = gs[src, :]
+            mb[dst, :] = meta_ref[src, :]
+            return inner
+
+        lax.fori_loop(0, tiles, fetch, 0, unroll=4)
+        gate = mb[:, 0:1]
+        dyb_new = (gb[...].astype(F32) * gate).astype(BF16)
+        dyb[...] = dyb_new
+        xt[...] = xb[...].T
+        dyt[...] = dyb_new.T
+        dbdown_ref[...] += fold_rows(dyb_new.astype(F32))
+
+        def one_chunk(f, inner):
+            cols = pl.ds(pl.multiple_of(f * FCHUNK, FCHUNK), FCHUNK)
+            u = dot_nn(xb[...], up[:, cols]) + bup_ref[:, cols]
+            sq = u * u
+            th = jnp.tanh(u * (0.7978845608028654 + 0.035677408136300125 * sq))
+            half = 0.5 + 0.5 * th
+            slope = half + u * (
+                (0.5 - 0.5 * th * th) * (0.7978845608028654 + 0.10703222440890037 * sq)
+            )
+            a = (u * half).astype(BF16)
+            du = (dot_nt(dyb[...], down[cols, :]) * slope).astype(BF16)
+            y_new = dot_nn(a, down[cols, :])
+            x_new = dot_nt(du, up[:, cols])
+
+            @pl.when(f == 0)
+            def _():
+                yacc[...] = y_new
+                xacc[...] = x_new
+
+            @pl.when(f > 0)
+            def _():
+                yacc[...] += y_new
+                xacc[...] += x_new
+
+            acc_up[:, cols] += dot_nn(xt[...], du)
+            acc_down[:, cols] += dot_nn(dyt[...], a)
+            dbup_ref[:, cols] += fold_rows(du.astype(F32))
+            return inner
+
+        lax.fori_loop(0, hidden // FCHUNK, one_chunk, 0)
+        y = (yacc[...] + bdown_ref[...]).astype(BF16).astype(F32)
+        inner_prod = jnp.sum(y * gb[...].astype(F32), axis=-1, keepdims=True)
+        lane = lax.broadcasted_iota(jnp.int32, (BLOCK, 128), 1).astype(F32)
+        dgate_ref[...] += fold_rows(jnp.where(lane == mb[:, 1:2], inner_prod, 0.0))
+        gb[...] = (y * gate).astype(BF16)
+        xb[...] = xacc[...].astype(BF16)
+
+        def store(k, inner):
+            dst = spot(list_ref[1 + b * tiles + k])
+            src = spot(k)
+            xs[dst, :] = xb[src, :]
+            gs[dst, :] = gb[src, :]
+            return inner
+
+        lax.fori_loop(0, tiles, store, 0, unroll=4)
+        return carry
+
+    lax.fori_loop(0, n_blocks, one_block, 0)
+
+    def clear(k, carry):
+        dst = spot(list_ref[1 + k])
+        xs[dst, :] = jnp.zeros((TILE, width), BF16)
+        gs[dst, :] = jnp.zeros((TILE, width), BF16)
+        return carry
+
+    lax.fori_loop(n_blocks * tiles, groups * rows // TILE, clear, 0)
+    outs = []
+
+    def save(src, dst):
+        copy = pltpu.make_async_copy(src, dst, sems.at[len(outs)])
+        copy.start()
+        outs.append(copy)
+
+    for k in range(groups):
+        owner = me ^ k
+        save(xs.at[pl.ds(k * rows, rows)], zd_ref.at[k])
+        save(gs.at[pl.ds(pl.multiple_of(owner * rows, rows), rows)], zy_refs[k])
+    up[...] = acc_up[...].astype(BF16)
+    for k in range(hidden // FCHUNK):
+        cols = slice(k * FCHUNK, (k + 1) * FCHUNK)
+        down[cols, :] = acc_down[:, cols].T.astype(BF16)
+    for k in range(planes):
+        owner = lax.rem(z + k, planes)
+        save(up.at[pl.ds(pl.multiple_of(owner * up_rows, up_rows), up_rows)], dup_refs[k])
+        save(
+            down.at[pl.ds(pl.multiple_of(owner * down_rows, down_rows), down_rows)], ddown_refs[k]
+        )
+    for copy in outs:
+        copy.wait()
+
+
+def experts(tile_list, meta, x_own, x_all, g_list, up_list, down_list, b_up, b_down):
+    groups, rows, width = x_all.shape
+    planes = len(up_list)
+    hidden = b_up.shape[1]
+    total = groups * rows
+    sd = jax.ShapeDtypeStruct
+    out = pl.pallas_call(
+        functools.partial(expert_kernel, planes, groups),
+        out_shape=(
+            [sd(x_all.shape, BF16)]
+            + [sd((rows, width), BF16)] * groups
+            + [sd((width // planes, hidden), BF16)] * planes
+            + [sd((hidden // planes, width), BF16)] * planes
+            + [sd((8, hidden), F32), sd((8, width), F32), sd((8, 128), F32)]
+        ),
+        in_specs=[smem_spec(), vmem_spec()]
+        + [any_spec()] * (2 + groups + 2 * planes)
+        + [vmem_spec()] * 2,
+        out_specs=[any_spec()] * (1 + groups + 2 * planes) + [vmem_spec()] * 3,
+        scratch_shapes=[
+            pltpu.VMEM((total, width), BF16),
+            pltpu.VMEM((total, width), BF16),
+            pltpu.VMEM((width, hidden), BF16),
+            pltpu.VMEM((hidden, width), BF16),
+            pltpu.VMEM((width, hidden), F32),
+            pltpu.VMEM((width, hidden), F32),
+            pltpu.VMEM((BLOCK, width), BF16),
+            pltpu.VMEM((BLOCK, width), BF16),
+            pltpu.VMEM((BLOCK, 128), F32),
+            pltpu.VMEM((BLOCK, width), BF16),
+            pltpu.VMEM((width, BLOCK), BF16),
+            pltpu.VMEM((width, BLOCK), BF16),
+            pltpu.VMEM((BLOCK, width), F32),
+            pltpu.VMEM((BLOCK, width), F32),
+            pltpu.VMEM((8, 128), F32),
+            pltpu.SemaphoreType.DMA((2 * (groups + planes),)),
+        ],
+        compiler_params=pltpu.CompilerParams(vmem_limit_bytes=VMEM_MAX),
+        cost_estimate=pl.CostEstimate(
+            flops=60_000_000_000, bytes_accessed=40_000_000, transcendentals=8_000_000
+        ),
+        name="experts",
+    )(tile_list, meta, x_own, x_all, *g_list, *up_list, *down_list, b_up, b_down)
+    zd = out[0]
+    zy = out[1 : 1 + groups]
+    dup = out[1 + groups : 1 + groups + planes]
+    ddown = out[1 + groups + planes : 1 + groups + 2 * planes]
+    return zd, zy, dup, ddown, out[-3], out[-2], out[-1]
+
+
+def fast_shards(
+    mesh_sizes,
+    tokens,
+    out_grad,
+    segment_ids,
+    key_mask,
+    sent_task,
+    task_experts,
+    ln1_gain,
+    ln1_bias,
+    w_qkv,
+    w_proj,
+    ln2_gain,
+    ln2_bias,
+    task_embed,
+    w_gate,
+    w_up,
+    b_up,
+    w_down,
+    b_down,
+):
+    groups, planes = mesh_sizes
+    row_count, piece, width = tokens.shape
+    length = piece * planes
+    total = groups * length
+    tasks = task_experts.shape[0]
+    n_experts = w_gate.shape[1]
+    hidden = w_up.shape[2]
+    capacity = 4 * row_count * piece // n_experts
+    me, z = lax.axis_index("dp"), lax.axis_index("fsdp")
+
+    def z_shift(x, k):
+        return lax.ppermute(x, "fsdp", [(i, (i + k) % planes) for i in range(planes)])
+
+    def d_swap(x, k):
+        return lax.ppermute(x, "dp", [(i, i ^ k) for i in range(groups)])
+
+    seg_hot = segment_ids[:, :, None] == jnp.arange(sent_task.shape[1])[None, None, :]
+    task_tok = jnp.sum(jnp.where(seg_hot, sent_task[:, None, :], 0), axis=-1)
+    code = (task_tok * 16 + segment_ids * 2 + key_mask).astype(F32)
+    logits_part = jnp.dot(task_embed.astype(F32), w_gate.astype(F32), precision=exact)
+    norm_part = jnp.stack([ln1_gain, ln1_bias, ln2_gain, ln2_bias]).astype(F32)
+    bias_part = jnp.concatenate([b_up[0], b_down[0]]).astype(F32)
+    parts = [code.reshape(-1), logits_part.reshape(-1), norm_part.reshape(-1), bias_part]
+    used = sum(p.shape[0] for p in parts)
+    pad_rows = -(-used // 1024) * 8
+    payload = jnp.concatenate(parts + [jnp.zeros((pad_rows * 128 - used,), F32)])
+    gathered = small_gather(payload.reshape(pad_rows, 128), planes, groups)
+    gathered = gathered.reshape(groups, planes, pad_rows * 128)
+    ends = []
+    at = 0
+    for p in parts:
+        ends.append((at, at + p.shape[0]))
+        at += p.shape[0]
+    codes = gathered[:, :, ends[0][0] : ends[0][1]].astype(jnp.int32)
+    codes = codes.reshape(groups, planes, row_count, piece)
+    logits_all = jnp.sum(gathered[:, :, ends[1][0] : ends[1][1]], axis=(0, 1))
+    logits_all = logits_all.reshape(tasks, n_experts)
+    norms = gathered[:, :, ends[2][0] : ends[2][1]].reshape(groups * planes, 4, -1)
+    norms = norms.transpose(1, 0, 2).reshape(4, width)
+    norms = jnp.concatenate([norms, jnp.zeros((4, width), F32)])
+    biases = lax.dynamic_index_in_dim(
+        gathered[:, :, ends[3][0] : ends[3][1]], me, 0, keepdims=False
+    )
+    bias_up = biases[:, : b_up.shape[1]].reshape(1, hidden)
+    bias_down = biases[:, b_up.shape[1] :].reshape(1, width)
+
+    seg_first = codes[:, 0, :, 0] % 16 // 2
+    seg_last = codes[:, planes - 1, :, piece - 1] % 16 // 2
+    single = jnp.argmax((seg_first == seg_last).astype(jnp.int32), axis=1)
+    target = jnp.arange(groups) % planes
+    slots = jnp.arange(planes)[None, :]
+    order = jnp.where(
+        slots == target[:, None],
+        single[:, None],
+        jnp.where(slots == single[:, None], target[:, None], slots),
+    ).astype(jnp.int32)
+    my_order = lax.dynamic_index_in_dim(order, me, 0, keepdims=False)
+    row_of = lax.dynamic_index_in_dim(order, z, 1, keepdims=False)
+
+    tokens_out, grads_out = pick_rows(my_order, (tokens, out_grad), (BF16, BF16))
+    dense = jnp.concatenate([w_qkv, w_proj], axis=1)
+    row, dense_full = enter(tokens_out, dense, planes, groups)
+    row = row.reshape(length, width)
+    dense_full = dense_full.reshape(width, 4 * width)
+
+    w_up, w_down, grads_out, row = lax.optimization_barrier((w_up, w_down, grads_out, row))
+    up_list = [w_up[0]] + [z_shift(w_up[0], planes - k) for k in range(1, planes)]
+    down_list = [w_down[0]] + [z_shift(w_down[0], planes - k) for k in range(1, planes)]
+
+    grad_pieces = [lax.dynamic_index_in_dim(grads_out, z, 0, keepdims=False)]
+    for k in range(1, planes):
+        grad_pieces.append(
+            z_shift(lax.dynamic_index_in_dim(grads_out, (z + k) % planes, 0, keepdims=False), k)
+        )
+    gm = jnp.zeros((planes, piece, width), BF16)
+    for k in range(planes):
+        gm = lax.dynamic_update_index_in_dim(gm, grad_pieces[k], (z - k) % planes, 0)
+    gm = gm.reshape(length, width)
+    g_list = [gm] + [d_swap(gm, k) for k in range(1, groups)]
+
+    my_codes = lax.dynamic_index_in_dim(codes, me, 0, keepdims=False)
+    my_code = lax.dynamic_index_in_dim(my_codes, row_of[me], 1, keepdims=False).reshape(length)
+    my_seg, my_key = my_code % 16 // 2, my_code % 2
+    pair = 2 * HD
+    feature = jnp.arange(pair)[None, :]
+    hot = my_seg[:, None] == feature
+    qf = hot.astype(BF16)
+    kf = jnp.where((feature < 8) & ~(hot & (my_key[:, None] == 1)), FAR, 0.0).astype(BF16)
+
+    qkv, o, lse, hres, xn2 = forward(row, norms, dense_full, qf, kf, HEADS)
+
+    choose = (task_experts[:, :, None] == jnp.arange(n_experts)[None, None, :]).astype(F32)
+
+    def gate_values(logits):
+        return jax.nn.softmax(jnp.sum(logits[:, None, :] * choose, axis=-1), axis=-1)
+
+    gates, gate_back = jax.vjp(gate_values, logits_all)
+    mine = task_experts == me
+    bits = jnp.sum(
+        jnp.where(mine, jnp.left_shift(1, jnp.arange(tasks, dtype=jnp.int32))[:, None], 0), axis=0
+    )
+    gate_of_task = jnp.sum(jnp.where(mine, gates, 0.0), axis=1)
+    task_all = codes // 16
+    hits = (jnp.right_shift(bits[None, None, :, None, None], task_all[:, :, None]) & 1).astype(F32)
+    lower = (jnp.arange(piece)[:, None] < jnp.arange(piece)[None, :]).astype(BF16)
+    before = jnp.dot(
+        hits.reshape(-1, piece).astype(BF16), lower, preferred_element_type=F32
+    ).reshape(hits.shape)
+    counts = jnp.sum(hits, axis=-1).reshape(groups, planes, 2 * row_count)
+    ahead = (jnp.cumsum(counts, axis=-1) - counts).reshape(groups, planes, 2, row_count)
+    rank = before + ahead[..., None]
+    kept = jnp.where(rank < capacity, hits, 0.0)
+    kept = jnp.sum(kept, axis=2)
+    here = (jnp.arange(row_count)[None, :] == row_of[:, None]).astype(F32)
+    kept_here = jnp.sum(kept * here[:, None, :, None], axis=2).reshape(total)
+    task_here = jnp.sum(
+        jnp.where(here[:, None, :, None] > 0, task_all, 0), axis=2
+    ).reshape(total)
+    task_hot = task_here[:, None] == jnp.arange(tasks)[None, :]
+    gate_here = jnp.sum(jnp.where(task_hot, gate_of_task[None, :], 0.0), axis=1) * kept_here
+    task_mark = jnp.where(kept_here > 0, task_here.astype(F32), -1.0)
+    lane = jnp.arange(128)[None, :]
+    meta = jnp.where(
+        lane == 0, gate_here[:, None], jnp.where(lane == 1, task_mark[:, None], 0.0)
+    )
+    n_tiles = total // TILE
+    tile_hit = (jnp.max(kept_here.reshape(n_tiles, TILE), axis=1) > 0).astype(jnp.int32)
+    hit_count = jnp.sum(tile_hit)
+    hit_rank = jnp.cumsum(tile_hit)
+    index = jnp.arange(n_tiles, dtype=jnp.int32)
+    place = jnp.where(tile_hit > 0, hit_rank - 1, hit_count + index - hit_rank)
+    tile_list = jnp.sum(
+        jnp.where(place[None, :] == index[:, None], index[None, :], 0), axis=1, dtype=jnp.int32
+    )
+    tile_list = jnp.concatenate([hit_count[None].astype(jnp.int32), tile_list])
+
+    x_all = plane_gather(xn2, groups)
+    zd, zy, dup, ddown, dbup, dbdown, dgate = experts(
+        tile_list, meta, xn2, x_all, g_list, up_list, down_list, bias_up, bias_down
+    )
+    small = jnp.concatenate(
+        [
+            jnp.sum(dgate, axis=0, keepdims=True),
+            jnp.sum(dbup, axis=0).reshape(-1, 128),
+            jnp.sum(dbdown, axis=0).reshape(-1, 128),
+        ]
+    )
+    small_rows = small.shape[0]
+    small = jnp.concatenate([small, jnp.zeros((-small_rows % 8, 128), F32)])
+    dxn2, small_all = plane_scatter(zd, small, planes, groups)
+
+    dup, ddown, zy, dxn2 = lax.optimization_barrier((dup, ddown, zy, dxn2))
+    d_w_up = dup[0].astype(F32)
+    d_w_down = ddown[0].astype(F32)
+    for k in range(1, planes):
+        d_w_up = d_w_up + z_shift(dup[k], k).astype(F32)
+        d_w_down = d_w_down + z_shift(ddown[k], k).astype(F32)
+    mixed = hres + zy[0].astype(F32)
+    for k in range(1, groups):
+        mixed = mixed + d_swap(zy[k], k).astype(F32)
+    mixed = mixed.astype(BF16).reshape(planes, piece, width)
+    out_pieces = jnp.zeros((planes, piece, width), BF16)
+    for k in range(planes):
+        part = lax.dynamic_index_in_dim(mixed, (z + k) % planes, 0, keepdims=False)
+        part = z_shift(part, k) if k else part
+        out_pieces = lax.dynamic_update_index_in_dim(out_pieces, part, (z - k) % planes, 0)
+
+    dtok, dense_grad, dnorm = backward(
+        row, norms, dense_full, qf, kf, qkv, o, lse, hres, dxn2, gm, HEADS
+    )
+    norm_cols = jnp.sum(dnorm, axis=1).T.astype(BF16)
+    terms = jnp.concatenate(
+        [dense_grad, norm_cols, jnp.zeros((width, 128 - norm_cols.shape[1]), BF16)], axis=1
+    )
+    pieces, shard = leave(
+        dtok.reshape(planes, piece, width),
+        terms.reshape(groups, width // groups, terms.shape[1]),
+        planes,
+        groups,
+    )
+    output, d_tokens = pick_rows(my_order, (out_pieces, pieces), (BF16, F32))
+
+    dgate_all = small_all[:, 0, :tasks].T
+    dgates = jnp.sum(dgate_all[:, None, :] * choose, axis=-1)
+    (dlogits,) = gate_back(dgates)
+    d_task_embed = jnp.dot(dlogits, w_gate.astype(F32).T, precision=exact)
+    d_w_gate = jnp.dot(task_embed.astype(F32).T, dlogits, precision=exact)
+    my_small = lax.dynamic_index_in_dim(small_all, me, 0, keepdims=False)
+    cut = 1 + hidden // 128
+    d_b_up = lax.dynamic_slice_in_dim(
+        my_small[1:cut].reshape(hidden), z * (hidden // planes), hidden // planes, 0
+    )
+    d_b_down = lax.dynamic_slice_in_dim(
+        my_small[cut : cut + width // 128].reshape(width), z * (width // planes), width // planes, 0
+    )
+    return (
+        output,
+        d_tokens,
+        shard[:, 4 * width],
+        shard[:, 4 * width + 1],
+        shard[:, : 3 * width],
+        shard[:, 3 * width : 4 * width],
+        shard[:, 4 * width + 2],
+        shard[:, 4 * width + 3],
+        d_task_embed,
+        d_w_gate,
+        d_w_up[None],
+        d_b_up[None],
+        d_w_down[None],
+        d_b_down[None],
+    )
+
+
+def fits_rows(mesh, tokens, w_gate):
+    groups, planes = mesh.shape["dp"], mesh.shape["fsdp"]
+    return (
+        groups == 8
+        and tokens.shape[0] == groups * planes
+        and w_gate.shape[1] == groups
+        and tokens.shape[1] % (planes * QCHUNK) == 0
+    )
+
+
 def solution(mesh):
     placed = (
         P("dp", "fsdp", None),
@@ -354,25 +1565,32 @@
         P("dp", "fsdp", None),
         P("dp", "fsdp"),
     )
-    return jax.shard_map(
-        shards,
-        mesh=mesh,
-        in_specs=placed,
-        out_specs=(
-            P("dp", "fsdp", None),
-            P("dp", "fsdp", None),
-            P(("dp", "fsdp")),
-            P(("dp", "fsdp")),
-            P(("dp", "fsdp"), None),
-            P(("dp", "fsdp"), None),
-            P(("dp", "fsdp")),
-            P(("dp", "fsdp")),
-            P(None, ("dp", "fsdp")),
-            P(("dp", "fsdp"), None),
-            P("dp", "fsdp", None),
-            P("dp", "fsdp"),
-            P("dp", "fsdp", None),
-            P("dp", "fsdp"),
-        ),
-        check_vma=False,
-    )
+    placed_out = (
+        P("dp", "fsdp", None),
+        P("dp", "fsdp", None),
+        P(("dp", "fsdp")),
+        P(("dp", "fsdp")),
+        P(("dp", "fsdp"), None),
+        P(("dp", "fsdp"), None),
+        P(("dp", "fsdp")),
+        P(("dp", "fsdp")),
+        P(None, ("dp", "fsdp")),
+        P(("dp", "fsdp"), None),
+        P("dp", "fsdp", None),
+        P("dp", "fsdp"),
+        P("dp", "fsdp", None),
+        P("dp", "fsdp"),
+    )
+
+    def program(*args):
+        fast = fits_rows(mesh, args[0], args[13])
+        sizes = (mesh.shape["dp"], mesh.shape["fsdp"])
+        return jax.shard_map(
+            functools.partial(fast_shards, sizes) if fast else shards,
+            mesh=mesh,
+            in_specs=placed,
+            out_specs=placed_out,
+            check_vma=False,
+        )(*args)
+
+    return program

time: 1840 us -> 735 us (0.40)
  waiting for transfers between devices: 874 us -> 172 us
  Pallas kernels: 0 us -> 439 us
  blocking collectives: 343 us -> 0 us
  matrix products: 318 us -> 2.6 us
  local copies, waits for them, and re-layouts: 165 us -> 21.4 us
  other arithmetic: 74.1 us -> 25.6 us
  starting transfers between devices: 32.7 us -> 59.7 us
    reduce_scatter x7 -> x0, waiting for transfers between devices: 548 us -> none  [the longest x1 135 us: shards(): lax.psum_scatter(grad_proj, ('dp', 'fsdp'), scatter_dimension=0, tiled=True)]
    pallas_call x0 -> x10, Pallas kernels: none -> 439 us  [the longest x1 123 us: plane_gather(): pl.pallas_call(plane_gather_kernel, out_shape=jax.ShapeDtypeStruct((group...]
    dot_general x87 -> x4, matrix products: 318 us -> 2.6 us  [the longest x1 0.85 us: fast_shards(): jnp.dot(task_embed.astype(F32), w_gate.astype(F32), precision=exact)]
    all_gather x6 -> x0, blocking collectives: 265 us -> none  [the longest x1 114 us: shards(): lax.all_gather(w_proj, ('dp', 'fsdp'), axis=0, tiled=True)]
    ppermute x0 -> x32, waiting for transfers between devices: none -> 172 us  [the longest x18 88.8 us: z_shift(): lax.ppermute(x, 'fsdp', [(i, (i + k) % planes) for i in range(planes)])]
    unnamed x18 -> x0, waiting for transfers between devices: 163 us -> none
    all_to_all x4 -> x0, waiting for transfers between devices: 91.1 us -> none  [the longest x1 45.6 us: shards(): lax.all_to_all(grad_slots.reshape(received.shape), 'dp', split_axis=0, co...]
    unnamed x2 -> x0, blocking collectives: 78.3 us -> none
  transfers between devices with their start and end apart: 19 -> 32, of which waited for: 15 -> 10; matrix products, arithmetic and copies ran while one was open for 7% -> 5% of each run, Pallas kernels for 0% -> 33%
where the time goes in v1:
time: 735 us; the launch traced here: 723 us
  Pallas kernels  439 us (60%)
  waiting for transfers between devices  172 us (23%)
  starting transfers between devices  59.7 us (8%)
  other arithmetic  25.6 us (3%)
  local copies, waits for them, and re-layouts  21.4 us (3%)
    pallas_call x1, Pallas kernels, plane_gather(): pl.pallas_call(plane_gather_kernel, out_shape=jax.ShapeDtypeStruct((group...  123 us
    pallas_call x1, Pallas kernels, experts(): pl.pallas_call(functools.partial(expert_kernel, planes, groups), out_shap...  96.7 us
    ppermute x18, waiting for transfers between devices, z_shift(): lax.ppermute(x, 'fsdp', [(i, (i + k) % planes) for i in range(planes)])  88.8 us
    ppermute x14, waiting for transfers between devices, d_swap(): return lax.ppermute(x, 'dp', [(i, i ^ k) for i in range(groups)])  83 us
    pallas_call x1, Pallas kernels, plane_scatter(): pl.pallas_call(functools.partial(plane_scatter_kernel, planes, groups), o...  54.1 us
    pallas_call x1, Pallas kernels, backward(): pl.pallas_call(functools.partial(backward_kernel, heads), out_shape=(jax....  46.1 us
    pallas_call x1, Pallas kernels, forward(): pl.pallas_call(functools.partial(forward_kernel, heads), out_shape=(jax.S...  34.2 us
    ppermute x18, starting transfers between devices, z_shift(): lax.ppermute(x, 'fsdp', [(i, (i + k) % planes) for i in range(planes)])  32.3 us
  transfers between devices with their start and end apart: 32, of which 10 were waited for; matrix products, arithmetic and copies ran while one was open for 5% of the time, Pallas kernels for 33%

profile of v1, /device:TPU:25, one launch (start us, length us, event | category | flops | bytes accessed | tf_op | source)
XLA Modules:
  0.0 723.4 jit_solution(13629497939262267727)
XLA Ops:
  6.6 11.9 %routing_gather.1 = f32[8,4,16,128]{3,2,1,0:T(8,128)} custom-call(f32[16,128]{1,0:T(8,128)} %bitcast.148), custom_call_target="tpu_custom_call" | custom-call | tf_op jit(solution)/shard_map/routing_gather/pallas_call | solution.py:498
  22.7 4.4 row_order.2
  27.2 31.7 %rows_and_dense_weights.1 = (bf16[4,256,512]{2,1,0:T(8,128)(2,1)}, bf16[8,64,2048]{2,1,0:T(8,128)(2,1)}) custom-call(bf16[4,256,512]{2,1,0:T(8,128)(2,1)} %get-tuple-element.76.tok_ref, bf16[16,2048]{1,0:T(8,128)(2,1)} %pad_maximum_fusion.w_ref), custom_call_target="tpu_custom_call" | custom-call | tf_op jit(solution)/shard_map/rows_and_dense_weights/pallas_call | solution.py:538
  60.4 2.3 collective-permute-start.12
  71.2 34.2 %attention_forward.1 = (bf16[1024,1536]{1,0:T(8,128)(2,1)}, bf16[1024,512]{1,0:T(8,128)(2,1)}, f32[1024,512]{1,0:T(8,128)}, f32[1024,512]{1,0:T(8,128)}, bf16[1024,512]{1,0:T(8,128)(2,1)}) custom-call(bf16[1024,512]{1,0:T(8,128)(2,1)} %bitcast.163, f32[8,512]{1,0:T(8,128)} %concatenate.24.norm_ref, bf16[512,2048]{1,0:T(8,128)(2,1)} %bitcast.161, ...), custom_call_target="tpu_custom_call" | custom-call | flops 40000000000 | bytes 10000000 | tf_op jit(solution)/shard_map/attention_forward/pallas_call | solution.py:889
  105.5 18.5 %collective-permute-start.2 = (bf16[256,512]{1,0:T(8,128)(2,1)S(1)}, bf16[256,512]{1,0:T(8,128)(2,1)S(1)}, u32[]{:S(2)}, u32[]{:S(2)}) collective-permute-start(bf16[256,512]{1,0:T(8,128)(2,1)S(1)} %get-tuple-element.146), channel_id=1, source_target_pairs={{0,3},{1,0},{2,1},{3,2},{4,7},{5,4},{6,5},{7,6},{8,11},{9,8},{10,9... | collective-permute-start | bytes 786440 | tf_op jit(solution)/shard_map/ppermute | solution.py:1335
  124.0 5.3 collective-permute-done.1
  129.5 3.3 collective-permute-start.15
  132.8 2.7 collective-permute-start.3
  136.4 5.6 select_select_fusion.refs_1_
  143.6 5.0 collective-permute-start.5
  148.6 17.5 %collective-permute-done.14.refs_18_ = bf16[512,512]{1,0:T(8,128)(2,1)} collective-permute-done((bf16[512,512]{1,0:T(8,128)(2,1)}, bf16[512,512]{1,0:T(8,128)(2,1)}, u32[]{:S(2)}, u32[]{:S(2)}) %collective-permute-start.14) | collective-permute-done | bytes 524320 | tf_op jit(solution)/shard_map/ppermute | solution.py:1335
  167.1 3.0 collective-permute-start.7
  172.3 123.4 %expert_rows_gather.1.refs_3_ = bf16[8,1024,512]{2,1,0:T(8,128)(2,1)} custom-call(bf16[1024,512]{1,0:T(8,128)(2,1)} %get-tuple-element.81.in_ref.refs_2_), custom_call_target="tpu_custom_call" | custom-call | tf_op jit(solution)/shard_map/expert_rows_gather/pallas_call | solution.py:567
  299.8 96.7 %experts.1 = (bf16[8,1024,512]{2,1,0:T(8,128)(2,1)}, bf16[1024,512]{1,0:T(8,128)(2,1)}, bf16[1024,512]{1,0:T(8,128)(2,1)}, bf16[1024,512]{1,0:T(8,128)(2,1)}, bf...) custom-call(s32[513]{0:T(1024)} %pad_add_fusion.refs_0_, ...), custom_call_target="tpu_custom_call" | custom-call | flops 60000002048 | bytes 40000000 | tf_op jit(solution)/shard_map/experts/pallas_call | solution.py:1259
  399.4 54.1 %expert_grads_scatter.1 = (f32[1024,512]{1,0:T(8,128)}, f32[8,24,128]{2,1,0:T(8,128)}) custom-call(bf16[8,1024,512]{2,1,0:T(8,128)(2,1)} %get-tuple-element.101.z_ref, f32[24,128]{1,0:T(8,128)} %maximum_maximum_fusion.small_ref), custom_call_target="tpu_custom_call" | custom-call | tf_op jit(solution)/shard_map/expert_grads_scatter/pallas_call | solution.py:687
  453.9 2.7 collective-permute-start.17
  456.6 46.1 %attention_backward.1 = (bf16[1024,512]{1,0:T(8,128)(2,1)}, bf16[512,2048]{1,0:T(8,128)(2,1)}, f32[4,8,512]{2,1,0:T(8,128)}) custom-call(bf16[1024,512]{1,0:T(8,128)(2,1)} %bitcast.164, f32[8,512]{1,0:T(8,128)} %concatenate.24.norm_ref, bf16[512,2048]{1,0:T(8,128)(2,1)} %bitcast.162, bf16[1024,128]{1,0:T(8,128)(2,1)} %fusion.6.qf_ref, ...), custom_call_target="tpu_custom_call" | custom-call | flops 80000000000 | bytes 20000000 | tf_op jit(solution)/shard_map/attention_backward/pallas_call | solution.py:1072
  503.8 4.6 concatenate.27
  508.4 31.9 %grads_and_rows_back.1 = (bf16[4,256,512]{2,1,0:T(8,128)(2,1)}, f32[16,2176]{1,0:T(8,128)}) custom-call(bf16[4,256,512]{2,1,0:T(8,128)(2,1)} %bitcast.126, bf16[8,64,2176]{2,1,0:T(8,128)(2,1)} %bitcast.124), custom_call_target="tpu_custom_call" | custom-call | tf_op jit(solution)/shard_map/grads_and_rows_back/pallas_call | solution.py:755
  540.3 1.7 slice.72
  550.1 5.8 collective-permute-done.26
  555.9 3.5 collective-permute-start.18
  559.4 28.7 %collective-permute-done.27 = bf16[128,2048]{1,0:T(8,128)(2,1)S(1)} collective-permute-done((bf16[128,2048]{1,0:T(8,128)(2,1)}, bf16[128,2048]{1,0:T(8,128)(2,1)S(1)}, u32[]{:S(2)}, u32[]{:S(2)}) %collective-permute-start.27) | collective-permute-done | bytes 524320 | tf_op jit(solution)/shard_map/ppermute | solution.py:1335
  589.0 3.5 collective-permute-start.20
  597.6 57.5 %collective-permute-done.19 = bf16[1024,512]{1,0:T(8,128)(2,1)S(1)} collective-permute-done((bf16[1024,512]{1,0:T(8,128)(2,1)}, bf16[1024,512]{1,0:T(8,128)(2,1)S(1)}, u32[]{:S(2)}, u32[]{:S(2)}) %collective-permute-start.19) | collective-permute-done | bytes 1048608 | tf_op jit(solution)/shard_map/ppermute | solution.py:1338
  655.1 25.5 %collective-permute-done.20 = bf16[1024,512]{1,0:T(8,128)(2,1)S(1)} collective-permute-done((bf16[1024,512]{1,0:T(8,128)(2,1)}, bf16[1024,512]{1,0:T(8,128)(2,1)S(1)}, u32[]{:S(2)}, u32[]{:S(2)}) %collective-permute-start.20) | collective-permute-done | bytes 1048608 | tf_op jit(solution)/shard_map/ppermute | solution.py:1338
  682.1 3.3 collective-permute-start.23
  685.5 11.1 %collective-permute-done.31 = bf16[512,512]{1,0:T(8,128)(2,1)S(1)} collective-permute-done((bf16[512,512]{1,0:T(8,128)(2,1)}, bf16[512,512]{1,0:T(8,128)(2,1)S(1)}, u32[]{:S(2)}, u32[]{:S(2)}) %collective-permute-start.31) | collective-permute-done | bytes 524320 | tf_op jit(solution)/shard_map/ppermute | solution.py:1335
  697.8 5.1 collective-permute-done.23
  702.9 14.8 %collective-permute-done.24 = bf16[256,512]{1,0:T(8,128)(2,1)S(1)} collective-permute-done((bf16[256,512]{1,0:T(8,128)(2,1)S(1)}, bf16[256,512]{1,0:T(8,128)(2,1)S(1)}, u32[]{:S(2)}, u32[]{:S(2)}) %collective-permute-start.24) | collective-permute-done | bytes 262176 | tf_op jit(solution)/shard_map/ppermute | solution.py:1335
  718.8 4.6 row_order.3
  (194 shorter events, 50.1 us)
Async XLA Ops:
  58.8 70.6 %collective-permute-start.10 = (bf16[128,2048]{1,0:T(8,128)(2,1)}, bf16[128,2048]{1,0:T(8,128)(2,1)}, u32[]{:S(2)}, u32[]{:S(2)}) collective-permute-start(bf16[128,2048]{1,0:T(8,128)(2,1)} %bitcast.28.refs_12_), channel_id=1, source_target_pairs={{0,3},{1,0},{2,1},{3,2},{4,7},{5,4},{6,5},{7,6},{8,11},{9,8},{10,9... | collective-permute-start | bytes 1572872 | tf_op jit(solution)/shard_map/ppermute | solution.py:1335
  58.9 73.9 %collective-permute-start.11 = (bf16[128,2048]{1,0:T(8,128)(2,1)}, bf16[128,2048]{1,0:T(8,128)(2,1)}, u32[]{:S(2)}, u32[]{:S(2)}) collective-permute-start(bf16[128,2048]{1,0:T(8,128)(2,1)} %bitcast.28.refs_12_), channel_id=1, source_target_pairs={{0,2},{1,3},{2,0},{3,1},{4,6},{5,7},{6,4},{7,5},{8,10},{9,11},{10,... | collective-permute-start | bytes 1572872 | tf_op jit(solution)/shard_map/ppermute | solution.py:1335
  60.4 75.0 %collective-permute-start.12 = (bf16[128,2048]{1,0:T(8,128)(2,1)}, bf16[128,2048]{1,0:T(8,128)(2,1)}, u32[]{:S(2)}, u32[]{:S(2)}) collective-permute-start(bf16[128,2048]{1,0:T(8,128)(2,1)} %bitcast.28.refs_12_), channel_id=1, source_target_pairs={{0,1},{1,2},{2,3},{3,0},{4,5},{5,6},{6,7},{7,4},{8,9},{9,10},{10,1... | collective-permute-start | bytes 1572872 | tf_op jit(solution)/shard_map/ppermute | solution.py:1335
  62.9 42.6 %collective-permute-start = (bf16[256,512]{1,0:T(8,128)(2,1)S(1)}, bf16[256,512]{1,0:T(8,128)(2,1)S(1)}, u32[]{:S(2)}, u32[]{:S(2)}) collective-permute-start(bf16[256,512]{1,0:T(8,128)(2,1)S(1)} %get-tuple-element.148), channel_id=1, source_target_pairs={{0,1},{1,2},{2,3},{3,0},{4,5},{5,6},{6,7},{7,4},{8,9},{9,10},{10,1... | collective-permute-start | bytes 786440 | tf_op jit(solution)/shard_map/ppermute | solution.py:1335
  63.0 66.3 %collective-permute-start.1 = (bf16[256,512]{1,0:T(8,128)(2,1)S(1)}, bf16[256,512]{1,0:T(8,128)(2,1)S(1)}, u32[]{:S(2)}, u32[]{:S(2)}) collective-permute-start(bf16[256,512]{1,0:T(8,128)(2,1)S(1)} %get-tuple-element.147), channel_id=1, source_target_pairs={{0,2},{1,3},{2,0},{3,1},{4,6},{5,7},{6,4},{7,5},{8,10},{9,11},{10,... | collective-permute-start | bytes 786440 | tf_op jit(solution)/shard_map/ppermute | solution.py:1335
  105.5 23.8 %collective-permute-start.2 = (bf16[256,512]{1,0:T(8,128)(2,1)S(1)}, bf16[256,512]{1,0:T(8,128)(2,1)S(1)}, u32[]{:S(2)}, u32[]{:S(2)}) collective-permute-start(bf16[256,512]{1,0:T(8,128)(2,1)S(1)} %get-tuple-element.146), channel_id=1, source_target_pairs={{0,3},{1,0},{2,1},{3,2},{4,7},{5,4},{6,5},{7,6},{8,11},{9,8},{10,9... | collective-permute-start | bytes 786440 | tf_op jit(solution)/shard_map/ppermute | solution.py:1335
  129.3 14.3 %collective-permute-start.13 = (bf16[512,512]{1,0:T(8,128)(2,1)}, bf16[512,512]{1,0:T(8,128)(2,1)}, u32[]{:S(2)}, u32[]{:S(2)}) collective-permute-start(bf16[512,512]{1,0:T(8,128)(2,1)} %bitcast.165), channel_id=1, source_target_pairs={{0,3},{1,0},{2,1},{3,2},{4,7},{5,4},{6,5},{7,6},{8,11},{9,8},{10,9... | collective-permute-start | bytes 1572872 | tf_op jit(solution)/shard_map/ppermute | solution.py:1335
  129.3 36.8 %collective-permute-start.14 = (bf16[512,512]{1,0:T(8,128)(2,1)}, bf16[512,512]{1,0:T(8,128)(2,1)}, u32[]{:S(2)}, u32[]{:S(2)}) collective-permute-start(bf16[512,512]{1,0:T(8,128)(2,1)} %bitcast.166), channel_id=1, source_target_pairs={{0,2},{1,3},{2,0},{3,1},{4,6},{5,7},{6,4},{7,5},{8,10},{9,11},{10,... | collective-permute-start | bytes 1572872 | tf_op jit(solution)/shard_map/ppermute | solution.py:1335
  129.5 37.6 %collective-permute-start.15 = (bf16[512,512]{1,0:T(8,128)(2,1)}, bf16[512,512]{1,0:T(8,128)(2,1)}, u32[]{:S(2)}, u32[]{:S(2)}) collective-permute-start(bf16[512,512]{1,0:T(8,128)(2,1)} %bitcast.167), channel_id=1, source_target_pairs={{0,1},{1,2},{2,3},{3,0},{4,5},{5,6},{6,7},{7,4},{8,9},{9,10},{10,1... | collective-permute-start | bytes 1572872 | tf_op jit(solution)/shard_map/ppermute | solution.py:1335
  132.8 37.3 %collective-permute-start.3 = (bf16[1024,512]{1,0:T(8,128)(2,1)S(1)}, bf16[1024,512]{1,0:T(8,128)(2,1)S(1)}, u32[]{:S(2)}, u32[]{:S(2)}) collective-permute-start(bf16[1024,512]{1,0:T(8,128)(2,1)S(1)} %bitcast.127), channel_id=1, source_target_pairs={{0,4},{4,0},{8,12},{12,8},{16,20},{20,16},{24,28},{28,24},{1,5},{5... | collective-permute-start | bytes 3145736 | tf_op jit(solution)/shard_map/ppermute | solution.py:1338
  135.4 35.5 %collective-permute-start.4 = (bf16[1024,512]{1,0:T(8,128)(2,1)S(1)}, bf16[1024,512]{1,0:T(8,128)(2,1)}, u32[]{:S(2)}, u32[]{:S(2)}) collective-permute-start(bf16[1024,512]{1,0:T(8,128)(2,1)S(1)} %bitcast.128), channel_id=1, source_target_pairs={{0,8},{4,12},{8,0},{12,4},{16,24},{20,28},{24,16},{28,20},{1,9},{5... | collective-permute-start | bytes 3145736 | tf_op jit(solution)/shard_map/ppermute | solution.py:1338
  143.6 156.1 %collective-permute-start.5 = (bf16[1024,512]{1,0:T(8,128)(2,1)S(1)}, bf16[1024,512]{1,0:T(8,128)(2,1)}, u32[]{:S(2)}, u32[]{:S(2)}) collective-permute-start(bf16[1024,512]{1,0:T(8,128)(2,1)S(1)} %bitcast.129), channel_id=1, source_target_pairs={{0,12},{4,8},{8,4},{12,0},{16,28},{20,24},{24,20},{28,16},{1,13},{... | collective-permute-start | bytes 3145736 | tf_op jit(solution)/shard_map/ppermute | solution.py:1338
  166.1 133.6 %collective-permute-start.6 = (bf16[1024,512]{1,0:T(8,128)(2,1)S(1)}, bf16[1024,512]{1,0:T(8,128)(2,1)}, u32[]{:S(2)}, u32[]{:S(2)}) collective-permute-start(bf16[1024,512]{1,0:T(8,128)(2,1)S(1)} %bitcast.130), channel_id=1, source_target_pairs={{0,16},{4,20},{8,24},{12,28},{16,0},{20,4},{24,8},{28,12},{1,17},{... | collective-permute-start | bytes 3145736 | tf_op jit(solution)/shard_map/ppermute | solution.py:1338
  167.1 132.6 %collective-permute-start.7 = (bf16[1024,512]{1,0:T(8,128)(2,1)S(1)}, bf16[1024,512]{1,0:T(8,128)(2,1)}, u32[]{:S(2)}, u32[]{:S(2)}) collective-permute-start(bf16[1024,512]{1,0:T(8,128)(2,1)S(1)} %bitcast.131), channel_id=1, source_target_pairs={{0,20},{4,16},{8,28},{12,24},{16,4},{20,0},{24,12},{28,8},{1,21},{... | collective-permute-start | bytes 3145736 | tf_op jit(solution)/shard_map/ppermute | solution.py:1338
  170.1 129.7 %collective-permute-start.8 = (bf16[1024,512]{1,0:T(8,128)(2,1)S(1)}, bf16[1024,512]{1,0:T(8,128)(2,1)}, u32[]{:S(2)}, u32[]{:S(2)}) collective-permute-start(bf16[1024,512]{1,0:T(8,128)(2,1)S(1)} %bitcast.132), channel_id=1, source_target_pairs={{0,24},{4,28},{8,16},{12,20},{16,8},{20,12},{24,0},{28,4},{1,25},{... | collective-permute-start | bytes 3145736 | tf_op jit(solution)/shard_map/ppermute | solution.py:1338
  171.0 128.8 %collective-permute-start.9 = (bf16[1024,512]{1,0:T(8,128)(2,1)S(1)}, bf16[1024,512]{1,0:T(8,128)(2,1)}, u32[]{:S(2)}, u32[]{:S(2)}) collective-permute-start(bf16[1024,512]{1,0:T(8,128)(2,1)S(1)} %bitcast.133), channel_id=1, source_target_pairs={{0,28},{4,24},{8,20},{12,16},{16,12},{20,8},{24,4},{28,0},{1,29},{... | collective-permute-start | bytes 3145736 | tf_op jit(solution)/shard_map/ppermute | solution.py:1338
  453.6 139.0 %collective-permute-start.16 = (bf16[1024,512]{1,0:T(8,128)(2,1)}, bf16[1024,512]{1,0:T(8,128)(2,1)S(1)}, u32[]{:S(2)}, u32[]{:S(2)}) collective-permute-start(bf16[1024,512]{1,0:T(8,128)(2,1)} %get-tuple-element.107), channel_id=1, source_target_pairs={{0,4},{4,0},{8,12},{12,8},{16,20},{20,16},{24,28},{28,24},{1,5},{5... | collective-permute-start | bytes 3145736 | tf_op jit(solution)/shard_map/ppermute | solution.py:1338
  453.9 140.0 %collective-permute-start.17 = (bf16[1024,512]{1,0:T(8,128)(2,1)}, bf16[1024,512]{1,0:T(8,128)(2,1)S(1)}, u32[]{:S(2)}, u32[]{:S(2)}) collective-permute-start(bf16[1024,512]{1,0:T(8,128)(2,1)} %get-tuple-element.108), channel_id=1, source_target_pairs={{0,8},{4,12},{8,0},{12,4},{16,24},{20,28},{24,16},{28,20},{1,9},{5... | collective-permute-start | bytes 3145736 | tf_op jit(solution)/shard_map/ppermute | solution.py:1338
  543.4 12.5 %collective-permute-start.26 = (bf16[128,2048]{1,0:T(8,128)(2,1)}, bf16[128,2048]{1,0:T(8,128)(2,1)S(1)}, u32[]{:S(2)}, u32[]{:S(2)}) collective-permute-start(bf16[128,2048]{1,0:T(8,128)(2,1)} %get-tuple-element.127), channel_id=1, source_target_pairs={{0,1},{1,2},{2,3},{3,0},{4,5},{5,6},{6,7},{7,4},{8,9},{9,10},{10,1... | collective-permute-start | bytes 1572872 | tf_op jit(solution)/shard_map/ppermute | solution.py:1335
  543.6 44.6 %collective-permute-start.27 = (bf16[128,2048]{1,0:T(8,128)(2,1)}, bf16[128,2048]{1,0:T(8,128)(2,1)S(1)}, u32[]{:S(2)}, u32[]{:S(2)}) collective-permute-start(bf16[128,2048]{1,0:T(8,128)(2,1)} %get-tuple-element.128), channel_id=1, source_target_pairs={{0,2},{1,3},{2,0},{3,1},{4,6},{5,7},{6,4},{7,5},{8,10},{9,11},{10,... | collective-permute-start | bytes 1572872 | tf_op jit(solution)/shard_map/ppermute | solution.py:1335
  544.1 44.9 %collective-permute-start.28 = (bf16[128,2048]{1,0:T(8,128)(2,1)}, bf16[128,2048]{1,0:T(8,128)(2,1)S(1)}, u32[]{:S(2)}, u32[]{:S(2)}) collective-permute-start(bf16[128,2048]{1,0:T(8,128)(2,1)} %get-tuple-element.129), channel_id=1, source_target_pairs={{0,3},{1,0},{2,1},{3,2},{4,7},{5,4},{6,5},{7,6},{8,11},{9,8},{10,9... | collective-permute-start | bytes 1572872 | tf_op jit(solution)/shard_map/ppermute | solution.py:1335
  555.9 41.8 %collective-permute-start.18 = (bf16[1024,512]{1,0:T(8,128)(2,1)}, bf16[1024,512]{1,0:T(8,128)(2,1)S(1)}, u32[]{:S(2)}, u32[]{:S(2)}) collective-permute-start(bf16[1024,512]{1,0:T(8,128)(2,1)} %get-tuple-element.109), channel_id=1, source_target_pairs={{0,12},{4,8},{8,4},{12,0},{16,28},{20,24},{24,20},{28,16},{1,13},{... | collective-permute-start | bytes 3145736 | tf_op jit(solution)/shard_map/ppermute | solution.py:1338
  588.1 67.0 %collective-permute-start.19 = (bf16[1024,512]{1,0:T(8,128)(2,1)}, bf16[1024,512]{1,0:T(8,128)(2,1)S(1)}, u32[]{:S(2)}, u32[]{:S(2)}) collective-permute-start(bf16[1024,512]{1,0:T(8,128)(2,1)} %get-tuple-element.110), channel_id=1, source_target_pairs={{0,16},{4,20},{8,24},{12,28},{16,0},{20,4},{24,8},{28,12},{1,17},{... | collective-permute-start | bytes 3145736 | tf_op jit(solution)/shard_map/ppermute | solution.py:1338
  589.0 91.6 %collective-permute-start.20 = (bf16[1024,512]{1,0:T(8,128)(2,1)}, bf16[1024,512]{1,0:T(8,128)(2,1)S(1)}, u32[]{:S(2)}, u32[]{:S(2)}) collective-permute-start(bf16[1024,512]{1,0:T(8,128)(2,1)} %get-tuple-element.111), channel_id=1, source_target_pairs={{0,20},{4,16},{8,28},{12,24},{16,4},{20,0},{24,12},{28,8},{1,21},{... | collective-permute-start | bytes 3145736 | tf_op jit(solution)/shard_map/ppermute | solution.py:1338
  592.6 88.1 %collective-permute-start.21 = (bf16[1024,512]{1,0:T(8,128)(2,1)}, bf16[1024,512]{1,0:T(8,128)(2,1)S(1)}, u32[]{:S(2)}, u32[]{:S(2)}) collective-permute-start(bf16[1024,512]{1,0:T(8,128)(2,1)} %get-tuple-element.112), channel_id=1, source_target_pairs={{0,24},{4,28},{8,16},{12,20},{16,8},{20,12},{24,0},{28,4},{1,25},{... | collective-permute-start | bytes 3145736 | tf_op jit(solution)/shard_map/ppermute | solution.py:1338
  593.9 86.8 %collective-permute-start.22 = (bf16[1024,512]{1,0:T(8,128)(2,1)S(1)}, bf16[1024,512]{1,0:T(8,128)(2,1)S(1)}, u32[]{:S(2)}, u32[]{:S(2)}) collective-permute-start(bf16[1024,512]{1,0:T(8,128)(2,1)S(1)} %copy-done.15), channel_id=1, source_target_pairs={{0,28},{4,24},{8,20},{12,16},{16,12},{20,8},{24,4},{28,0},{1,29},{... | collective-permute-start | bytes 3145736 | tf_op jit(solution)/shard_map/ppermute | solution.py:1338
  597.6 87.8 %collective-permute-start.29 = (bf16[512,512]{1,0:T(8,128)(2,1)}, bf16[512,512]{1,0:T(8,128)(2,1)S(1)}, u32[]{:S(2)}, u32[]{:S(2)}) collective-permute-start(bf16[512,512]{1,0:T(8,128)(2,1)} %get-tuple-element.131), channel_id=1, source_target_pairs={{0,1},{1,2},{2,3},{3,0},{4,5},{5,6},{6,7},{7,4},{8,9},{9,10},{10,1... | collective-permute-start | bytes 1572872 | tf_op jit(solution)/shard_map/ppermute | solution.py:1335
  655.1 30.3 %collective-permute-start.30 = (bf16[512,512]{1,0:T(8,128)(2,1)}, bf16[512,512]{1,0:T(8,128)(2,1)S(1)}, u32[]{:S(2)}, u32[]{:S(2)}) collective-permute-start(bf16[512,512]{1,0:T(8,128)(2,1)} %get-tuple-element.132), channel_id=1, source_target_pairs={{0,2},{1,3},{2,0},{3,1},{4,6},{5,7},{6,4},{7,5},{8,10},{9,11},{10,... | collective-permute-start | bytes 1572872 | tf_op jit(solution)/shard_map/ppermute | solution.py:1335
  680.6 15.9 %collective-permute-start.31 = (bf16[512,512]{1,0:T(8,128)(2,1)}, bf16[512,512]{1,0:T(8,128)(2,1)S(1)}, u32[]{:S(2)}, u32[]{:S(2)}) collective-permute-start(bf16[512,512]{1,0:T(8,128)(2,1)} %get-tuple-element.133), channel_id=1, source_target_pairs={{0,3},{1,0},{2,1},{3,2},{4,7},{5,4},{6,5},{7,6},{8,11},{9,8},{10,9... | collective-permute-start | bytes 1572872 | tf_op jit(solution)/shard_map/ppermute | solution.py:1335
  682.1 20.8 %collective-permute-start.23 = (bf16[256,512]{1,0:T(8,128)(2,1)S(1)}, bf16[256,512]{1,0:T(8,128)(2,1)S(1)}, u32[]{:S(2)}, u32[]{:S(2)}) collective-permute-start(bf16[256,512]{1,0:T(8,128)(2,1)S(1)} %get-tuple-element.144), channel_id=1, source_target_pairs={{0,1},{1,2},{2,3},{3,0},{4,5},{5,6},{6,7},{7,4},{8,9},{9,10},{10,1... | collective-permute-start | bytes 786440 | tf_op jit(solution)/shard_map/ppermute | solution.py:1335
  685.5 32.3 %collective-permute-start.24 = (bf16[256,512]{1,0:T(8,128)(2,1)S(1)}, bf16[256,512]{1,0:T(8,128)(2,1)S(1)}, u32[]{:S(2)}, u32[]{:S(2)}) collective-permute-start(bf16[256,512]{1,0:T(8,128)(2,1)S(1)} %get-tuple-element.143), channel_id=1, source_target_pairs={{0,2},{1,3},{2,0},{3,1},{4,6},{5,7},{6,4},{7,5},{8,10},{9,11},{10,... | collective-permute-start | bytes 786440 | tf_op jit(solution)/shard_map/ppermute | solution.py:1335
  697.8 20.0 %collective-permute-start.25 = (bf16[256,512]{1,0:T(8,128)(2,1)S(1)}, bf16[256,512]{1,0:T(8,128)(2,1)S(1)}, u32[]{:S(2)}, u32[]{:S(2)}) collective-permute-start(bf16[256,512]{1,0:T(8,128)(2,1)S(1)} %get-tuple-element.142), channel_id=1, source_target_pairs={{0,3},{1,0},{2,1},{3,2},{4,7},{5,4},{6,5},{7,6},{8,11},{9,8},{10,9... | collective-permute-start | bytes 786440 | tf_op jit(solution)/shard_map/ppermute | solution.py:1335
  (17 other events, 951.7 us)

commit v2 on v1

v2 whole, which is shorter than its diff:
```python
import functools

import jax
import jax.numpy as jnp
from jax import lax
from jax.experimental import pallas as pl
from jax.experimental.pallas import tpu as pltpu
from jax.sharding import PartitionSpec as P

HEADS = 8
HD = 64


exact = lax.Precision.HIGHEST


def layer_norm(values_in, gain_vec, shift_vec):
    centre = values_in - jnp.mean(values_in, axis=-1, keepdims=True)
    spread = jnp.mean(centre * centre, axis=-1, keepdims=True)
    return centre * lax.rsqrt(spread + 1e-05) * gain_vec + shift_vec


def allow_table(query_codes, key_codes):
    query_int = query_codes.astype(jnp.int32)
    key_int = key_codes.astype(jnp.int32)
    same_sentence = (query_int // 2)[:, :, None] == (key_int // 2)[:, None, :]
    return same_sentence & ((key_int % 2)[:, None, :] == 1)


def row_scores(query_row, key_row, allow_row):
    scores = (
        jnp.einsum("qhd,khd->hqk", query_row, key_row, preferred_element_type=jnp.float32) * 0.125
    )
    return jnp.where(allow_row[None], scores, -1000000000.0)


def attend_forward(queries, key_heads, value_heads, allowed):

    def one_row(parts):
        query_row, key_row, value_row, allow_row = parts
        scores = row_scores(query_row, key_row, allow_row)
        biggest = jnp.max(scores, axis=-1, keepdims=True)
        weights = jnp.exp(scores - biggest)
        row_total = jnp.sum(weights, axis=-1, keepdims=True)
        weights_low = (weights / row_total).astype(jnp.bfloat16)
        mixed_row = jnp.einsum(
            "hqk,khd->qhd", weights_low, value_row, preferred_element_type=jnp.float32
        )
        return (mixed_row.astype(jnp.bfloat16), (biggest + jnp.log(row_total))[..., 0])

    return lax.map(one_row, (queries, key_heads, value_heads, allowed))


def attend_backward(queries, key_heads, value_heads, allowed, logsum, grad_out):

    def one_row(parts):
        query_row, key_row, value_row, allow_row, logsum_row, grad_row = parts
        scores = row_scores(query_row, key_row, allow_row)
        weights = jnp.exp(scores - logsum_row[..., None])
        grad_weights = jnp.einsum(
            "qhd,khd->hqk", grad_row, value_row, preferred_element_type=jnp.float32
        )
        inner = jnp.sum(weights * grad_weights, axis=-1, keepdims=True)
        grad_scores = (weights * (grad_weights - inner)).astype(jnp.bfloat16)
        grad_query = (
            jnp.einsum("hqk,khd->qhd", grad_scores, key_row, preferred_element_type=jnp.float32)
            * 0.125
        )
        grad_key = (
            jnp.einsum("hqk,qhd->khd", grad_scores, query_row, preferred_element_type=jnp.float32)
            * 0.125
        )
        grad_value = jnp.einsum(
            "hqk,qhd->khd",
            weights.astype(jnp.bfloat16),
            grad_row,
            preferred_element_type=jnp.float32,
        )
        return (grad_query, grad_key, grad_value)

    return lax.map(one_row, (queries, key_heads, value_heads, allowed, logsum, grad_out))


def shards(
    tokens,
    out_grad,
    segment_ids,
    key_mask,
    sent_task,
    task_experts,
    ln1_gain,
    ln1_bias,
    w_qkv,
    w_proj,
    ln2_gain,
    ln2_bias,
    task_embed,
    w_gate,
    w_up,
    b_up,
    w_down,
    b_down,
):
    row_count, piece_len, model_width = tokens.shape
    tok_count = row_count * piece_len
    gain_one, bias_one, qkv_full, proj_full, gain_two, bias_two, embed_full, router_full = (
        lax.all_gather(ln1_gain, ("dp", "fsdp"), axis=0, tiled=True),
        lax.all_gather(ln1_bias, ("dp", "fsdp"), axis=0, tiled=True),
        lax.all_gather(w_qkv, ("dp", "fsdp"), axis=0, tiled=True),
        lax.all_gather(w_proj, ("dp", "fsdp"), axis=0, tiled=True),
        lax.all_gather(ln2_gain, ("dp", "fsdp"), axis=0, tiled=True),
        lax.all_gather(ln2_bias, ("dp", "fsdp"), axis=0, tiled=True),
        lax.all_gather(task_embed, ("dp", "fsdp"), axis=1, tiled=True),
        lax.all_gather(w_gate, ("dp", "fsdp"), axis=0, tiled=True),
    )
    up_full, up_bias, down_full, down_bias = (
        lax.all_gather(w_up, "fsdp", axis=1, tiled=True),
        lax.all_gather(b_up, "fsdp", axis=1, tiled=True),
        lax.all_gather(w_down, "fsdp", axis=1, tiled=True),
        lax.all_gather(b_down, "fsdp", axis=1, tiled=True),
    )
    up_full = up_full[0]
    down_full = down_full[0]
    up_bias_f = up_bias[0].astype(jnp.float32)
    down_bias_f = down_bias[0].astype(jnp.float32)
    experts_count = router_full.shape[1]
    task_count = embed_full.shape[0]
    capacity = 4 * tok_count // experts_count
    inputs = tokens.astype(jnp.float32).reshape(tok_count, model_width)
    normed, norm_back = jax.vjp(
        layer_norm, inputs, gain_one.astype(jnp.float32), bias_one.astype(jnp.float32)
    )
    normed_low = normed.astype(jnp.bfloat16)
    projected = jnp.dot(normed_low, qkv_full, preferred_element_type=jnp.float32).astype(
        jnp.bfloat16
    )
    projected = projected.reshape(row_count, piece_len, 3, HEADS, HD)
    queries = projected[:, :, 0]
    key_heads = projected[:, :, 1]
    value_heads = projected[:, :, 2]
    row_codes = (2 * segment_ids + key_mask).astype(jnp.bfloat16)
    keys_all, values_all, codes_all = (
        lax.all_gather(key_heads, "fsdp", axis=1, tiled=True),
        lax.all_gather(value_heads, "fsdp", axis=1, tiled=True),
        lax.all_gather(row_codes, "fsdp", axis=1, tiled=True),
    )
    allowed = allow_table(row_codes, codes_all)
    attended, logsum = attend_forward(queries, keys_all, values_all, allowed)
    attended_flat = attended.reshape(tok_count, model_width)
    hidden = inputs + jnp.dot(attended_flat, proj_full, preferred_element_type=jnp.float32)
    normed_two, norm_two_back = jax.vjp(
        layer_norm, hidden, gain_two.astype(jnp.float32), bias_two.astype(jnp.float32)
    )
    normed_two_low = normed_two.astype(jnp.bfloat16)
    choose = (task_experts[:, :, None] == jnp.arange(experts_count)[None, None, :]).astype(
        jnp.float32
    )

    def gate_values(embed_in, router_in):
        logits = jnp.einsum(
            "te,tke->tk", jnp.dot(embed_in, router_in, precision=exact), choose, precision=exact
        )
        return jax.nn.softmax(logits, axis=-1)

    gate_probs, gate_back = jax.vjp(
        gate_values, embed_full.astype(jnp.float32), router_full.astype(jnp.float32)
    )
    segment_hot = (segment_ids[:, :, None] == jnp.arange(sent_task.shape[1])[None, None, :]).astype(
        jnp.int32
    )
    task_tok = jnp.sum(segment_hot * sent_task[:, None, :], axis=-1).reshape(tok_count)
    task_hot = (task_tok[:, None] == jnp.arange(task_count)[None, :]).astype(jnp.float32)
    gate_tok = jnp.dot(task_hot, gate_probs, precision=exact)
    expert_tok = jnp.sum(task_hot.astype(jnp.int32)[:, :, None] * task_experts[None], axis=1)
    copy_expert = expert_tok.T.reshape(-1)
    one_hot = (copy_expert[:, None] == jnp.arange(experts_count)[None, :]).astype(jnp.int32)
    rank = jnp.sum((jnp.cumsum(one_hot, axis=0) - one_hot) * one_hot, axis=-1)
    kept_copy = rank < capacity
    slot_index = jnp.where(kept_copy, copy_expert * capacity + rank, experts_count * capacity)
    send_rows = (
        jnp.zeros((experts_count * capacity + 1, model_width), jnp.bfloat16)
        .at[slot_index]
        .set(jnp.tile(normed_two_low, (2, 1)))
    )
    send_rows = send_rows[:-1].reshape(experts_count, capacity, model_width)
    received = lax.all_to_all(send_rows, "dp", split_axis=0, concat_axis=0, tiled=True)
    slot_total = received.shape[0] * received.shape[1]
    block_rows = min(512, slot_total)
    block_count = slot_total // block_rows
    slot_blocks = received.reshape(block_count, block_rows, model_width)

    def expert_forward(slot_rows):
        pre_act = jnp.dot(slot_rows, up_full, preferred_element_type=jnp.float32) + up_bias_f
        activated = jax.nn.gelu(pre_act, approximate=True).astype(jnp.bfloat16)
        return (
            jnp.dot(activated, down_full, preferred_element_type=jnp.float32) + down_bias_f
        ).astype(jnp.bfloat16)

    produced = lax.map(expert_forward, slot_blocks).reshape(received.shape)
    returned = lax.all_to_all(produced, "dp", split_axis=0, concat_axis=0, tiled=True)
    return_pad = jnp.concatenate(
        [returned.reshape(-1, model_width), jnp.zeros((1, model_width), jnp.bfloat16)], axis=0
    )
    copies = jnp.take(return_pad, slot_index, axis=0).reshape(2, tok_count, model_width)
    kept_float = kept_copy.reshape(2, tok_count).astype(jnp.float32)
    copy_weight = gate_tok.T * kept_float
    mixed_rows = (
        hidden
        + copy_weight[0][:, None] * copies[0].astype(jnp.float32)
        + copy_weight[1][:, None] * copies[1].astype(jnp.float32)
    )
    output = mixed_rows.astype(jnp.bfloat16).reshape(tokens.shape)
    grad_mixed = out_grad.astype(jnp.float32).reshape(tok_count, model_width)
    grad_copies = (copy_weight[:, :, None] * grad_mixed[None]).astype(jnp.bfloat16)
    grad_gate_copy = jnp.sum(copies.astype(jnp.float32) * grad_mixed[None], axis=-1) * kept_float
    grad_send = (
        jnp.zeros((experts_count * capacity + 1, model_width), jnp.bfloat16)
        .at[slot_index]
        .set(grad_copies.reshape(-1, model_width))
    )
    grad_send = grad_send[:-1].reshape(experts_count, capacity, model_width)
    grad_received = lax.all_to_all(grad_send, "dp", split_axis=0, concat_axis=0, tiled=True)

    def expert_backward(totals, parts):
        slot_rows, grad_rows = parts
        pre_act = jnp.dot(slot_rows, up_full, preferred_element_type=jnp.float32) + up_bias_f
        activated, gelu_back = jax.vjp(
            lambda values_in: jax.nn.gelu(values_in, approximate=True), pre_act
        )
        activated_low = activated.astype(jnp.bfloat16)
        grad_act = jnp.dot(grad_rows, down_full.T, preferred_element_type=jnp.float32)
        grad_pre = gelu_back(grad_act)[0].astype(jnp.bfloat16)
        grad_inputs_slot = jnp.dot(grad_pre, up_full.T, preferred_element_type=jnp.float32).astype(
            jnp.bfloat16
        )
        totals = (
            totals[0] + jnp.dot(slot_rows.T, grad_pre, preferred_element_type=jnp.float32),
            totals[1] + jnp.sum(grad_pre.astype(jnp.float32), axis=0),
            totals[2] + jnp.dot(activated_low.T, grad_rows, preferred_element_type=jnp.float32),
            totals[3] + jnp.sum(grad_rows.astype(jnp.float32), axis=0),
        )
        return (totals, grad_inputs_slot)

    start_totals = (
        jnp.zeros(up_full.shape, jnp.float32),
        jnp.zeros(up_bias_f.shape, jnp.float32),
        jnp.zeros(down_full.shape, jnp.float32),
        jnp.zeros(down_bias_f.shape, jnp.float32),
    )
    totals, grad_slots = lax.scan(
        expert_backward,
        start_totals,
        (slot_blocks, grad_received.reshape(block_count, block_rows, model_width)),
    )
    grad_back = lax.all_to_all(
        grad_slots.reshape(received.shape), "dp", split_axis=0, concat_axis=0, tiled=True
    )
    grad_pad = jnp.concatenate(
        [grad_back.reshape(-1, model_width), jnp.zeros((1, model_width), jnp.bfloat16)], axis=0
    )
    grad_taken = (
        jnp.take(grad_pad, slot_index, axis=0)
        .reshape(2, tok_count, model_width)
        .astype(jnp.float32)
    )
    grad_normed_two = grad_taken[0] + grad_taken[1]
    grad_up, grad_up_bias, grad_down, grad_down_bias = (
        lax.psum_scatter(
            totals[0][None].astype(jnp.bfloat16), "fsdp", scatter_dimension=1, tiled=True
        ).astype(jnp.float32),
        lax.psum_scatter(
            totals[1][None].astype(jnp.bfloat16), "fsdp", scatter_dimension=1, tiled=True
        ).astype(jnp.float32),
        lax.psum_scatter(
            totals[2][None].astype(jnp.bfloat16), "fsdp", scatter_dimension=1, tiled=True
        ).astype(jnp.float32),
        lax.psum_scatter(
            totals[3][None].astype(jnp.bfloat16), "fsdp", scatter_dimension=1, tiled=True
        ).astype(jnp.float32),
    )
    grad_hidden_part, grad_gain_two, grad_bias_two = norm_two_back(grad_normed_two)
    grad_hidden = grad_mixed + grad_hidden_part
    grad_branch = grad_hidden.astype(jnp.bfloat16)
    grad_proj = jnp.dot(attended_flat.T, grad_branch, preferred_element_type=jnp.float32)
    grad_attended = jnp.dot(grad_branch, proj_full.T, preferred_element_type=jnp.float32).astype(
        jnp.bfloat16
    )
    grad_attended = grad_attended.reshape(row_count, piece_len, HEADS, HD)
    part_query, part_key, part_value = attend_backward(
        queries, keys_all, values_all, allowed, logsum, grad_attended
    )
    summed_key, summed_value = (
        lax.psum_scatter(
            part_key.astype(jnp.bfloat16), "fsdp", scatter_dimension=1, tiled=True
        ).astype(jnp.float32),
        lax.psum_scatter(
            part_value.astype(jnp.bfloat16), "fsdp", scatter_dimension=1, tiled=True
        ).astype(jnp.float32),
    )
    grad_query = part_query.astype(jnp.bfloat16)
    grad_key = summed_key.astype(jnp.bfloat16)
    grad_value = summed_value.astype(jnp.bfloat16)
    grad_projected = jnp.stack([grad_query, grad_key, grad_value], axis=2).reshape(
        tok_count, 3 * model_width
    )
    grad_qkv_weight = jnp.dot(normed_low.T, grad_projected, preferred_element_type=jnp.float32)
    grad_normed = jnp.dot(grad_projected, qkv_full.T, preferred_element_type=jnp.float32)
    grad_inputs, grad_gain_one, grad_bias_one = norm_back(grad_normed)
    grad_tokens = (grad_hidden + grad_inputs).reshape(tokens.shape)
    grad_gate_task = jnp.dot(task_hot.T, grad_gate_copy.T, precision=exact)
    grad_embed, grad_router = gate_back(grad_gate_task)
    reduced = (
        lax.psum_scatter(grad_gain_one, ("dp", "fsdp"), scatter_dimension=0, tiled=True),
        lax.psum_scatter(grad_bias_one, ("dp", "fsdp"), scatter_dimension=0, tiled=True),
        lax.psum_scatter(grad_qkv_weight, ("dp", "fsdp"), scatter_dimension=0, tiled=True),
        lax.psum_scatter(grad_proj, ("dp", "fsdp"), scatter_dimension=0, tiled=True),
        lax.psum_scatter(grad_gain_two, ("dp", "fsdp"), scatter_dimension=0, tiled=True),
        lax.psum_scatter(grad_bias_two, ("dp", "fsdp"), scatter_dimension=0, tiled=True),
        lax.psum_scatter(grad_embed, ("dp", "fsdp"), scatter_dimension=1, tiled=True),
        lax.psum_scatter(grad_router, ("dp", "fsdp"), scatter_dimension=0, tiled=True),
    )
    return (
        output,
        grad_tokens,
        reduced[0],
        reduced[1],
        reduced[2],
        reduced[3],
        reduced[4],
        reduced[5],
        reduced[6],
        reduced[7],
        grad_up,
        grad_up_bias,
        grad_down,
        grad_down_bias,
    )


MESH_ID = pl.DeviceIdType.MESH
VMEM_MAX = 60 * 1024 * 1024
TILE = 16
BLOCK = 512
FCHUNK = 512
QCHUNK = 256
FAR = -float(2**30)
F32 = jnp.float32
BF16 = jnp.bfloat16


def dot_nn(lhs, rhs):
    return lax.dot_general(lhs, rhs, (((1,), (0,)), ((), ())), preferred_element_type=F32)


def dot_nt(lhs, rhs):
    return lax.dot_general(lhs, rhs, (((1,), (1,)), ((), ())), preferred_element_type=F32)


def dot_tn(lhs, rhs):
    return lax.dot_general(lhs, rhs, (((0,), (0,)), ((), ())), preferred_element_type=F32)


def vmem_spec():
    return pl.BlockSpec(memory_space=pltpu.VMEM)


def any_spec():
    return pl.BlockSpec(memory_space=pl.ANY)


def smem_spec():
    return pl.BlockSpec(memory_space=pltpu.SMEM)


def norm_parts(values):
    centre = values - jnp.mean(values, axis=-1, keepdims=True)
    spread = jnp.mean(centre * centre, axis=-1, keepdims=True)
    scale = lax.rsqrt(spread + 1e-05)
    return centre * scale, scale


def norm_back_parts(grad, normal, scale):
    mean_grad = jnp.mean(grad, axis=-1, keepdims=True)
    mean_prod = jnp.mean(grad * normal, axis=-1, keepdims=True)
    return (grad - mean_grad - normal * mean_prod) * scale


def fold_rows(values):
    rows, width = values.shape
    return jnp.sum(values.reshape(rows // 8, 8, width), axis=0)


def plane_ids():
    me = lax.axis_index("dp")
    core, xpos, ypos = lax.rem(me, 2), lax.rem(me // 2, 2), me // 4

    def at(ypos, xpos, core):
        return (ypos * 2 + xpos) * 2 + core

    return me, core, xpos, ypos, at


def greet(peers):
    barrier = pltpu.get_barrier_semaphore()
    for peer in peers:
        pl.semaphore_signal(barrier, inc=1, device_id=peer, device_id_type=MESH_ID)
    pl.semaphore_wait(barrier, len(peers))


class Sender:
    def __init__(self, send_sems, recv_sems):
        self.send_sems, self.recv_sems, self.count, self.all = send_sems, recv_sems, 0, []

    def start(self, src, dst, peer):
        copy = pltpu.make_async_remote_copy(
            src_ref=src,
            dst_ref=dst,
            send_sem=self.send_sems.at[self.count],
            recv_sem=self.recv_sems.at[self.count],
            device_id=peer,
            device_id_type=MESH_ID,
        )
        copy.start()
        self.count += 1
        self.all.append(copy)
        return copy

    def drain(self):
        for copy in self.all:
            copy.wait_send()


def plane_gather_steps(block, own, rows, sender, z):
    me, core, xpos, ypos, at = plane_ids()
    sib, xn, yn = at(ypos, xpos, 1 - core), at(ypos, 1 - xpos, core), at(1 - ypos, xpos, core)
    diag = at(1 - ypos, 1 - xpos, core)
    half = rows // 2

    def part(i, k):
        return block(i).at[pl.ds(k * half, half)]

    def send(i, k, peer):
        src = own.at[pl.ds(k * half, half)] if i is me else part(i, k)
        return sender.start(src, part(i, k), (peer, z))

    x_own = [send(me, 0, xn)]
    y_own = [send(me, 1, yn)]
    x_own.append(send(me, 1, xn))
    y_own.insert(0, send(me, 0, yn))
    last = [send(me, 0, sib), send(me, 1, sib)]
    x_own[0].wait_recv()
    to_y = send(xn, 0, yn)
    y_own[1].wait_recv()
    to_x = send(yn, 1, xn)
    last.append(send(xn, 0, sib))
    last.append(send(yn, 1, sib))
    x_own[1].wait_recv()
    last.append(send(xn, 1, sib))
    y_own[0].wait_recv()
    last.append(send(yn, 0, sib))
    to_y.wait_recv()
    last.append(send(diag, 0, sib))
    to_x.wait_recv()
    last.append(send(diag, 1, sib))
    for copy in last:
        copy.wait_recv()


PLANE_GATHER_COPIES = 14


def plane_peers(z):
    me, core, xpos, ypos, at = plane_ids()
    return [
        (at(ypos, xpos, 1 - core), z),
        (at(ypos, 1 - xpos, core), z),
        (at(1 - ypos, xpos, core), z),
    ]


def column_peers(planes):
    me, z = lax.axis_index("dp"), lax.axis_index("fsdp")
    peers = [(me, lax.rem(z + k, planes)) for k in range(1, planes)]
    return peers + [(me ^ 1, lax.rem(z + k, planes)) for k in range(1, planes)]


class PlaneGather:
    COPIES = 28

    def __init__(self, block, own, send_sems, recv_sems):
        me, core, xpos, ypos, at = plane_ids()
        self.z = lax.axis_index("fsdp")
        self.me = me
        self.sib = at(ypos, xpos, 1 - core)
        self.xn, self.yn = at(ypos, 1 - xpos, core), at(1 - ypos, xpos, core)
        self.diag = at(1 - ypos, 1 - xpos, core)
        self.block, self.own = block, own
        self.send_sems, self.recv_sems = send_sems, recv_sems
        self.all = {}

    def send(self, kind, c, src, owner, peer):
        copy = pltpu.make_async_remote_copy(
            src_ref=src,
            dst_ref=self.block(owner).at[c],
            send_sem=self.send_sems.at[kind * 4 + c],
            recv_sem=self.recv_sems.at[kind * 4 + c],
            device_id=(peer, self.z),
            device_id_type=MESH_ID,
        )
        copy.start()
        self.all[kind, c] = copy

    def start(self, c):
        src = self.own.at[c]
        self.send(0, c, src, self.me, self.xn)
        self.send(1, c, src, self.me, self.yn)
        self.send(2, c, src, self.me, self.sib)

    def pass_on(self, c):
        x_part, y_part = self.block(self.xn).at[c], self.block(self.yn).at[c]
        self.all[0, c].wait_recv()
        if c < 2:
            self.send(3, c, x_part, self.xn, self.yn)
        self.send(4, c, x_part, self.xn, self.sib)
        self.all[1, c].wait_recv()
        if c >= 2:
            self.send(3, c, y_part, self.yn, self.xn)
        self.send(5, c, y_part, self.yn, self.sib)

    def pass_diag(self, c):
        self.all[3, c].wait_recv()
        self.send(6, c, self.block(self.diag).at[c], self.diag, self.sib)

    def finish(self):
        for kind in (2, 4, 5, 6):
            for c in range(4):
                self.all[kind, c].wait_recv()
        for copy in self.all.values():
            copy.wait_send()


def small_gather_kernel(planes, groups, in_ref, out_ref, send_sems, recv_sems):
    me, z = lax.axis_index("dp"), lax.axis_index("fsdp")
    z_peers = [(me, lax.rem(z + k, planes)) for k in range(1, planes)]
    d_peers = [(lax.rem(me + k, groups), z) for k in range(1, groups)]
    greet(z_peers + d_peers)
    sender = Sender(send_sems, recv_sems)
    out_ref[me, z] = in_ref[...]
    first = [sender.start(in_ref, out_ref.at[me, z], peer) for peer in z_peers]
    for copy in first:
        copy.wait_recv()
    second = [sender.start(out_ref.at[me], out_ref.at[me], peer) for peer in d_peers]
    for copy in second:
        copy.wait_recv()
    sender.drain()


def small_gather(payload, planes, groups):
    return pl.pallas_call(
        functools.partial(small_gather_kernel, planes, groups),
        out_shape=jax.ShapeDtypeStruct((groups, planes) + payload.shape, payload.dtype),
        in_specs=[vmem_spec()],
        out_specs=vmem_spec(),
        scratch_shapes=[
            pltpu.SemaphoreType.DMA((planes + groups,)),
            pltpu.SemaphoreType.DMA((planes + groups,)),
        ],
        compiler_params=pltpu.CompilerParams(collective_id=1, has_side_effects=True),
        name="routing_gather",
    )(payload)


def plane_scatter_steps(z_ref, own, theirs, deep, near_x, near_y, sender, loc_sems, z):
    me, core, xpos, ypos, at = plane_ids()
    sib, xn, yn = at(ypos, xpos, 1 - core), at(ypos, 1 - xpos, core), at(1 - ypos, xpos, core)
    chips = [(ypos, xpos), (ypos, 1 - xpos), (1 - ypos, xpos), (1 - ypos, 1 - xpos)]
    rows = z_ref.shape[1]
    half = rows // 2
    first, second = pl.ds(0, half), pl.ds(half, half)
    loads, trades = {}, {}
    for slot in (3, 1, 2, 0):
        pos = chips[slot]
        loads[slot] = pltpu.make_async_copy(
            z_ref.at[at(pos[0], pos[1], core)], own.at[slot], loc_sems.at[slot]
        )
        loads[slot].start()
        trades[slot] = sender.start(
            z_ref.at[at(pos[0], pos[1], 1 - core)], theirs.at[slot], (sib, z)
        )

    yield

    def add(slot, part):
        own[slot, part] = (
            own[slot, part].astype(F32) + theirs[slot, part].astype(F32)
        ).astype(own.dtype)

    loads[3].wait()
    trades[3].wait_recv()
    add(3, first)
    deep_x = sender.start(own.at[3, first], deep.at[0], (xn, z))
    add(3, second)
    deep_y = sender.start(own.at[3, second], deep.at[1], (yn, z))
    loads[1].wait()
    trades[1].wait_recv()
    add(1, first)
    x_first = sender.start(own.at[1, first], near_x.at[first], (xn, z))
    loads[2].wait()
    trades[2].wait_recv()
    add(2, second)
    y_second = sender.start(own.at[2, second], near_y.at[second], (yn, z))
    add(1, second)
    add(2, first)
    yield
    deep_y.wait_recv()
    own[1, second] = (own[1, second].astype(F32) + deep[1].astype(F32)).astype(own.dtype)
    x_second = sender.start(own.at[1, second], near_x.at[second], (xn, z))
    deep_x.wait_recv()
    own[2, first] = (own[2, first].astype(F32) + deep[0].astype(F32)).astype(own.dtype)
    y_first = sender.start(own.at[2, first], near_y.at[first], (yn, z))
    yield
    loads[0].wait()
    trades[0].wait_recv()
    yield
    mine = own[0].astype(F32) + theirs[0].astype(F32)
    x_first.wait_recv()
    y_second.wait_recv()
    x_second.wait_recv()
    y_first.wait_recv()
    yield mine + near_x[...].astype(F32) + near_y[...].astype(F32)


PLANE_SCATTER_COPIES = 10


def pick_rows_kernel(order_ref, *refs):
    count = len(refs) // 2
    for a in range(count):
        refs[count + a][...] = refs[a][...].astype(refs[count + a].dtype)


def pick_rows(order, arrays, kinds):
    def block(array):
        return (1,) + array.shape[1:]

    return pl.pallas_call(
        pick_rows_kernel,
        out_shape=tuple(
            jax.ShapeDtypeStruct(array.shape, kind) for array, kind in zip(arrays, kinds)
        ),
        grid_spec=pltpu.PrefetchScalarGridSpec(
            num_scalar_prefetch=1,
            grid=(arrays[0].shape[0],),
            in_specs=[
                pl.BlockSpec(block(array), lambda r, order_ref: (order_ref[r], 0, 0))
                for array in arrays
            ],
            out_specs=tuple(
                pl.BlockSpec(block(array), lambda r, order_ref: (r, 0, 0)) for array in arrays
            ),
        ),
        name="row_order",
    )(order, *arrays)


def unit_copy(src, dst, send_sem, recv_sem, peer):
    return pltpu.make_async_remote_copy(
        src_ref=src,
        dst_ref=dst,
        send_sem=send_sem,
        recv_sem=recv_sem,
        device_id=peer,
        device_id_type=MESH_ID,
    )


class WeightSpread:
    def __init__(self, up_ref, down_ref, up_all, down_all, sems):
        self.me, self.z = lax.axis_index("dp"), lax.axis_index("fsdp")
        self.core = lax.rem(self.me, 2)
        self.src = (up_ref, down_ref)
        self.dst = (up_all, down_all)
        self.own_send, self.pass_send, self.recv, self.local = sems
        self.side = self.z // 2
        self.near = self.z ^ 1
        self.far = 2 - self.side
        self.inner = (self.z == 1) | (self.z == 2)

    def targets(self):
        chip = self.me - self.core
        return [
            (self.core, self.near),
            (self.core, self.far),
            (1 - self.core, self.near),
            (1 - self.core, self.far),
            (1 - self.core, self.z),
        ], chip

    def copy(self, kind, src, m, p, send_sem, peer):
        return unit_copy(
            src,
            self.dst[kind].at[m, p],
            send_sem,
            self.recv.at[kind * 8 + m * 4 + p],
            peer,
        )

    def own(self):
        targets, chip = self.targets()
        out = []
        for kind in range(2):
            for k, (h, p) in enumerate(targets):
                out.append(
                    self.copy(
                        kind,
                        self.src[kind].at[h],
                        self.core,
                        self.z,
                        self.own_send.at[kind * 5 + k],
                        (chip + h, p),
                    )
                )
        return out

    def mine(self):
        return [
            pltpu.make_async_copy(
                self.src[kind].at[self.core],
                self.dst[kind].at[self.core, self.z],
                self.local.at[kind],
            )
            for kind in range(2)
        ]

    def passed(self, j):
        p = 2 * (1 - self.side) + j
        return [
            self.copy(
                kind,
                self.dst[kind].at[m, p],
                m,
                p,
                self.pass_send.at[kind * 4 + m * 2 + j],
                (self.me, self.near),
            )
            for kind in range(2)
            for m in range(2)
        ]

    def start(self):
        for copy in self.mine() + self.own():
            copy.start()

    def pass_on(self, first):
        for side in range(2):

            @pl.when((self.z == 1 + side))
            def _():
                j = side if first else 1 - side
                for copy in self.passed(j):
                    copy.wait_recv()
                    copy.start()

    def finish(self):
        for copy in self.mine():
            copy.wait()
        for copy in self.own():
            copy.wait_send()

        def arrived(kind, m, p):
            self.copy(
                kind, self.dst[kind].at[m, p], m, p, self.own_send.at[0], (self.me, self.near)
            ).wait_recv()

        for kind in range(2):
            arrived(kind, 1 - self.core, self.z)
            for m in range(2):
                arrived(kind, m, self.near)

        @pl.when(self.inner)
        def _():
            for j in range(2):
                for copy in self.passed(j):
                    copy.wait_send()

        @pl.when(jnp.logical_not(self.inner))
        def _():
            for kind in range(2):
                for m in range(2):
                    for j in range(2):
                        arrived(kind, m, 2 * (1 - self.side) + j)


def forward_kernel(
    heads,
    planes,
    tok_ref,
    gm_ref,
    w_ref,
    upw_ref,
    downw_ref,
    norm_ref,
    qf_ref,
    kf_ref,
    row_ref,
    dense_ref,
    qkv_ref,
    o_ref,
    lse_ref,
    hres_ref,
    xn2_ref,
    x_all,
    g_all,
    up_all,
    down_all,
    kaug,
    vaug,
    z_send,
    z_recv,
    w_send,
    w_recv,
    x_send,
    x_recv,
    g_send,
    g_recv,
    u_own,
    u_pass,
    u_recv,
    loc_sems,
):
    me, z = lax.axis_index("dp"), lax.axis_index("fsdp")
    z_peers = [(me, lax.rem(z + k, planes)) for k in range(1, planes)]
    greet(column_peers(planes) + plane_peers(z))
    rows, width = qkv_ref.shape[0], row_ref.shape[2]
    chunk = row_ref.shape[1]
    head = width // heads
    pair = 2 * head
    shard = w_ref.shape[0]
    sender = Sender(z_send, z_recv)
    dense_own = pltpu.make_async_copy(
        w_ref, dense_ref.at[me, pl.ds(z * shard, shard)], loc_sems.at[0]
    )
    dense_own.start()
    tok_own = pltpu.make_async_copy(tok_ref.at[z], row_ref.at[z], loc_sems.at[1])
    tok_own.start()
    gm_own = pltpu.make_async_copy(gm_ref.at[z], g_all.at[me, z], loc_sems.at[2])
    gm_own.start()
    dense_z = [
        sender.start(w_ref, dense_ref.at[me, pl.ds(z * shard, shard)], peer) for peer in z_peers
    ]
    toks = [sender.start(tok_ref.at[peer[1]], row_ref.at[z], peer) for peer in z_peers]
    dense_own.wait()
    for copy in dense_z:
        copy.wait_recv()
    dense_sender = Sender(w_send, w_recv)
    plane_gather_steps(
        lambda i: dense_ref.at[i], dense_ref.at[me], planes * shard, dense_sender, z
    )
    for copy in toks:
        copy.wait_recv()
    tok_own.wait()
    gms = [sender.start(gm_ref.at[peer[1]], g_all.at[me, z], peer) for peer in z_peers]
    spread = WeightSpread(upw_ref, downw_ref, up_all, down_all, (u_own, u_pass, u_recv, loc_sems.at[pl.ds(3, 2)]))
    x_gather = PlaneGather(lambda i: x_all.at[i], xn2_ref, x_send, x_recv)
    g_gather = PlaneGather(lambda i: g_all.at[i], g_all.at[me], g_send, g_recv)

    lane = lax.broadcasted_iota(jnp.int32, (rows, pair), 1)
    lane_c = lax.broadcasted_iota(jnp.int32, (chunk, pair), 1)
    w_qkv = dense_ref[:, :, : 3 * width].reshape(width, 3 * width)

    def project(c, carry):
        part = pl.ds(pl.multiple_of(c * chunk, chunk), chunk)
        normal, _ = norm_parts(row_ref[c].astype(F32))
        xn1 = (normal * norm_ref[0:1, :] + norm_ref[1:2, :]).astype(BF16)
        out = dot_nn(xn1, dense_ref[:, :, : 3 * width].reshape(width, 3 * width))
        qkv_ref[part, :width] = (out[:, :width] * 0.125).astype(BF16)
        qkv_ref[part, width:] = out[:, width:].astype(BF16)
        return carry

    lax.fori_loop(0, planes, project, 0)

    def prepare(g, carry):
        k_pair = qkv_ref[:, pl.ds(pl.multiple_of(width + g * pair, pair), pair)]
        v_pair = qkv_ref[:, pl.ds(pl.multiple_of(2 * width + g * pair, pair), pair)]
        zero = jnp.zeros_like(k_pair)
        for side in range(2):
            mine = (lane // head) == side
            kaug[g, side, :, :pair] = jnp.where(mine, k_pair, zero)
            vaug[g, side, :, :pair] = jnp.where(mine, v_pair, zero)
            kaug[g, side, :, pair:] = kf_ref[...]
            vaug[g, side, :, pair:] = jnp.where(mine, 1.0, 0.0).astype(BF16)
        return carry

    lax.fori_loop(0, heads // 2, prepare, 0)

    def attend(c):
        part = pl.ds(c * chunk, chunk)

        def one_pair(g, carry):
            cols = pl.ds(pl.multiple_of(g * pair, pair), pair)
            qa = jnp.concatenate([qkv_ref[part, cols], qf_ref[part, :]], axis=1)
            acc = jnp.zeros((chunk, 2 * pair), F32)
            tops = []
            for side in range(2):
                s = dot_nt(qa, kaug[g, side])
                top = jnp.max(s, axis=-1, keepdims=True)
                acc = acc + dot_nn(jnp.exp(s - top).astype(BF16), vaug[g, side])
                tops.append(top)
            total = acc[:, pair:]
            o_ref[part, cols] = (acc[:, :pair] / total).astype(BF16)
            top = jnp.where(lane_c < head, tops[0], tops[1])
            lse_ref[part, cols] = top + jnp.log(total)
            return carry

        lax.fori_loop(0, heads // 2, one_pair, 0)
        w_proj = dense_ref[:, :, 3 * width :].reshape(width, width)
        hres = row_ref[c].astype(F32) + dot_nn(o_ref[part, :], w_proj)
        hres_ref[part, :] = hres
        normal, _ = norm_parts(hres)
        xn2_ref[c] = (normal * norm_ref[2:3, :] + norm_ref[3:4, :]).astype(BF16)
        x_gather.start(c)

    attend(0)
    attend(1)
    for copy in gms:
        copy.wait_recv()
    gm_own.wait()
    spread.start()
    for c in range(4):
        g_gather.start(c)
    attend(2)
    x_gather.pass_on(0)
    x_gather.pass_on(1)
    attend(3)
    x_gather.pass_on(2)
    for c in range(4):
        g_gather.pass_on(c)
    x_gather.pass_on(3)
    spread.pass_on(True)
    for c in range(4):
        x_gather.pass_diag(c)
        g_gather.pass_diag(c)
    spread.pass_on(False)
    x_gather.finish()
    g_gather.finish()
    spread.finish()
    sender.drain()
    dense_sender.drain()


def forward(tokens, grads, dense, up, down, norms, qf, kf, heads, groups):
    planes, piece, width = tokens.shape
    rows = planes * piece
    pair = 2 * (width // heads)
    sd = jax.ShapeDtypeStruct
    dma = pltpu.SemaphoreType.DMA
    return pl.pallas_call(
        functools.partial(forward_kernel, heads, planes),
        out_shape=(
            sd(tokens.shape, BF16),
            sd((groups, planes * dense.shape[0], dense.shape[1]), BF16),
            sd((rows, 3 * width), BF16),
            sd((rows, width), BF16),
            sd((rows, width), F32),
            sd((rows, width), F32),
            sd(tokens.shape, BF16),
            sd((groups,) + tokens.shape, BF16),
            sd((groups,) + tokens.shape, BF16),
            sd((2, planes) + up.shape[1:], BF16),
            sd((2, planes) + down.shape[1:], BF16),
        ),
        in_specs=[any_spec()] * 5 + [vmem_spec()] * 3,
        out_specs=tuple([vmem_spec()] * 7 + [any_spec()] * 4),
        scratch_shapes=[
            pltpu.VMEM((heads // 2, 2, rows, 2 * pair), BF16),
            pltpu.VMEM((heads // 2, 2, rows, 2 * pair), BF16),
            dma((3 * planes,)),
            dma((3 * planes,)),
            dma((PLANE_GATHER_COPIES,)),
            dma((PLANE_GATHER_COPIES,)),
            dma((PlaneGather.COPIES,)),
            dma((PlaneGather.COPIES,)),
            dma((PlaneGather.COPIES,)),
            dma((PlaneGather.COPIES,)),
            dma((10,)),
            dma((8,)),
            dma((16,)),
            dma((5,)),
        ],
        compiler_params=pltpu.CompilerParams(
            collective_id=2, has_side_effects=True, vmem_limit_bytes=VMEM_MAX
        ),
        cost_estimate=pl.CostEstimate(
            flops=40_000_000_000, bytes_accessed=10_000_000, transcendentals=8_000_000
        ),
        name="attention_forward",
    )(tokens, grads, dense, up, down, norms, qf, kf)


def split3(values):
    high = values.astype(BF16)
    rest = values - high.astype(F32)
    middle = rest.astype(BF16)
    low = (rest - middle.astype(F32)).astype(BF16)
    return high, middle, low


def backward_kernel(
    heads,
    planes,
    groups,
    row_ref,
    norm_ref,
    dense_ref,
    qf_ref,
    kf_ref,
    qkv_ref,
    o_ref,
    lse_ref,
    hres_ref,
    g_all,
    zd_ref,
    zy_ref,
    gu_ref,
    gd_ref,
    small_ref,
    out_ref,
    dtok_ref,
    shard_ref,
    gu_in,
    gd_in,
    small_out,
    gm,
    kaug,
    vaug,
    dh,
    db,
    do,
    delta,
    qt,
    dot_t,
    dkt,
    dvt,
    dqkv,
    xn1,
    dw,
    dnorm,
    moved,
    own,
    d_theirs,
    d_deep,
    d_x,
    d_y,
    y_theirs,
    y_deep,
    y_x,
    y_y,
    w_own,
    w_theirs,
    w_deep,
    w_x,
    w_y,
    w_sum,
    w_in,
    small_in,
    s_send,
    s_recv,
    d_send,
    d_recv,
    y_send,
    y_recv,
    w_send,
    w_recv,
    z_send,
    z_recv,
    u_send,
    u_recv,
    loc_sems,
):
    me, z = lax.axis_index("dp"), lax.axis_index("fsdp")
    core = lax.rem(me, 2)
    chip = me - core
    z_peers = [(me, lax.rem(z + k, planes)) for k in range(1, planes)]
    d_peers = [(lax.rem(me + k, groups), z) for k in range(1, groups)]
    greet(column_peers(planes) + d_peers)
    rows, width = hres_ref.shape
    chunk = row_ref.shape[1]
    head = width // heads
    pair = 2 * head

    gm_load = pltpu.make_async_copy(g_all.at[me], gm, loc_sems.at[4])
    gm_load.start()
    small_sender = Sender(s_send, s_recv)
    small_z = [small_sender.start(small_ref, small_in.at[k], p) for k, p in enumerate(z_peers)]
    d_sender = Sender(d_send, d_recv)
    d_scatter = plane_scatter_steps(
        zd_ref, own, d_theirs, d_deep, d_x, d_y, d_sender, loc_sems, z
    )
    next(d_scatter)
    unit_copies = []
    for kind, (src, dst) in enumerate(((gu_ref, gu_in), (gd_ref, gd_in))):
        for t in range(2):
            for k in range(planes):
                h, p = (core + t) % 2, lax.rem(z + k, planes)
                if t == 0 and k == 0:
                    copy = pltpu.make_async_copy(
                        src.at[z, core], dst.at[core, z], loc_sems.at[5 + kind]
                    )
                    copy.start()
                else:
                    i = kind * 8 + t * 4 + k
                    copy = unit_copy(
                        src.at[p, h], dst.at[core, z], u_send.at[i], u_recv.at[i], (chip + h, p)
                    )
                    copy.start()
                unit_copies.append(copy)
    for copy in small_z:
        copy.wait_recv()
    small_out[me] = small_ref[...] + jnp.sum(small_in[...], axis=0)
    small_d = [small_sender.start(small_out.at[me], small_out.at[me], p) for p in d_peers]
    gm_load.wait()

    for _ in range(3):
        next(d_scatter)
    dh[...] = next(d_scatter)
    y_sender = Sender(y_send, y_recv)
    y_scatter = plane_scatter_steps(
        zy_ref, own, y_theirs, y_deep, y_x, y_y, y_sender, loc_sems, z
    )
    d_sender.drain()
    next(y_scatter)

    lane = lax.broadcasted_iota(jnp.int32, (rows, pair), 1)
    lane_c = lax.broadcasted_iota(jnp.int32, (chunk, pair), 1)
    same = (
        lax.broadcasted_iota(jnp.int32, (pair, pair), 0) // head
        == lax.broadcasted_iota(jnp.int32, (pair, pair), 1) // head
    )
    ones = jnp.where(same, 1.0, 0.0).astype(BF16)
    dnorm[...] = jnp.zeros_like(dnorm)

    def begin(c, carry):
        part = pl.ds(pl.multiple_of(c * chunk, chunk), chunk)
        normal, scale = norm_parts(hres_ref[part, :])
        grad = dh[part, :]
        dnorm[2] += fold_rows(grad * normal)
        dnorm[3] += fold_rows(grad)
        dh_part = gm[c].astype(F32) + norm_back_parts(grad * norm_ref[2:3, :], normal, scale)
        dh[part, :] = dh_part
        low = dh_part.astype(BF16)
        db[part, :] = low
        do_part = dot_nt(low, dense_ref[:, :, 3 * width :].reshape(width, width)).astype(BF16)
        do[part, :] = do_part
        prod = do_part.astype(F32) * o_ref[part, :].astype(F32)
        high = prod.astype(BF16)
        rest = (prod - high.astype(F32)).astype(BF16)
        for g in range(heads // 2):
            cols = slice(g * pair, (g + 1) * pair)
            delta[part, cols] = dot_nn(high[:, cols], ones) + dot_nn(rest[:, cols], ones)
        normal, _ = norm_parts(row_ref[c].astype(F32))
        xn1[part, :] = (normal * norm_ref[0:1, :] + norm_ref[1:2, :]).astype(BF16)
        return carry

    lax.fori_loop(0, planes, begin, 0)
    next(y_scatter)
    w_rows = w_sum.shape[0]
    w_cols = w_sum.shape[1]
    dw[:, :, 3 * width : 4 * width] = (
        dot_tn(o_ref[...], db[...]).astype(BF16).reshape(groups, w_rows, width)
    )

    mark = (lane >= heads) & (lane < heads + 3)
    for side in range(2):
        kaug[side, :, pair:] = jnp.where(mark, 1.0, kf_ref[...].astype(F32)).astype(BF16)
        vaug[side, :, pair:] = jnp.where(mark, 1.0, 0.0).astype(BF16)

    def put_parts(base, values):
        high, middle, low = split3(-values)
        out = jnp.where(lane_c == heads, high.astype(F32), base)
        out = jnp.where(lane_c == heads + 1, middle.astype(F32), out)
        return jnp.where(lane_c == heads + 2, low.astype(F32), out).astype(BF16)

    def one_pair(g):
        cols = slice(g * pair, (g + 1) * pair)
        k_pair = qkv_ref[:, width + g * pair : width + (g + 1) * pair]
        v_pair = qkv_ref[:, 2 * width + g * pair : 2 * width + (g + 1) * pair]
        zero = jnp.zeros_like(k_pair)
        for side in range(2):
            mine = (lane // head) == side
            kaug[side, :, :pair] = jnp.where(mine, k_pair, zero)
            vaug[side, :, :pair] = jnp.where(mine, v_pair, zero)
        qt[...] = qkv_ref[:, cols].T
        dot_t[...] = do[:, cols].T
        dkt[...] = jnp.zeros_like(dkt)
        dvt[...] = jnp.zeros_like(dvt)

        def one_chunk(c, inner):
            part = pl.ds(pl.multiple_of(c * chunk, chunk), chunk)
            q_pair, do_pair = qkv_ref[part, cols], do[part, cols]
            lse_pair, delta_pair = lse_ref[part, cols], delta[part, cols]
            base = qf_ref[part, :].astype(F32)
            acc = jnp.zeros((chunk, pair), F32)
            for side in range(2):
                lse = lse_pair[:, side * head : side * head + 1]
                qa = jnp.concatenate([q_pair, put_parts(base, lse)], axis=1)
                pr = jnp.exp(dot_nt(qa, kaug[side]))
                dlt = delta_pair[:, side * head : side * head + 1]
                da = jnp.concatenate([do_pair, put_parts(jnp.zeros_like(base), dlt)], axis=1)
                ds = (pr * dot_nt(da, vaug[side])).astype(BF16)
                acc = acc + dot_nn(ds, kaug[side, :, :pair])
                here = slice(side * head, (side + 1) * head)
                dkt[here, :] += dot_nn(qt[here, part], ds)
                dvt[here, :] += dot_nn(dot_t[here, part], pr.astype(BF16))
            dqkv[part, cols] = (acc * 0.125).astype(BF16)
            return inner

        lax.fori_loop(0, planes, one_chunk, 0)
        dqkv[:, width + g * pair : width + (g + 1) * pair] = dkt[...].T.astype(BF16)
        dqkv[:, 2 * width + g * pair : 2 * width + (g + 1) * pair] = dvt[...].T.astype(BF16)

    out_sender = Sender(z_send, z_recv)
    one_pair(0)
    next(y_scatter)
    one_pair(1)
    next(y_scatter)
    one_pair(2)
    mixed = hres_ref[...] + next(y_scatter)
    moved[0] = mixed.astype(BF16).reshape(planes, chunk, width)
    out_keep = pltpu.make_async_copy(moved.at[0, z], out_ref.at[z], loc_sems.at[7])
    out_keep.start()
    sent = [out_sender.start(moved.at[0, p[1]], out_ref.at[z], p) for p in z_peers]
    one_pair(3)

    def finish(c, carry):
        part = pl.ds(pl.multiple_of(c * chunk, chunk), chunk)
        grad = dot_nt(
            dqkv[part, :], dense_ref[:, :, : 3 * width].reshape(width, 3 * width)
        )
        normal, scale = norm_parts(row_ref[c].astype(F32))
        dnorm[0] += fold_rows(grad * normal)
        dnorm[1] += fold_rows(grad)
        moved[1, c] = (
            dh[part, :] + norm_back_parts(grad * norm_ref[0:1, :], normal, scale)
        ).astype(BF16)
        return carry

    lax.fori_loop(0, planes, finish, 0)
    tok_keep = pltpu.make_async_copy(moved.at[1, z], dtok_ref.at[z], loc_sems.at[8])
    tok_keep.start()
    sent += [out_sender.start(moved.at[1, p[1]], dtok_ref.at[z], p) for p in z_peers]
    for c in range(3):
        cols = slice(c * width, (c + 1) * width)
        dw[:, :, cols] = (
            dot_tn(xn1[...], dqkv[:, cols]).astype(BF16).reshape(groups, w_rows, width)
        )
    lanes = lax.broadcasted_iota(jnp.int32, (8, width), 0)
    table = jnp.zeros((8, width), F32)
    for k in range(4):
        table = jnp.where(lanes == k, jnp.sum(dnorm[k], axis=0, keepdims=True), table)
    table = jnp.concatenate([table, jnp.zeros((w_cols - 4 * width - 8, width), F32)], axis=0)
    dw[:, :, 4 * width :] = table.T.astype(BF16).reshape(groups, w_rows, w_cols - 4 * width)
    w_sender = Sender(w_send, w_recv)
    w_scatter = plane_scatter_steps(
        dw, w_own, w_theirs, w_deep, w_x, w_y, w_sender, loc_sems, z
    )
    for _ in range(4):
        next(w_scatter)
    w_sum[...] = next(w_scatter).astype(BF16)
    shard = shard_ref.shape[0]
    last = [
        out_sender.start(w_sum.at[pl.ds(p[1] * shard, shard)], w_in.at[k], p)
        for k, p in enumerate(z_peers)
    ]
    total = w_sum[pl.ds(z * shard, shard)].astype(F32)
    for k, copy in enumerate(last):
        copy.wait_recv()
        total = total + w_in[k].astype(F32)
    shard_ref[...] = total
    for copy in sent + small_d:
        copy.wait_recv()
    for i, copy in enumerate(unit_copies):
        if i % 8 == 0:
            copy.wait()
        else:
            copy.wait_recv()
            copy.wait_send()
    out_keep.wait()
    tok_keep.wait()
    for sender in (small_sender, y_sender, w_sender, out_sender):
        sender.drain()


def scatter_scratch(rows, width):
    return [
        pltpu.VMEM((4, rows, width), BF16),
        pltpu.VMEM((2, rows // 2, width), BF16),
        pltpu.VMEM((rows, width), BF16),
        pltpu.VMEM((rows, width), BF16),
    ]


def backward(row, norms, dense, qf, kf, qkv, o, lse, hres, g_all, zd, zy, gu, gd, small, heads):
    planes, piece, width = row.shape
    groups = zd.shape[0]
    rows = planes * piece
    pair = 2 * (width // heads)
    w_rows, w_cols = width // groups, 4 * width + 128
    sd = jax.ShapeDtypeStruct
    dma = pltpu.SemaphoreType.DMA
    return pl.pallas_call(
        functools.partial(backward_kernel, heads, planes, groups),
        out_shape=(
            sd(row.shape, BF16),
            sd(row.shape, BF16),
            sd((w_rows // planes, w_cols), F32),
            sd((2, planes) + gu.shape[2:], BF16),
            sd((2, planes) + gd.shape[2:], BF16),
            sd((groups,) + small.shape, F32),
        ),
        in_specs=[vmem_spec()] * 9 + [any_spec()] * 5 + [vmem_spec()],
        out_specs=(any_spec(), any_spec(), vmem_spec(), any_spec(), any_spec(), vmem_spec()),
        scratch_shapes=[
            pltpu.VMEM(row.shape, BF16),
            pltpu.VMEM((2, rows, 2 * pair), BF16),
            pltpu.VMEM((2, rows, 2 * pair), BF16),
            pltpu.VMEM((rows, width), F32),
            pltpu.VMEM((rows, width), BF16),
            pltpu.VMEM((rows, width), BF16),
            pltpu.VMEM((rows, width), F32),
            pltpu.VMEM((pair, rows), BF16),
            pltpu.VMEM((pair, rows), BF16),
            pltpu.VMEM((pair, rows), F32),
            pltpu.VMEM((pair, rows), F32),
            pltpu.VMEM((rows, 3 * width), BF16),
            pltpu.VMEM((rows, width), BF16),
            pltpu.VMEM((groups, w_rows, w_cols), BF16),
            pltpu.VMEM((4, 8, width), F32),
            pltpu.VMEM((2,) + row.shape, BF16),
            pltpu.VMEM((4, rows, width), BF16),
        ]
        + scatter_scratch(rows, width)
        + scatter_scratch(rows, width)
        + [pltpu.VMEM((4, w_rows, w_cols), BF16)]
        + scatter_scratch(w_rows, w_cols)
        + [
            pltpu.VMEM((w_rows, w_cols), BF16),
            pltpu.VMEM((planes - 1, w_rows // planes, w_cols), BF16),
            pltpu.VMEM((planes - 1,) + small.shape, F32),
            dma((planes + groups,)),
            dma((planes + groups,)),
            dma((PLANE_SCATTER_COPIES,)),
            dma((PLANE_SCATTER_COPIES,)),
            dma((PLANE_SCATTER_COPIES,)),
            dma((PLANE_SCATTER_COPIES,)),
            dma((PLANE_SCATTER_COPIES,)),
            dma((PLANE_SCATTER_COPIES,)),
            dma((3 * planes,)),
            dma((3 * planes,)),
            dma((16,)),
            dma((16,)),
            dma((9,)),
        ],
        compiler_params=pltpu.CompilerParams(
            collective_id=4, has_side_effects=True, vmem_limit_bytes=VMEM_MAX
        ),
        cost_estimate=pl.CostEstimate(
            flops=80_000_000_000, bytes_accessed=20_000_000, transcendentals=8_000_000
        ),
        name="attention_backward",
    )(row, norms, dense, qf, kf, qkv, o, lse, hres, g_all, zd, zy, gu, gd, small)


def expert_kernel(
    list_ref,
    meta_ref,
    own_ref,
    x_ref,
    g_ref,
    up_ref,
    down_ref,
    bup_ref,
    bdown_ref,
    zd_ref,
    zy_ref,
    gu_ref,
    gd_ref,
    dbup_ref,
    dbdown_ref,
    dgate_ref,
    xs,
    gs,
    zds,
    zys,
    up,
    down,
    acc_up,
    acc_down,
    xb,
    gb,
    mb,
    dyb,
    xt,
    dyt,
    yacc,
    xacc,
    sems,
):
    me = lax.axis_index("dp")
    groups, rows, width = x_ref.shape
    hidden = up.shape[2]
    planes = gu_ref.shape[0]
    tiles = BLOCK // TILE
    copies = []

    def load(src, dst):
        copy = pltpu.make_async_copy(src, dst, sems.at[len(copies)])
        copy.start()
        copies.append(copy)

    load(up_ref, up)
    load(down_ref, down)
    load(g_ref, gs)
    load(own_ref, xs.at[me])
    for k in range(1, groups):
        load(x_ref.at[me ^ k], xs.at[me ^ k])

    def wipe(k, carry):
        part = pl.ds(pl.multiple_of(k * BLOCK, BLOCK), BLOCK)
        zds[part, :] = jnp.zeros((BLOCK, width), BF16)
        zys[part, :] = jnp.zeros((BLOCK, width), BF16)
        return carry

    lax.fori_loop(0, groups * rows // BLOCK, wipe, 0)
    dbup_ref[...] = jnp.zeros_like(dbup_ref)
    dbdown_ref[...] = jnp.zeros_like(dbdown_ref)
    dgate_ref[...] = jnp.zeros_like(dgate_ref)
    for copy in copies:
        copy.wait()

    def spot(index):
        return pl.ds(pl.multiple_of(index * TILE, TILE), TILE)

    saves = []

    def save(src, dst):
        copy = pltpu.make_async_copy(src, dst, sems.at[len(copies) + len(saves)])
        copy.start()
        saves.append(copy)

    per_row = rows // TILE

    def one_expert(e):
        acc_up[...] = jnp.zeros_like(acc_up)
        acc_down[...] = jnp.zeros_like(acc_down)
        n_blocks = lax.div(list_ref[e, 0] + (tiles - 1), tiles)

        def one_block(b, carry):
            def fetch(k, inner):
                index = list_ref[e, 1 + b * tiles + k]
                src, part = lax.div(index, per_row), spot(lax.rem(index, per_row))
                dst = spot(k)
                xb[dst, :] = xs[src, part, :]
                gb[dst, :] = gs[src, part, :]
                mb[dst, :] = meta_ref[spot(index), :]
                return inner

            lax.fori_loop(0, tiles, fetch, 0, unroll=4)
            gate = mb[:, 2 * e : 2 * e + 1]
            dyb_new = (gb[...].astype(F32) * gate).astype(BF16)
            dyb[...] = dyb_new
            xt[...] = xb[...].T
            dyt[...] = dyb_new.T
            dbdown_ref[e] += fold_rows(dyb_new.astype(F32))

            def one_chunk(f, inner):
                cols = pl.ds(pl.multiple_of(f * FCHUNK, FCHUNK), FCHUNK)
                u = dot_nn(xb[...], up[e, :, cols]) + bup_ref[e, :, cols]
                sq = u * u
                th = jnp.tanh(u * (0.7978845608028654 + 0.035677408136300125 * sq))
                half = 0.5 + 0.5 * th
                slope = half + u * (
                    (0.5 - 0.5 * th * th) * (0.7978845608028654 + 0.10703222440890037 * sq)
                )
                a = (u * half).astype(BF16)
                du = (dot_nt(dyb[...], down[e, cols, :]) * slope).astype(BF16)
                y_new = dot_nn(a, down[e, cols, :])
                x_new = dot_nt(du, up[e, :, cols])

                @pl.when(f == 0)
                def _():
                    yacc[...] = y_new
                    xacc[...] = x_new

                @pl.when(f > 0)
                def _():
                    yacc[...] += y_new
                    xacc[...] += x_new

                acc_up[:, cols] += dot_nn(xt[...], du)
                acc_down[:, cols] += dot_nn(dyt[...], a)
                dbup_ref[e, :, cols] += fold_rows(du.astype(F32))
                return inner

            lax.fori_loop(0, hidden // FCHUNK, one_chunk, 0)
            y = yacc[...] + bdown_ref[e]
            inner_prod = jnp.sum(y * gb[...].astype(F32), axis=-1, keepdims=True)
            lane = lax.broadcasted_iota(jnp.int32, (BLOCK, 128), 1).astype(F32)
            dgate_ref[e] += fold_rows(jnp.where(lane == mb[:, 2 * e + 1 : 2 * e + 2], inner_prod, 0.0))
            gb[...] = (y * gate).astype(BF16)
            xb[...] = xacc[...].astype(BF16)

            def store(k, inner):
                dst = spot(list_ref[e, 1 + b * tiles + k])
                src = spot(k)
                if e == 0:
                    zds[dst, :] = xb[src, :]
                    zys[dst, :] = gb[src, :]
                else:
                    zds[dst, :] = (zds[dst, :].astype(F32) + xb[src, :].astype(F32)).astype(BF16)
                    zys[dst, :] = (zys[dst, :].astype(F32) + gb[src, :].astype(F32)).astype(BF16)
                return inner

            lax.fori_loop(0, tiles, store, 0, unroll=4)
            return carry

        lax.fori_loop(0, n_blocks, one_block, 0)
        up[e] = acc_up[...].astype(BF16)
        for k in range(hidden // FCHUNK):
            cols = slice(k * FCHUNK, (k + 1) * FCHUNK)
            down[e, cols, :] = acc_down[:, cols].T.astype(BF16)
        up_rows, down_rows = width // planes, hidden // planes
        for k in range(planes):
            save(up.at[e, pl.ds(k * up_rows, up_rows)], gu_ref.at[k, e])
            save(down.at[e, pl.ds(k * down_rows, down_rows)], gd_ref.at[k, e])

    one_expert(0)
    one_expert(1)
    save(zds, zd_ref)
    save(zys, zy_ref)
    for copy in saves:
        copy.wait()


def experts(tile_list, meta, x_own, x_all, g_all, up, down, b_up, b_down):
    groups, rows, width = x_all.shape
    hidden = up.shape[2]
    planes = 4
    total = groups * rows
    sd = jax.ShapeDtypeStruct
    return pl.pallas_call(
        expert_kernel,
        out_shape=(
            sd((total, width), BF16),
            sd((total, width), BF16),
            sd((planes, 2, width // planes, hidden), BF16),
            sd((planes, 2, hidden // planes, width), BF16),
            sd((2, 8, hidden), F32),
            sd((2, 8, width), F32),
            sd((2, 8, 128), F32),
        ),
        in_specs=[smem_spec(), vmem_spec()] + [any_spec()] * 5 + [vmem_spec()] * 2,
        out_specs=tuple([any_spec()] * 4 + [vmem_spec()] * 3),
        scratch_shapes=[
            pltpu.VMEM((groups, rows, width), BF16),
            pltpu.VMEM((groups, rows, width), BF16),
            pltpu.VMEM((total, width), BF16),
            pltpu.VMEM((total, width), BF16),
            pltpu.VMEM((2, width, hidden), BF16),
            pltpu.VMEM((2, hidden, width), BF16),
            pltpu.VMEM((width, hidden), F32),
            pltpu.VMEM((width, hidden), F32),
            pltpu.VMEM((BLOCK, width), BF16),
            pltpu.VMEM((BLOCK, width), BF16),
            pltpu.VMEM((BLOCK, 128), F32),
            pltpu.VMEM((BLOCK, width), BF16),
            pltpu.VMEM((width, BLOCK), BF16),
            pltpu.VMEM((width, BLOCK), BF16),
            pltpu.VMEM((BLOCK, width), F32),
            pltpu.VMEM((BLOCK, width), F32),
            pltpu.SemaphoreType.DMA((40,)),
        ],
        compiler_params=pltpu.CompilerParams(vmem_limit_bytes=VMEM_MAX),
        cost_estimate=pl.CostEstimate(
            flops=60_000_000_000, bytes_accessed=40_000_000, transcendentals=8_000_000
        ),
        name="experts",
    )(tile_list, meta, x_own, x_all, g_all, up, down, b_up, b_down)


def fast_shards(
    mesh_sizes,
    tokens,
    out_grad,
    segment_ids,
    key_mask,
    sent_task,
    task_experts,
    ln1_gain,
    ln1_bias,
    w_qkv,
    w_proj,
    ln2_gain,
    ln2_bias,
    task_embed,
    w_gate,
    w_up,
    b_up,
    w_down,
    b_down,
):
    groups, planes = mesh_sizes
    row_count, piece, width = tokens.shape
    length = piece * planes
    total = groups * length
    tasks = task_experts.shape[0]
    n_experts = w_gate.shape[1]
    hidden = w_up.shape[2]
    capacity = 4 * row_count * piece // n_experts
    me, z = lax.axis_index("dp"), lax.axis_index("fsdp")

    seg_hot = segment_ids[:, :, None] == jnp.arange(sent_task.shape[1])[None, None, :]
    task_tok = jnp.sum(jnp.where(seg_hot, sent_task[:, None, :], 0), axis=-1)
    code = (task_tok * 16 + segment_ids * 2 + key_mask).astype(F32)
    logits_part = jnp.dot(task_embed.astype(F32), w_gate.astype(F32), precision=exact)
    norm_part = jnp.stack([ln1_gain, ln1_bias, ln2_gain, ln2_bias]).astype(F32)
    bias_part = jnp.concatenate([b_up[0], b_down[0]]).astype(F32)
    parts = [code.reshape(-1), logits_part.reshape(-1), norm_part.reshape(-1), bias_part]
    used = sum(p.shape[0] for p in parts)
    pad_rows = -(-used // 1024) * 8
    payload = jnp.concatenate(parts + [jnp.zeros((pad_rows * 128 - used,), F32)])
    gathered = small_gather(payload.reshape(pad_rows, 128), planes, groups)
    gathered = gathered.reshape(groups, planes, pad_rows * 128)
    ends = []
    at = 0
    for p in parts:
        ends.append((at, at + p.shape[0]))
        at += p.shape[0]
    codes = gathered[:, :, ends[0][0] : ends[0][1]].astype(jnp.int32)
    codes = codes.reshape(groups, planes, row_count, piece)
    logits_all = jnp.sum(gathered[:, :, ends[1][0] : ends[1][1]], axis=(0, 1))
    logits_all = logits_all.reshape(tasks, n_experts)
    norms = gathered[:, :, ends[2][0] : ends[2][1]].reshape(groups * planes, 4, -1)
    norms = norms.transpose(1, 0, 2).reshape(4, width)
    norms = jnp.concatenate([norms, jnp.zeros((4, width), F32)])
    core = me % 2
    biases = lax.dynamic_slice_in_dim(
        gathered[:, :, ends[3][0] : ends[3][1]], me - core, 2, 0
    )
    half = hidden // 2
    bias_up = biases[:, :, : b_up.shape[1]].reshape(2, planes, 2, half // planes)
    bias_up = lax.dynamic_index_in_dim(bias_up, core, 2, keepdims=False).reshape(2, 1, half)
    bias_down = biases[:, :, b_up.shape[1] :].reshape(2, 1, width)
    bias_down = jnp.where(core == 0, bias_down, 0.0)

    seg_first = codes[:, 0, :, 0] % 16 // 2
    seg_last = codes[:, planes - 1, :, piece - 1] % 16 // 2
    single = jnp.argmax((seg_first == seg_last).astype(jnp.int32), axis=1)
    target = jnp.arange(groups) % planes
    slots = jnp.arange(planes)[None, :]
    order = jnp.where(
        slots == target[:, None],
        single[:, None],
        jnp.where(slots == single[:, None], target[:, None], slots),
    ).astype(jnp.int32)
    my_order = lax.dynamic_index_in_dim(order, me, 0, keepdims=False)
    row_of = lax.dynamic_index_in_dim(order, z, 1, keepdims=False)

    tokens_out, grads_out = pick_rows(my_order, (tokens, out_grad), (BF16, BF16))
    dense = jnp.concatenate([w_qkv, w_proj], axis=1)
    my_codes = lax.dynamic_index_in_dim(codes, me, 0, keepdims=False)
    my_code = lax.dynamic_index_in_dim(my_codes, row_of[me], 1, keepdims=False).reshape(length)
    my_seg, my_key = my_code % 16 // 2, my_code % 2
    pair = 2 * HD
    feature = jnp.arange(pair)[None, :]
    hot = my_seg[:, None] == feature
    qf = hot.astype(BF16)
    kf = jnp.where((feature < 8) & ~(hot & (my_key[:, None] == 1)), FAR, 0.0).astype(BF16)

    up_halves = w_up[0].reshape(-1, planes, 2, half // planes).transpose(2, 0, 1, 3)
    up_halves = up_halves.reshape(2, -1, half)
    down_halves = w_down[0].reshape(2, -1, width)
    (row, dense_full, qkv, o, lse, hres, xn2, x_all, g_all, up_all, down_all) = forward(
        tokens_out, grads_out, dense, up_halves, down_halves, norms, qf, kf, HEADS, groups
    )

    choose = (task_experts[:, :, None] == jnp.arange(n_experts)[None, None, :]).astype(F32)

    def gate_values(logits):
        return jax.nn.softmax(jnp.sum(logits[:, None, :] * choose, axis=-1), axis=-1)

    gates, gate_back = jax.vjp(gate_values, logits_all)
    chip_experts = me - core + jnp.arange(2)
    mine = task_experts[None] == chip_experts[:, None, None]
    shifts = jnp.left_shift(1, jnp.arange(tasks, dtype=jnp.int32))
    bits = jnp.sum(jnp.where(mine, shifts[None, :, None], 0), axis=1)
    gate_of_task = jnp.sum(jnp.where(mine, gates[None], 0.0), axis=2)
    task_all = codes // 16
    hits = jnp.right_shift(bits[:, None, None, :, None, None], task_all[None, :, :, None]) & 1
    hits = hits.astype(F32)
    lower = (jnp.arange(piece)[:, None] < jnp.arange(piece)[None, :]).astype(BF16)
    before = jnp.dot(
        hits.reshape(-1, piece).astype(BF16), lower, preferred_element_type=F32
    ).reshape(hits.shape)
    counts = jnp.sum(hits, axis=-1).reshape(2, groups, planes, 2 * row_count)
    ahead = (jnp.cumsum(counts, axis=-1) - counts).reshape(2, groups, planes, 2, row_count)
    rank = before + ahead[..., None]
    kept = jnp.sum(jnp.where(rank < capacity, hits, 0.0), axis=3)
    here = (jnp.arange(row_count)[None, :] == row_of[:, None])[:, None, :, None]
    kept_here = jnp.sum(jnp.where(here[None], kept, 0.0), axis=3).reshape(2, total)
    task_here = jnp.sum(jnp.where(here, task_all, 0), axis=2).reshape(total)
    task_hot = task_here[:, None] == jnp.arange(tasks)[None, :]
    gate_here = jnp.sum(jnp.where(task_hot[None], gate_of_task[:, None, :], 0.0), axis=2)
    gate_here = gate_here * kept_here
    task_mark = jnp.where(kept_here > 0, task_here.astype(F32)[None], -1.0)
    lane = jnp.arange(128)[None, :]
    meta = jnp.zeros((total, 128), F32)
    for k in range(2):
        meta = jnp.where(lane == 2 * k, gate_here[k][:, None], meta)
        meta = jnp.where(lane == 2 * k + 1, task_mark[k][:, None], meta)
    n_tiles = total // TILE
    tile_hit = jnp.max(kept_here.reshape(2, n_tiles, TILE), axis=2) > 0
    hit_rank = jnp.cumsum(tile_hit.astype(jnp.int32), axis=1)
    hit_count = hit_rank[:, -1:]
    index = jnp.arange(n_tiles, dtype=jnp.int32)
    place = jnp.where(tile_hit, hit_rank - 1, hit_count + index[None] - hit_rank)
    tile_list = jnp.sum(
        jnp.where(place[:, None, :] == index[None, :, None], index[None, None, :], 0),
        axis=2,
        dtype=jnp.int32,
    )
    tile_list = jnp.concatenate([hit_count, tile_list], axis=1)

    zd, zy, gu, gd, dbup, dbdown, dgate = experts(
        tile_list,
        meta,
        xn2.reshape(length, width),
        x_all.reshape(groups, length, width),
        g_all.reshape(groups, length, width),
        up_all.reshape(2, width, half),
        down_all.reshape(2, half, width),
        bias_up,
        bias_down,
    )
    small = jnp.concatenate(
        [
            jnp.sum(dgate, axis=1),
            jnp.sum(dbup, axis=1).reshape(-1, 128),
            jnp.sum(dbdown, axis=1).reshape(-1, 128),
        ]
    )
    small = jnp.concatenate([small, jnp.zeros((-small.shape[0] % 8, 128), F32)])
    out_pieces, tok_pieces, shard, gu_in, gd_in, small_all = backward(
        row,
        norms,
        dense_full,
        qf,
        kf,
        qkv,
        o,
        lse,
        hres,
        g_all,
        zd.reshape(groups, length, width),
        zy.reshape(groups, length, width),
        gu,
        gd,
        small,
        HEADS,
    )
    d_w_up = jnp.sum(gu_in.astype(F32), axis=1).reshape(2, -1, planes, half // planes)
    d_w_up = d_w_up.transpose(1, 2, 0, 3).reshape(-1, hidden)
    d_w_down = jnp.sum(gd_in.astype(F32), axis=1).reshape(-1, width)
    output, d_tokens = pick_rows(my_order, (out_pieces, tok_pieces), (BF16, F32))

    chips = small_all.reshape(groups // 2, 2, -1, 128)
    dgate_all = jnp.sum(chips[:, :, :2, :tasks], axis=1).reshape(n_experts, tasks).T
    dgates = jnp.sum(dgate_all[:, None, :] * choose, axis=-1)
    (dlogits,) = gate_back(dgates)
    d_task_embed = jnp.dot(dlogits, w_gate.astype(F32).T, precision=exact)
    d_w_gate = jnp.dot(task_embed.astype(F32).T, dlogits, precision=exact)
    my_chip = lax.dynamic_index_in_dim(chips, me // 2, 0, keepdims=False)
    cut = 2 + 2 * half // 128
    d_b_up = lax.dynamic_index_in_dim(
        my_chip[:, 2:cut].reshape(2, 2, planes, half // planes), core, 1, keepdims=False
    )
    d_b_up = lax.dynamic_index_in_dim(d_b_up, z, 1, keepdims=False).reshape(hidden // planes)
    d_b_down = lax.dynamic_index_in_dim(
        my_chip[0, cut : cut + 2 * width // 128].reshape(2, planes, width // planes),
        core,
        0,
        keepdims=False,
    )
    d_b_down = lax.dynamic_index_in_dim(d_b_down, z, 0, keepdims=False)
    return (
        output,
        d_tokens,
        shard[:, 4 * width],
        shard[:, 4 * width + 1],
        shard[:, : 3 * width],
        shard[:, 3 * width : 4 * width],
        shard[:, 4 * width + 2],
        shard[:, 4 * width + 3],
        d_task_embed,
        d_w_gate,
        d_w_up[None],
        d_b_up[None],
        d_w_down[None],
        d_b_down[None],
    )


def fits_rows(mesh, tokens, w_gate):
    groups, planes = mesh.shape["dp"], mesh.shape["fsdp"]
    return (
        groups == 8
        and planes == 4
        and tokens.shape[0] == groups * planes
        and w_gate.shape[1] == groups
        and tokens.shape[1] % (planes * QCHUNK) == 0
    )


def solution(mesh):
    placed = (
        P("dp", "fsdp", None),
        P("dp", "fsdp", None),
        P("dp", "fsdp"),
        P("dp", "fsdp"),
        P("dp", None),
        P(),
        P(("dp", "fsdp")),
        P(("dp", "fsdp")),
        P(("dp", "fsdp"), None),
        P(("dp", "fsdp"), None),
        P(("dp", "fsdp")),
        P(("dp", "fsdp")),
        P(None, ("dp", "fsdp")),
        P(("dp", "fsdp"), None),
        P("dp", "fsdp", None),
        P("dp", "fsdp"),
        P("dp", "fsdp", None),
        P("dp", "fsdp"),
    )
    placed_out = (
        P("dp", "fsdp", None),
        P("dp", "fsdp", None),
        P(("dp", "fsdp")),
        P(("dp", "fsdp")),
        P(("dp", "fsdp"), None),
        P(("dp", "fsdp"), None),
        P(("dp", "fsdp")),
        P(("dp", "fsdp")),
        P(None, ("dp", "fsdp")),
        P(("dp", "fsdp"), None),
        P("dp", "fsdp", None),
        P("dp", "fsdp"),
        P("dp", "fsdp", None),
        P("dp", "fsdp"),
    )

    def program(*args):
        fast = fits_rows(mesh, args[0], args[13])
        sizes = (mesh.shape["dp"], mesh.shape["fsdp"])
        return jax.shard_map(
            functools.partial(fast_shards, sizes) if fast else shards,
            mesh=mesh,
            in_specs=placed,
            out_specs=placed_out,
            check_vma=False,
        )(*args)

    return program
```

time: 735 us -> 501 us (0.68); the launches traced: 723 us -> 508 us
  waiting for transfers between devices: 172 us -> 0 us
  starting transfers between devices: 59.7 us -> 0 us
  Pallas kernels: 439 us -> 458 us
    ppermute x32 -> x0, waiting for transfers between devices: 172 us -> none  [the longest x18 88.8 us: z_shift(): lax.ppermute(x, 'fsdp', [(i, (i + k) % planes) for i in range(planes)])]
    ppermute x32 -> x0, starting transfers between devices: 59.7 us -> none  [the longest x18 32.3 us: z_shift(): lax.ppermute(x, 'fsdp', [(i, (i + k) % planes) for i in range(planes)])]
    pallas_call x7 -> x3, Pallas kernels: 418 us -> 437 us  [the longest x1 192 us: backward(): pl.pallas_call(functools.partial(backward_kernel, heads, planes, groups),...]
  transfers between devices with their start and end apart: 32 -> 0, of which waited for: 10 -> 0; matrix products, arithmetic and copies ran while one was open for 5% -> 0% of each run, Pallas kernels for 33% -> 0%
where the time goes in v2:
time: 501 us; the launch traced here: 508 us
  Pallas kernels  458 us (91%)
  other arithmetic  26.7 us (5%)
  local copies, waits for them, and re-layouts  16.9 us (3%)
    pallas_call x1, Pallas kernels, backward(): pl.pallas_call(functools.partial(backward_kernel, heads, planes, groups),...  192 us
    pallas_call x1, Pallas kernels, forward(): pl.pallas_call(functools.partial(forward_kernel, heads, planes), out_shap...  146 us
    pallas_call x1, Pallas kernels, experts(): pl.pallas_call(expert_kernel, out_shape=(sd((total, width), BF16), sd((to...  99 us
    pallas_call x1, Pallas kernels, small_gather(): pl.pallas_call(functools.partial(small_gather_kernel, planes, groups), ou...  11.9 us

profile of v2, /device:TPU:25, one launch (start us, length us, event | category | flops | bytes accessed | tf_op | source)
XLA Modules:
  0.0 508.3 jit_solution(15719758442031660980)
XLA Ops:
  0.8 0.9 fusion.25
  2.4 0.7 maximum_convert_fusion.1
  3.9 0.8 select_reduce_fusion.5
  4.7 0.7 convert_bitcast_fusion
  5.4 0.9 fusion.38
  7.0 1.4 pad_maximum_fusion.w_ref
  8.5 11.9 %routing_gather.1 = f32[8,4,16,128]{3,2,1,0:T(8,128)} custom-call(f32[16,128]{1,0:T(8,128)} %bitcast.109), custom_call_target="tpu_custom_call" | custom-call | tf_op jit(solution)/shard_map/routing_gather/pallas_call | solution.py:559
  20.4 1.0 reshape.457
  21.6 0.7 select_reduce_fusion.8
  22.9 0.8 fusion.26
  29.4 0.7 fusion.19.order_ref
  32.4 1.1 select_convert_fusion.kf_ref
  33.5 0.9 fusion.6.qf_ref
  37.8 1.2 reshape.459.upw_ref
  39.0 4.4 row_order.2
  43.4 6.3 %select_select_fusion.meta_ref = f32[8192,128]{1,0:T(8,128)} fusion(f32[8192]{0:T(1024)S(1)} %bitcast.103, f32[8192]{0:T(1024)S(1)} %bitcast.102, f32[8192]{0:T(1024)S(1)} %bitcast.104, f32[8192]{0:T(1024)S(1)} %bitcast.101, pred[128]{0:T(512)(128)(4,1)S(1)} %get-tuple-element.188, pred[128]{0:T(512)(128)(4,1)S(1)} %get-tuple-element.189, ...), kind=kLoop, calls=%fused_computation.2 | loop fusion | flops 4194304 | bytes 4325888 | tf_op jit(solution)/shard_map/jit(_where)/select_n | solution.py:1719
  49.7 146.3 %attention_forward.1 = (bf16[4,256,512]{2,1,0:T(8,128)(2,1)}, bf16[8,64,2048]{2,1,0:T(8,128)(2,1)}, bf16[1024,1536]{1,0:T(8,128)(2,1)}, bf16[1024,512]{1,0:T(8,1...) custom-call(bf16[4,256,512]{2,1,0:T(8,128)(2,1)} %get-tuple-element., ...), custom_call_target="tpu_custom_call" | custom-call | flops 40000000000 | bytes 10000000 | tf_op jit(solution)/shard_map/attention_forward/pallas_call | solution.py:957
  196.0 99.0 %experts.1 = (bf16[8192,512]{1,0:T(8,128)(2,1)}, bf16[8192,512]{1,0:T(8,128)(2,1)}, bf16[4,2,128,1024]{3,2,1,0:T(8,128)(2,1)}, bf16[4,2,256,512]{3,2,1,0:T(8,128...) custom-call(s32[2,513]{1,0:T(2,128)} %pad_add_fusion.list_ref, ...), custom_call_target="tpu_custom_call" | custom-call | flops 60000002048 | bytes 40000000 | tf_op jit(solution)/shard_map/experts/pallas_call | solution.py:1550
  295.0 0.7 reduce_sum.209
  295.8 0.8 reduce_sum.211
  296.5 0.9 reduce_sum.210
  298.1 192.1 %attention_backward.1 = (bf16[4,256,512]{2,1,0:T(8,128)(2,1)}, bf16[4,256,512]{2,1,0:T(8,128)(2,1)}, f32[16,2176]{1,0:T(8,128)}, bf16[2,4,128,1024]{3,2,1,0:T(8,...) custom-call(bf16[4,256,512]{2,1,0:T(8,128)(2,1)} %get-tuple-element.46.row_ref, ...), custom_call_target="tpu_custom_call" | custom-call | flops 80000000000 | bytes 20000000 | tf_op jit(solution)/shard_map/attention_backward/pallas_call | solution.py:1310
  490.3 1.6 slice_reduce_fusion.2
  491.9 0.8 slice_reduce_fusion.1
  492.7 0.8 dynamic-slice_bitcast_fusion
  493.5 0.7 convolution_bitcast_fusion
  494.3 0.8 fusion.39
  496.2 1.4 slice.90
  497.6 1.5 slice.89
  499.1 4.6 row_order.3
  504.5 1.3 copy.159
  506.5 1.3 convert_reduce_fusion
  (121 shorter events, 15.6 us)
Async XLA Ops:
  0.6 4.8 copy-start
  22.4 1.3 copy-start.4
  22.4 1.3 copy-start.7
  22.4 1.3 copy-start.9
  31.3 5.9 %copy-start.3 = (bf16[1,128,2048]{2,1,0:T(8,128)(2,1)S(1)}, bf16[1,128,2048]{2,1,0:T(8,128)(2,1)}, u32[]{:S(2)}) copy-start(bf16[1,128,2048]{2,1,0:T(8,128)(2,1)} %param.32) | copy-start | bytes 1572868
  298.1 195.3 %copy-start.6 = (s32[32,2]{0,1:T(2,128)S(1)}, s32[32,2]{0,1:T(2,128)}, u32[]{:S(2)}) copy-start(s32[32,2]{0,1:T(2,128)} %param.23) | copy-start | bytes 772
  298.1 195.3 %copy-start.5 = (f32[32,2]{0,1:T(2,128)S(1)}, f32[32,2]{0,1:T(2,128)}, u32[]{:S(2)}) copy-start(f32[32,2]{0,1:T(2,128)} %copy-done.4) | copy-start | bytes 772
  298.1 195.3 %copy-start.8 = (f32[32]{0:T(128)S(1)}, f32[32]{0:T(128)}, u32[]{:S(2)}) copy-start(f32[32]{0:T(128)} %copy-done.7) | copy-start | bytes 388
  298.1 195.3 %copy-start.12 = (f32[32]{0:T(128)S(1)}, f32[32]{0:T(128)}, u32[]{:S(2)}) copy-start(f32[32]{0:T(128)} %multiply_divide_fusion) | copy-start | bytes 388
  298.1 195.4 %copy-start.10 = (f32[32]{0:T(128)S(1)}, f32[32]{0:T(128)}, u32[]{:S(2)}) copy-start(f32[32]{0:T(128)} %copy-done.9) | copy-start | bytes 388
  298.1 196.1 %copy-start.11 = (bf16[16,8]{0,1:T(8,128)(2,1)S(1)}, bf16[16,8]{0,1:T(8,128)(2,1)}, u32[]{:S(2)}) copy-start(bf16[16,8]{0,1:T(8,128)(2,1)} %param.31) | copy-start | bytes 772
  490.2 13.5 %copy-start.2 = (bf16[2,4,128,1024]{3,2,1,0:T(8,128)(2,1)S(1)}, bf16[2,4,128,1024]{3,2,1,0:T(8,128)(2,1)}, u32[]{:S(2)}) copy-start(bf16[2,4,128,1024]{3,2,1,0:T(8,128)(2,1)} %get-tuple-element.70) | copy-start | bytes 6291460
  504.5 2.0 copy-start.1

commit v3 on v2

--- a/solution.py
+++ b/solution.py
@@ -338,10 +338,10 @@
 
 
 MESH_ID = pl.DeviceIdType.MESH
-VMEM_MAX = 60 * 1024 * 1024
+VMEM_MAX = 62 * 1024 * 1024
 TILE = 16
 BLOCK = 512
-FCHUNK = 512
+FCHUNK = 1024
 QCHUNK = 256
 FAR = -float(2**30)
 F32 = jnp.float32
@@ -519,11 +519,11 @@
     def pass_on(self, c):
         x_part, y_part = self.block(self.xn).at[c], self.block(self.yn).at[c]
         self.all[0, c].wait_recv()
-        if c < 2:
+        if c % 2 == 0:
             self.send(3, c, x_part, self.xn, self.yn)
         self.send(4, c, x_part, self.xn, self.sib)
         self.all[1, c].wait_recv()
-        if c >= 2:
+        if c % 2 == 1:
             self.send(3, c, y_part, self.yn, self.xn)
         self.send(5, c, y_part, self.yn, self.sib)
 
@@ -537,37 +537,6 @@
                 self.all[kind, c].wait_recv()
         for copy in self.all.values():
             copy.wait_send()
-
-
-def small_gather_kernel(planes, groups, in_ref, out_ref, send_sems, recv_sems):
-    me, z = lax.axis_index("dp"), lax.axis_index("fsdp")
-    z_peers = [(me, lax.rem(z + k, planes)) for k in range(1, planes)]
-    d_peers = [(lax.rem(me + k, groups), z) for k in range(1, groups)]
-    greet(z_peers + d_peers)
-    sender = Sender(send_sems, recv_sems)
-    out_ref[me, z] = in_ref[...]
-    first = [sender.start(in_ref, out_ref.at[me, z], peer) for peer in z_peers]
-    for copy in first:
-        copy.wait_recv()
-    second = [sender.start(out_ref.at[me], out_ref.at[me], peer) for peer in d_peers]
-    for copy in second:
-        copy.wait_recv()
-    sender.drain()
-
-
-def small_gather(payload, planes, groups):
-    return pl.pallas_call(
-        functools.partial(small_gather_kernel, planes, groups),
-        out_shape=jax.ShapeDtypeStruct((groups, planes) + payload.shape, payload.dtype),
-        in_specs=[vmem_spec()],
-        out_specs=vmem_spec(),
-        scratch_shapes=[
-            pltpu.SemaphoreType.DMA((planes + groups,)),
-            pltpu.SemaphoreType.DMA((planes + groups,)),
-        ],
-        compiler_params=pltpu.CompilerParams(collective_id=1, has_side_effects=True),
-        name="routing_gather",
-    )(payload)
 
 
 def plane_scatter_steps(z_ref, own, theirs, deep, near_x, near_y, sender, loc_sems, z):
@@ -580,14 +549,17 @@
     loads, trades = {}, {}
     for slot in (3, 1, 2, 0):
         pos = chips[slot]
+        trades[slot] = sender.start(
+            z_ref.at[at(pos[0], pos[1], 1 - core)], theirs.at[slot], (sib, z)
+        )
+
+    yield
+    for slot in (3, 1, 2, 0):
+        pos = chips[slot]
         loads[slot] = pltpu.make_async_copy(
             z_ref.at[at(pos[0], pos[1], core)], own.at[slot], loc_sems.at[slot]
         )
         loads[slot].start()
-        trades[slot] = sender.start(
-            z_ref.at[at(pos[0], pos[1], 1 - core)], theirs.at[slot], (sib, z)
-        )
-
     yield
 
     def add(slot, part):
@@ -636,31 +608,194 @@
 def pick_rows_kernel(order_ref, *refs):
     count = len(refs) // 2
     for a in range(count):
-        refs[count + a][...] = refs[a][...].astype(refs[count + a].dtype)
+        for r in range(refs[a].shape[0]):
+            refs[count + a][r] = refs[a][order_ref[0, r]].astype(refs[count + a].dtype)
 
 
 def pick_rows(order, arrays, kinds):
-    def block(array):
-        return (1,) + array.shape[1:]
-
     return pl.pallas_call(
         pick_rows_kernel,
         out_shape=tuple(
             jax.ShapeDtypeStruct(array.shape, kind) for array, kind in zip(arrays, kinds)
         ),
-        grid_spec=pltpu.PrefetchScalarGridSpec(
-            num_scalar_prefetch=1,
-            grid=(arrays[0].shape[0],),
-            in_specs=[
-                pl.BlockSpec(block(array), lambda r, order_ref: (order_ref[r], 0, 0))
-                for array in arrays
-            ],
-            out_specs=tuple(
-                pl.BlockSpec(block(array), lambda r, order_ref: (r, 0, 0)) for array in arrays
-            ),
-        ),
+        in_specs=[smem_spec()] + [vmem_spec()] * len(arrays),
+        out_specs=tuple(vmem_spec() for _ in arrays),
+        compiler_params=pltpu.CompilerParams(vmem_limit_bytes=VMEM_MAX),
         name="row_order",
     )(order, *arrays)
+
+
+PAYLOAD = 48
+CODE_LOW, CODE_HIGH, BIAS_UP, BIAS_DOWN, NORMS, LOGITS = 0, 4, 8, 12, 13, 16
+
+
+def make_payload(payload, sent_ref, seg_ref, key_ref, logit_ref, norm_ref, bup_ref, bdown_ref):
+    seg = seg_ref[...]
+    row_count, piece = seg.shape
+    row = lax.broadcasted_iota(jnp.int32, seg.shape, 0)
+    task = jnp.zeros_like(seg)
+    for r in range(row_count):
+        for k in range(sent_ref.shape[1]):
+            task = jnp.where((row == r) & (seg == k), sent_ref[r, k], task)
+    code = (task * 16 + seg * 2 + key_ref[...]).astype(F32)
+    payload[...] = jnp.zeros_like(payload)
+    payload[CODE_LOW : CODE_LOW + row_count] = code[:, : piece // 2]
+    payload[CODE_HIGH : CODE_HIGH + row_count] = code[:, piece // 2 :]
+    for k in range(bup_ref.shape[1] // 128):
+        payload[BIAS_UP + k : BIAS_UP + k + 1] = bup_ref[:, k * 128 : (k + 1) * 128].astype(F32)
+    payload[BIAS_DOWN : BIAS_DOWN + 1] = bdown_ref[...].astype(F32)
+    payload[NORMS : NORMS + 1] = norm_ref[...]
+    tasks, n_experts = logit_ref.shape
+    payload[LOGITS : LOGITS + tasks, :n_experts] = logit_ref[...]
+
+
+def code_segment(code):
+    return lax.shift_right_logical(code.astype(jnp.int32), 1) & 7
+
+
+def row_order(codes_ref, me, planes):
+    single = jnp.int32(0)
+    for r in reversed(range(planes)):
+        first = jnp.max(code_segment(codes_ref[me, 0, CODE_LOW + r : CODE_LOW + r + 1, :1]))
+        last = jnp.max(
+            code_segment(codes_ref[me, planes - 1, CODE_HIGH + r : CODE_HIGH + r + 1, 127:])
+        )
+        single = jnp.where(first == last, r, single)
+    target = lax.rem(me, planes)
+    return [
+        jnp.where(p == target, single, jnp.where(p == single, target, p)) for p in range(planes)
+    ]
+
+
+def row_features(codes_ref, me, order, z, planes, qf_ref, kf_ref, order_ref):
+    mine = order[0]
+    for p in range(1, planes):
+        mine = jnp.where(z == p, order[p], mine)
+    parts = []
+    for p in range(planes):
+        low, high = codes_ref[me, p, CODE_LOW : CODE_LOW + 4], codes_ref[me, p, CODE_HIGH : CODE_HIGH + 4]
+        row = lax.broadcasted_iota(jnp.int32, low.shape, 0)
+        for half in (low, high):
+            parts.append(jnp.sum(jnp.where(row == mine, half, 0.0), axis=0, keepdims=True))
+    columns = jnp.concatenate(parts, axis=0).T
+    lane = lax.broadcasted_iota(jnp.int32, (128, qf_ref.shape[1]), 1)
+    for k in range(2 * planes):
+        code = columns[:, k : k + 1].astype(jnp.int32)
+        hot = (lax.shift_right_logical(code, 1) & 7) == lane
+        part = slice(k * 128, (k + 1) * 128)
+        qf_ref[part, :] = jnp.where(hot, 1.0, 0.0).astype(BF16)
+        seen = hot & ((code & 1) == 1)
+        kf_ref[part, :] = jnp.where((lane < 8) & jnp.logical_not(seen), FAR, 0.0).astype(BF16)
+    spot = lax.broadcasted_iota(jnp.int32, order_ref.shape, 1)
+    table = jnp.zeros(order_ref.shape, jnp.int32)
+    for p in range(planes):
+        table = jnp.where(spot == p, order[p], table)
+    order_ref[...] = table
+
+
+def gather_norms(codes_ref, norm_ref):
+    devices = codes_ref.shape[0] * codes_ref.shape[1]
+    width = norm_ref.shape[1]
+    size = width // devices
+    shards = codes_ref[:, :, NORMS : NORMS + 1, :].reshape(devices, 128).astype(BF16)
+    lane = lax.broadcasted_iota(jnp.int32, (128, width), 0)
+    column = lax.broadcasted_iota(jnp.int32, (128, width), 1)
+    owner = lax.broadcasted_iota(jnp.int32, (devices, width), 0)
+    owned = lax.broadcasted_iota(jnp.int32, (devices, width), 1) // size
+    for k in range(4):
+        place = jnp.where(lane == k * size + lax.rem(column, size), 1.0, 0.0).astype(BF16)
+        full = jnp.where(owner == owned, dot_nn(shards, place), 0.0)
+        norm_ref[k : k + 1] = jnp.sum(full, axis=0, keepdims=True)
+
+
+def routing_marks(codes_ref, te_ref, marks_ref, gates_ref, me, z, planes, capacity):
+    groups = codes_ref.shape[0]
+    tasks = te_ref.shape[0]
+    count = groups * planes * planes
+    low = codes_ref[:, :, CODE_LOW : CODE_LOW + planes, :].reshape(count, 128)
+    high = codes_ref[:, :, CODE_HIGH : CODE_HIGH + planes, :].reshape(count, 128)
+    code = jnp.concatenate([low, high], axis=1).astype(jnp.int32)
+    piece = code.shape[1]
+    task = lax.shift_right_logical(code, 4)
+    one = lax.broadcasted_iota(jnp.int32, (count, count), 0)
+    two = lax.broadcasted_iota(jnp.int32, (count, count), 1)
+    block_one, block_two = one // planes, two // planes
+    row_one, row_two = lax.rem(one, planes), lax.rem(two, planes)
+
+    def table(mask):
+        return jnp.where(mask, 1.0, 0.0).astype(BF16)
+
+    whole = table(block_one == block_two)
+    ahead_rows = table((block_one == block_two) & (row_two < row_one))
+    group_one, group_two = block_one // planes, block_two // planes
+    plane_two = lax.rem(block_two, planes)
+    same_row = (group_one == group_two) & (row_one == row_two)
+
+    def wide(column):
+        return jnp.broadcast_to(column, (count, 128)).astype(BF16)
+
+    seg = lax.shift_right_logical(code, 1) & 7
+    first = dot_nn(table(same_row & (plane_two == 0)), wide(seg[:, :1].astype(F32)))
+    last = dot_nn(
+        table(same_row & (plane_two == planes - 1)), wide(seg[:, piece - 1 :].astype(F32))
+    )
+    lone = jnp.where(first == last, 1.0, 0.0)
+    lone = jnp.where(dot_nn(ahead_rows, lone.astype(BF16)) == 0.0, lone, 0.0)
+    row = lax.rem(lax.broadcasted_iota(jnp.int32, (count, 128), 0), planes)
+    group = lax.broadcasted_iota(jnp.int32, (count, 128), 0) // (planes * planes)
+    single = dot_nn(whole, (lone * row.astype(F32)).astype(BF16)).astype(jnp.int32)
+    target = lax.rem(group, planes)
+    picked = jnp.where(z == target, single, jnp.where(z == single, target, z))
+    here = jnp.where(row == picked, 1.0, 0.0)[:, :1]
+
+    before_table = table(
+        lax.broadcasted_iota(jnp.int32, (piece, piece), 0)
+        < lax.broadcasted_iota(jnp.int32, (piece, piece), 1)
+    )
+    gather = table(
+        lax.broadcasted_iota(jnp.int32, (count // planes, count), 0)
+        == lax.broadcasted_iota(jnp.int32, (count // planes, count), 1) // planes
+    )
+    chip = me - lax.rem(me, 2)
+    for e in range(2):
+        hits = []
+        for j in range(2):
+            bits = jnp.int32(0)
+            for t in range(tasks):
+                bit = (1 << t) if t < 31 else -(1 << 31)
+                bits = bits | jnp.where(te_ref[t, j] == chip + e, jnp.int32(bit), jnp.int32(0))
+            hits.append((lax.shift_right_logical(jnp.full(task.shape, bits), task) & 1).astype(F32))
+        kept = jnp.zeros(task.shape, F32)
+        base = jnp.zeros((count, 128), F32)
+        for j in range(2):
+            total = wide(jnp.sum(hits[j], axis=1, keepdims=True))
+            rank = dot_nn(hits[j].astype(BF16), before_table)
+            rank = rank + (base + dot_nn(ahead_rows, total))[:, :1]
+            kept = kept + jnp.where(rank < capacity, hits[j], 0.0)
+            base = base + dot_nn(whole, total)
+        mark = kept * here * (task + 1).astype(F32)
+        marks_ref[e] = dot_nn(gather, mark.astype(BF16)) - 1.0
+
+    logits = jnp.sum(
+        codes_ref[:, :, LOGITS : LOGITS + tasks, :].reshape(groups * planes, tasks, 128), axis=0
+    )
+    lane = lax.broadcasted_iota(jnp.int32, (tasks, 128), 1)
+    task_row = lax.broadcasted_iota(jnp.int32, (tasks, 128), 0)
+    hot = []
+    for j in range(2):
+        chosen = jnp.zeros((tasks, 128), jnp.int32)
+        for t in range(tasks):
+            chosen = jnp.where(task_row == t, te_ref[t, j], chosen)
+        hot.append(lane == chosen)
+    level = [jnp.sum(jnp.where(h, logits, 0.0), axis=1, keepdims=True) for h in hot]
+    top = jnp.maximum(level[0], level[1])
+    weight = [jnp.exp(v - top) for v in level]
+    both = weight[0] + weight[1]
+    grid = jnp.zeros((tasks, 128), F32)
+    for j in range(2):
+        grid = jnp.where(hot[j], weight[j] / both, grid)
+    grid = jnp.concatenate([grid, jnp.zeros((128 - tasks, 128), F32)], axis=0)
+    gates_ref[...] = grid.T[:groups]
 
 
 def unit_copy(src, dst, send_sem, recv_sem, peer):
@@ -747,17 +882,33 @@
             for m in range(2)
         ]
 
-    def start(self):
-        for copy in self.mine() + self.own():
-            copy.start()
-
-    def pass_on(self, first):
+    def start(self, kind):
+        self.mine()[kind].start()
+        copies = self.own()[5 * kind : 5 * kind + 5]
+        for k, copy in enumerate(copies):
+            if k not in (1, 3):
+                copy.start()
+
+        @pl.when(self.inner)
+        def _():
+            for k, copy in enumerate(copies):
+                if k in (1, 3):
+                    copy.start()
+
+    def start_far(self, kind):
+        @pl.when(jnp.logical_not(self.inner))
+        def _():
+            for k, copy in enumerate(self.own()):
+                if k in (5 * kind + 1, 5 * kind + 3):
+                    copy.start()
+
+    def pass_on(self, first, kind):
         for side in range(2):
 
             @pl.when((self.z == 1 + side))
             def _():
                 j = side if first else 1 - side
-                for copy in self.passed(j):
+                for copy in self.passed(j)[2 * kind : 2 * kind + 2]:
                     copy.wait_recv()
                     copy.start()
 
@@ -794,27 +945,55 @@
 def forward_kernel(
     heads,
     planes,
+    capacity,
+    sent_ref,
+    te_ref,
+    seg_ref,
+    key_ref,
+    logit_ref,
+    shard_norms,
+    bup_ref,
+    bdown_ref,
     tok_ref,
     gm_ref,
-    w_ref,
-    upw_ref,
-    downw_ref,
+    wqkv_ref,
+    wproj_ref,
+    upw_in,
+    downw_in,
+    codes_ref,
+    marks_ref,
+    gates_ref,
+    order_ref,
     norm_ref,
     qf_ref,
     kf_ref,
+    row_out,
+    dense_out,
+    qkv_out,
+    o_out,
+    lse_out,
+    hres_out,
+    xn2_ref,
+    x_all,
+    g_all,
+    up_all,
+    down_all,
     row_ref,
     dense_ref,
     qkv_ref,
     o_ref,
     lse_ref,
     hres_ref,
-    xn2_ref,
-    x_all,
-    g_all,
-    up_all,
-    down_all,
     kaug,
     vaug,
+    w_ref,
+    upw_ref,
+    downw_ref,
+    payload,
+    tok_out,
+    gm_out,
+    p_send,
+    p_recv,
     z_send,
     z_recv,
     w_send,
@@ -827,11 +1006,35 @@
     u_pass,
     u_recv,
     loc_sems,
+    out_sems,
+    in_sems,
 ):
     me, z = lax.axis_index("dp"), lax.axis_index("fsdp")
     z_peers = [(me, lax.rem(z + k, planes)) for k in range(1, planes)]
-    greet(column_peers(planes) + plane_peers(z))
-    rows, width = qkv_ref.shape[0], row_ref.shape[2]
+    groups = codes_ref.shape[0]
+    d_peers = [(lax.rem(me + k, groups), z) for k in range(1, groups)]
+    width = row_ref.shape[2]
+    stages = [
+        pltpu.make_async_copy(wqkv_ref, w_ref.at[:, pl.ds(0, 3 * width)], in_sems.at[0]),
+        pltpu.make_async_copy(wproj_ref, w_ref.at[:, pl.ds(3 * width, width)], in_sems.at[1]),
+        pltpu.make_async_copy(downw_in.at[0], downw_ref, in_sems.at[2]),
+    ]
+    part = upw_ref.shape[2] // planes
+    for p in range(planes):
+        for h in range(2):
+            stages.append(
+                pltpu.make_async_copy(
+                    upw_in.at[0, :, pl.ds((2 * p + h) * part, part)],
+                    upw_ref.at[h, :, pl.ds(p * part, part)],
+                    in_sems.at[len(stages)],
+                )
+            )
+    for copy in stages:
+        copy.start()
+    greet(column_peers(planes) + d_peers)
+    rows = qkv_ref.shape[0]
+    for copy in stages:
+        copy.wait()
     chunk = row_ref.shape[1]
     head = width // heads
     pair = 2 * head
@@ -841,14 +1044,27 @@
         w_ref, dense_ref.at[me, pl.ds(z * shard, shard)], loc_sems.at[0]
     )
     dense_own.start()
-    tok_own = pltpu.make_async_copy(tok_ref.at[z], row_ref.at[z], loc_sems.at[1])
-    tok_own.start()
-    gm_own = pltpu.make_async_copy(gm_ref.at[z], g_all.at[me, z], loc_sems.at[2])
-    gm_own.start()
+    make_payload(payload, sent_ref, seg_ref, key_ref, logit_ref, shard_norms, bup_ref, bdown_ref)
+    codes_ref[me, z] = payload[...]
+    p_sender = Sender(p_send, p_recv)
+    codes_z = [p_sender.start(payload, codes_ref.at[me, z], peer) for peer in z_peers]
     dense_z = [
         sender.start(w_ref, dense_ref.at[me, pl.ds(z * shard, shard)], peer) for peer in z_peers
     ]
-    toks = [sender.start(tok_ref.at[peer[1]], row_ref.at[z], peer) for peer in z_peers]
+    spread = WeightSpread(upw_ref, downw_ref, up_all, down_all, (u_own, u_pass, u_recv, loc_sems.at[pl.ds(3, 2)]))
+    spread.start(0)
+    for copy in codes_z:
+        copy.wait_recv()
+    order = row_order(codes_ref, me, planes)
+    for c in range(planes):
+        tok_out[c] = tok_ref[order[c]]
+        gm_out[c] = gm_ref[order[c]]
+    toks = [sender.start(tok_out.at[peer[1]], row_ref.at[z], peer) for peer in z_peers]
+    tok_own = pltpu.make_async_copy(tok_out.at[z], row_ref.at[z], loc_sems.at[1])
+    tok_own.start()
+    gm_own = pltpu.make_async_copy(gm_out.at[z], g_all.at[me, z], loc_sems.at[2])
+    gm_own.start()
+    codes_d = [p_sender.start(codes_ref.at[me], codes_ref.at[me], peer) for peer in d_peers]
     dense_own.wait()
     for copy in dense_z:
         copy.wait_recv()
@@ -856,17 +1072,21 @@
     plane_gather_steps(
         lambda i: dense_ref.at[i], dense_ref.at[me], planes * shard, dense_sender, z
     )
+    row_features(codes_ref, me, order, z, planes, qf_ref, kf_ref, order_ref)
+    for copy in codes_d:
+        copy.wait_recv()
+    gather_norms(codes_ref, norm_ref)
+    routing_marks(codes_ref, te_ref, marks_ref, gates_ref, me, z, planes, capacity)
+    x_gather = PlaneGather(lambda i: x_all.at[i], xn2_ref, x_send, x_recv)
+    g_gather = PlaneGather(lambda i: g_all.at[i], g_all.at[me], g_send, g_recv)
+
     for copy in toks:
         copy.wait_recv()
     tok_own.wait()
-    gms = [sender.start(gm_ref.at[peer[1]], g_all.at[me, z], peer) for peer in z_peers]
-    spread = WeightSpread(upw_ref, downw_ref, up_all, down_all, (u_own, u_pass, u_recv, loc_sems.at[pl.ds(3, 2)]))
-    x_gather = PlaneGather(lambda i: x_all.at[i], xn2_ref, x_send, x_recv)
-    g_gather = PlaneGather(lambda i: g_all.at[i], g_all.at[me], g_send, g_recv)
+    gms = [sender.start(gm_out.at[peer[1]], g_all.at[me, z], peer) for peer in z_peers]
 
     lane = lax.broadcasted_iota(jnp.int32, (rows, pair), 1)
     lane_c = lax.broadcasted_iota(jnp.int32, (chunk, pair), 1)
-    w_qkv = dense_ref[:, :, : 3 * width].reshape(width, 3 * width)
 
     def project(c, carry):
         part = pl.ds(pl.multiple_of(c * chunk, chunk), chunk)
@@ -908,12 +1128,15 @@
                 tops.append(top)
             total = acc[:, pair:]
             o_ref[part, cols] = (acc[:, :pair] / total).astype(BF16)
-            top = jnp.where(lane_c < head, tops[0], tops[1])
-            lse_ref[part, cols] = top + jnp.log(total)
+            table = lse_ref[part, :]
+            for side in range(2):
+                level = tops[side] + jnp.log(total[:, side * head : side * head + 1])
+                table = jnp.where(lane_c == 2 * g + side, level, table)
+            lse_ref[part, :] = table
             return carry
 
         lax.fori_loop(0, heads // 2, one_pair, 0)
-        w_proj = dense_ref[:, :, 3 * width :].reshape(width, width)
+        w_proj = dense_ref[:, :, 3 * width : 4 * width].reshape(width, width)
         hres = row_ref[c].astype(F32) + dot_nn(o_ref[part, :], w_proj)
         hres_ref[part, :] = hres
         normal, _ = norm_parts(hres)
@@ -925,55 +1148,105 @@
     for copy in gms:
         copy.wait_recv()
     gm_own.wait()
-    spread.start()
+    spread.start(1)
+    spread.pass_on(True, 0)
     for c in range(4):
         g_gather.start(c)
     attend(2)
     x_gather.pass_on(0)
     x_gather.pass_on(1)
+    spread.start_far(0)
     attend(3)
+    spread.start_far(1)
+    spread.pass_on(True, 1)
+    pairs = (
+        (row_ref, row_out),
+        (dense_ref, dense_out),
+        (qkv_ref, qkv_out),
+        (o_ref, o_out),
+        (lse_ref, lse_out),
+        (hres_ref, hres_out),
+    )
+    saves = [pltpu.make_async_copy(a, b, out_sems.at[k]) for k, (a, b) in enumerate(pairs)]
+    for copy in saves:
+        copy.start()
     x_gather.pass_on(2)
-    for c in range(4):
-        g_gather.pass_on(c)
+    g_gather.pass_on(0)
+    g_gather.pass_on(1)
+    spread.pass_on(False, 0)
     x_gather.pass_on(3)
-    spread.pass_on(True)
+    g_gather.pass_on(2)
+    spread.pass_on(False, 1)
+    g_gather.pass_on(3)
     for c in range(4):
         x_gather.pass_diag(c)
         g_gather.pass_diag(c)
-    spread.pass_on(False)
+    for copy in saves:
+        copy.wait()
     x_gather.finish()
     g_gather.finish()
     spread.finish()
-    sender.drain()
-    dense_sender.drain()
-
-
-def forward(tokens, grads, dense, up, down, norms, qf, kf, heads, groups):
+    for sender in (p_sender, sender, dense_sender):
+        sender.drain()
+
+
+def forward(
+    sent_task, task_experts, routing, tokens, grads, w_qkv, w_proj, up, down, heads, groups, capacity
+):
     planes, piece, width = tokens.shape
     rows = planes * piece
+    half = up.shape[2] // 2
+    dense = jax.ShapeDtypeStruct((w_qkv.shape[0], 4 * width), BF16)
+    up_half = (2, up.shape[1], half)
+    down_half = (2, down.shape[1] // 2, width)
     pair = 2 * (width // heads)
     sd = jax.ShapeDtypeStruct
     dma = pltpu.SemaphoreType.DMA
     return pl.pallas_call(
-        functools.partial(forward_kernel, heads, planes),
+        functools.partial(forward_kernel, heads, planes, capacity),
         out_shape=(
+            sd((groups, planes, PAYLOAD, 128), F32),
+            sd((2, groups * planes, piece), F32),
+            sd((groups, 128), F32),
+            sd((8, 128), jnp.int32),
+            sd((8, width), F32),
+            sd((rows, pair), BF16),
+            sd((rows, pair), BF16),
             sd(tokens.shape, BF16),
             sd((groups, planes * dense.shape[0], dense.shape[1]), BF16),
             sd((rows, 3 * width), BF16),
             sd((rows, width), BF16),
-            sd((rows, width), F32),
+            sd((rows, pair), F32),
             sd((rows, width), F32),
             sd(tokens.shape, BF16),
             sd((groups,) + tokens.shape, BF16),
             sd((groups,) + tokens.shape, BF16),
-            sd((2, planes) + up.shape[1:], BF16),
-            sd((2, planes) + down.shape[1:], BF16),
+            sd((2, planes) + up_half[1:], BF16),
+            sd((2, planes) + down_half[1:], BF16),
         ),
-        in_specs=[any_spec()] * 5 + [vmem_spec()] * 3,
-        out_specs=tuple([vmem_spec()] * 7 + [any_spec()] * 4),
+        in_specs=[smem_spec()] * 2
+        + [vmem_spec()] * (len(routing) + 2)
+        + [any_spec()] * 4,
+        out_specs=tuple(
+            [vmem_spec()] * 7 + [any_spec()] * 6 + [vmem_spec()] + [any_spec()] * 4
+        ),
         scratch_shapes=[
+            pltpu.VMEM(tokens.shape, BF16),
+            pltpu.VMEM((groups, planes * dense.shape[0], dense.shape[1]), BF16),
+            pltpu.VMEM((rows, 3 * width), BF16),
+            pltpu.VMEM((rows, width), BF16),
+            pltpu.VMEM((rows, pair), F32),
+            pltpu.VMEM((rows, width), F32),
             pltpu.VMEM((heads // 2, 2, rows, 2 * pair), BF16),
             pltpu.VMEM((heads // 2, 2, rows, 2 * pair), BF16),
+            pltpu.VMEM(dense.shape, BF16),
+            pltpu.VMEM(up_half, BF16),
+            pltpu.VMEM(down_half, BF16),
+            pltpu.VMEM((PAYLOAD, 128), F32),
+            pltpu.VMEM(tokens.shape, BF16),
+            pltpu.VMEM(tokens.shape, BF16),
+            dma((planes + groups,)),
+            dma((planes + groups,)),
             dma((3 * planes,)),
             dma((3 * planes,)),
             dma((PLANE_GATHER_COPIES,)),
@@ -986,6 +1259,8 @@
             dma((8,)),
             dma((16,)),
             dma((5,)),
+            dma((6,)),
+            dma((3 + 2 * planes,)),
         ],
         compiler_params=pltpu.CompilerParams(
             collective_id=2, has_side_effects=True, vmem_limit_bytes=VMEM_MAX
@@ -994,7 +1269,17 @@
             flops=40_000_000_000, bytes_accessed=10_000_000, transcendentals=8_000_000
         ),
         name="attention_forward",
-    )(tokens, grads, dense, up, down, norms, qf, kf)
+    )(
+        sent_task,
+        task_experts,
+        *routing,
+        tokens,
+        grads,
+        w_qkv,
+        w_proj,
+        up,
+        down.reshape((1,) + down_half),
+    )
 
 
 def split3(values):
@@ -1005,12 +1290,184 @@
     return high, middle, low
 
 
+class GradChain:
+    def __init__(self, src, land, out, stage, temp, sems):
+        self.me, self.z = lax.axis_index("dp"), lax.axis_index("fsdp")
+        self.core = lax.rem(self.me, 2)
+        self.src, self.land, self.out, self.stage, self.temp = src, land, out, stage, temp
+        self.load_sems, self.send_sems, self.recv_sems, self.last_sems = sems
+        self.near = self.z ^ 1
+        self.inner = (self.z == 1) | (self.z == 2)
+        self.outer = jnp.logical_not(self.inner)
+
+    def load(self, kind, plane, k):
+        return pltpu.make_async_copy(
+            self.src[kind].at[plane], self.stage[kind].at[k], self.load_sems.at[kind * 4 + k]
+        )
+
+    def link(self, kind, src, place, plane):
+        return unit_copy(
+            src,
+            self.land[kind].at[place],
+            self.send_sems.at[kind * 5 + place],
+            self.recv_sems.at[kind * 5 + place],
+            (self.me, plane),
+        )
+
+    def loads(self):
+        planes = (3 - self.z, 3 - self.near, self.near)
+        return [self.load(kind, planes[k], k) for kind in range(2) for k in range(3)]
+
+    def outer_sends(self):
+        planes = (3 - self.near, 3 - self.z, self.near)
+        return [
+            self.link(kind, self.src[kind].at[planes[place]], place, self.near)
+            for place in range(3)
+            for kind in range(2)
+        ]
+
+    def start(self):
+        for copy in self.loads():
+            copy.start()
+
+        @pl.when(self.outer)
+        def _():
+            for copy in self.outer_sends():
+                copy.start()
+
+    def gather(self, kind, place, k):
+        self.link(kind, self.land[kind].at[place], place, self.near).wait_recv()
+        fetch = pltpu.make_async_copy(
+            self.land[kind].at[place], self.temp[kind], self.load_sems.at[kind * 4 + 3]
+        )
+        fetch.start()
+        fetch.wait()
+        self.stage[kind][k] = (
+            self.stage[kind][k].astype(F32) + self.temp[kind][...].astype(F32)
+        ).astype(BF16)
+
+    def inner_sends(self, step):
+        place = (3, 4, 3)[step]
+        plane = (3 - self.z, 3 - self.z, self.near)[step]
+        out = []
+        for kind in range(2):
+            copy = pltpu.make_async_remote_copy(
+                src_ref=self.stage[kind].at[step],
+                dst_ref=self.land[kind].at[place],
+                send_sem=self.send_sems.at[kind * 5 + step],
+                recv_sem=self.recv_sems.at[kind * 5 + place],
+                device_id=(self.me, plane),
+                device_id_type=MESH_ID,
+            )
+            out.append(copy)
+        return out
+
+    def step(self, step):
+        @pl.when(self.inner)
+        def _():
+            sends = self.inner_sends(step)
+            for kind in range(2):
+                self.loads()[kind * 3 + step].wait()
+                self.gather(kind, (0, 1, 4)[step], step)
+                sends[kind].start()
+
+    def last_copies(self):
+        out = []
+        chip = self.me - self.core
+        for kind in range(2):
+            out.append(
+                unit_copy(
+                    self.stage[kind].at[0, 1 - self.core],
+                    self.out[kind].at[self.core],
+                    self.last_sems.at[kind],
+                    self.last_sems.at[2 + kind],
+                    (chip + 1 - self.core, self.z),
+                )
+            )
+        return out
+
+    def keep_copies(self):
+        return [
+            pltpu.make_async_copy(
+                self.stage[kind].at[0, self.core],
+                self.out[kind].at[self.core],
+                self.last_sems.at[4 + kind],
+            )
+            for kind in range(2)
+        ]
+
+    def total(self):
+        @pl.when(self.outer)
+        def _():
+            for copy in self.loads():
+                copy.wait()
+            for copy in self.outer_sends():
+                copy.wait_send()
+
+        @pl.when(self.inner)
+        def _():
+            for step in range(3):
+                for copy in self.inner_sends(step):
+                    copy.wait_send()
+
+        own = [self.load(kind, self.z, 0) for kind in range(2)]
+        for copy in own:
+            copy.start()
+        for copy in own:
+            copy.wait()
+
+        @pl.when(self.inner)
+        def _():
+            for kind in range(2):
+                self.gather(kind, 2, 0)
+
+        for kind in range(2):
+            self.gather(kind, 3, 0)
+        for copy in self.last_copies() + self.keep_copies():
+            copy.start()
+
+    def finish(self):
+        for copy in self.last_copies():
+            copy.wait_recv()
+            copy.wait_send()
+        for copy in self.keep_copies():
+            copy.wait()
+
+
 def backward_kernel(
     heads,
     planes,
     groups,
+    row_in,
+    norm_ref,
+    dense_in,
+    qf_in,
+    kf_in,
+    qkv_in,
+    o_in,
+    lse_in,
+    hres_in,
+    g_all,
+    zd_ref,
+    zy_ref,
+    gu_ref,
+    gd_ref,
+    small_ref,
+    gates_ref,
+    out_ref,
+    dtok_ref,
+    dqkv_out,
+    dproj_out,
+    ln_out,
+    gu_in,
+    gd_in,
+    dlogit_out,
+    dbup_out,
+    dbdown_out,
+    norm_out,
+    gu_land,
+    gd_land,
     row_ref,
-    norm_ref,
     dense_ref,
     qf_ref,
     kf_ref,
@@ -1018,18 +1475,6 @@
     o_ref,
     lse_ref,
     hres_ref,
-    g_all,
-    zd_ref,
-    zy_ref,
-    gu_ref,
-    gd_ref,
-    small_ref,
-    out_ref,
-    dtok_ref,
-    shard_ref,
-    gu_in,
-    gd_in,
-    small_out,
     gm,
     kaug,
     vaug,
@@ -1063,6 +1508,12 @@
     w_sum,
     w_in,
     small_in,
+    small_out,
+    norm_part,
+    norm_in,
+    norm_all,
+    n_send,
+    n_recv,
     s_send,
     s_recv,
     d_send,
@@ -1073,9 +1524,16 @@
     w_recv,
     z_send,
     z_recv,
-    u_send,
-    u_recv,
+    gu_stage,
+    gd_stage,
+    gu_temp,
+    gd_temp,
+    c_load,
+    c_send,
+    c_recv,
+    c_last,
     loc_sems,
+    in_sems,
 ):
     me, z = lax.axis_index("dp"), lax.axis_index("fsdp")
     core = lax.rem(me, 2)
@@ -1097,44 +1555,54 @@
         zd_ref, own, d_theirs, d_deep, d_x, d_y, d_sender, loc_sems, z
     )
     next(d_scatter)
-    unit_copies = []
-    for kind, (src, dst) in enumerate(((gu_ref, gu_in), (gd_ref, gd_in))):
-        for t in range(2):
-            for k in range(planes):
-                h, p = (core + t) % 2, lax.rem(z + k, planes)
-                if t == 0 and k == 0:
-                    copy = pltpu.make_async_copy(
-                        src.at[z, core], dst.at[core, z], loc_sems.at[5 + kind]
-                    )
-                    copy.start()
-                else:
-                    i = kind * 8 + t * 4 + k
-                    copy = unit_copy(
-                        src.at[p, h], dst.at[core, z], u_send.at[i], u_recv.at[i], (chip + h, p)
-                    )
-                    copy.start()
-                unit_copies.append(copy)
+    next(d_scatter)
+    pairs = (
+        (hres_in, hres_ref),
+        (o_in, o_ref),
+        (dense_in, dense_ref),
+        (row_in, row_ref),
+        (qf_in, qf_ref),
+        (kf_in, kf_ref),
+        (qkv_in, qkv_ref),
+        (lse_in, lse_ref),
+    )
+    fetched = [pltpu.make_async_copy(a, b, in_sems.at[k]) for k, (a, b) in enumerate(pairs)]
+    for copy in fetched:
+        copy.start()
+    chain = GradChain(
+        (gu_ref, gd_ref),
+        (gu_land, gd_land),
+        (gu_in, gd_in),
+        (gu_stage, gd_stage),
+        (gu_temp, gd_temp),
+        (c_load, c_send, c_recv, c_last),
+    )
+    chain.start()
     for copy in small_z:
         copy.wait_recv()
     small_out[me] = small_ref[...] + jnp.sum(small_in[...], axis=0)
     small_d = [small_sender.start(small_out.at[me], small_out.at[me], p) for p in d_peers]
-    gm_load.wait()
-
-    for _ in range(3):
-        next(d_scatter)
-    dh[...] = next(d_scatter)
     y_sender = Sender(y_send, y_recv)
     y_scatter = plane_scatter_steps(
         zy_ref, own, y_theirs, y_deep, y_x, y_y, y_sender, loc_sems, z
     )
+    next(y_scatter)
+    gm_load.wait()
+    for copy in fetched:
+        copy.wait()
+
+    next(d_scatter)
+    next(d_scatter)
+    chain.step(0)
+    next(d_scatter)
+    dh[...] = next(d_scatter)
     d_sender.drain()
     next(y_scatter)
 
     lane = lax.broadcasted_iota(jnp.int32, (rows, pair), 1)
     lane_c = lax.broadcasted_iota(jnp.int32, (chunk, pair), 1)
-    same = (
-        lax.broadcasted_iota(jnp.int32, (pair, pair), 0) // head
-        == lax.broadcasted_iota(jnp.int32, (pair, pair), 1) // head
+    same = lax.broadcasted_iota(jnp.int32, (width, pair), 0) // head == lax.broadcasted_iota(
+        jnp.int32, (width, pair), 1
     )
     ones = jnp.where(same, 1.0, 0.0).astype(BF16)
     dnorm[...] = jnp.zeros_like(dnorm)
@@ -1149,20 +1617,19 @@
         dh[part, :] = dh_part
         low = dh_part.astype(BF16)
         db[part, :] = low
-        do_part = dot_nt(low, dense_ref[:, :, 3 * width :].reshape(width, width)).astype(BF16)
+        do_part = dot_nt(low, dense_ref[:, :, 3 * width : 4 * width].reshape(width, width)).astype(BF16)
         do[part, :] = do_part
         prod = do_part.astype(F32) * o_ref[part, :].astype(F32)
         high = prod.astype(BF16)
         rest = (prod - high.astype(F32)).astype(BF16)
-        for g in range(heads // 2):
-            cols = slice(g * pair, (g + 1) * pair)
-            delta[part, cols] = dot_nn(high[:, cols], ones) + dot_nn(rest[:, cols], ones)
+        delta[part, :] = dot_nn(high, ones) + dot_nn(rest, ones)
         normal, _ = norm_parts(row_ref[c].astype(F32))
         xn1[part, :] = (normal * norm_ref[0:1, :] + norm_ref[1:2, :]).astype(BF16)
         return carry
 
+    next(y_scatter)
     lax.fori_loop(0, planes, begin, 0)
-    next(y_scatter)
+    chain.step(1)
     w_rows = w_sum.shape[0]
     w_cols = w_sum.shape[1]
     dw[:, :, 3 * width : 4 * width] = (
@@ -1197,14 +1664,14 @@
         def one_chunk(c, inner):
             part = pl.ds(pl.multiple_of(c * chunk, chunk), chunk)
             q_pair, do_pair = qkv_ref[part, cols], do[part, cols]
-            lse_pair, delta_pair = lse_ref[part, cols], delta[part, cols]
+            lse_all, delta_all = lse_ref[part, :], delta[part, :]
             base = qf_ref[part, :].astype(F32)
             acc = jnp.zeros((chunk, pair), F32)
             for side in range(2):
-                lse = lse_pair[:, side * head : side * head + 1]
+                lse = lse_all[:, 2 * g + side : 2 * g + side + 1]
                 qa = jnp.concatenate([q_pair, put_parts(base, lse)], axis=1)
                 pr = jnp.exp(dot_nt(qa, kaug[side]))
-                dlt = delta_pair[:, side * head : side * head + 1]
+                dlt = delta_all[:, 2 * g + side : 2 * g + side + 1]
                 da = jnp.concatenate([do_pair, put_parts(jnp.zeros_like(base), dlt)], axis=1)
                 ds = (pr * dot_nt(da, vaug[side])).astype(BF16)
                 acc = acc + dot_nn(ds, kaug[side, :, :pair])
@@ -1219,35 +1686,37 @@
         dqkv[:, 2 * width + g * pair : 2 * width + (g + 1) * pair] = dvt[...].T.astype(BF16)
 
     out_sender = Sender(z_send, z_recv)
+    next(y_scatter)
     one_pair(0)
-    next(y_scatter)
+    for copy in small_d:
+        copy.wait_recv()
+    dgate = jnp.concatenate(
+        [
+            small_out[2 * (e // 2), e % 2 : e % 2 + 1] + small_out[2 * (e // 2) + 1, e % 2 : e % 2 + 1]
+            for e in range(groups)
+        ]
+    )
+    gates = gates_ref[...]
+    dlogit_out[...] = gates * (dgate - jnp.sum(gates * dgate, axis=0, keepdims=True))
+    up_part, up_rows = dbup_out.shape[1] // 256, gu_ref.shape[3] // 128
+    for h in range(2):
+        for q in range(up_part):
+            at = 2 + core * up_rows + z * up_part + q
+            spot = (h * up_part + q) * 128
+            dbup_out[:, spot : spot + 128] = small_out[chip + h, pl.ds(at, 1), :]
+    dbdown_out[...] = small_out[me, pl.ds(2 + 2 * up_rows + core * (width // 128) + z, 1), :]
+    chain.step(2)
     one_pair(1)
     next(y_scatter)
-    one_pair(2)
     mixed = hres_ref[...] + next(y_scatter)
     moved[0] = mixed.astype(BF16).reshape(planes, chunk, width)
     out_keep = pltpu.make_async_copy(moved.at[0, z], out_ref.at[z], loc_sems.at[7])
     out_keep.start()
     sent = [out_sender.start(moved.at[0, p[1]], out_ref.at[z], p) for p in z_peers]
+    one_pair(2)
+    chain.total()
     one_pair(3)
 
-    def finish(c, carry):
-        part = pl.ds(pl.multiple_of(c * chunk, chunk), chunk)
-        grad = dot_nt(
-            dqkv[part, :], dense_ref[:, :, : 3 * width].reshape(width, 3 * width)
-        )
-        normal, scale = norm_parts(row_ref[c].astype(F32))
-        dnorm[0] += fold_rows(grad * normal)
-        dnorm[1] += fold_rows(grad)
-        moved[1, c] = (
-            dh[part, :] + norm_back_parts(grad * norm_ref[0:1, :], normal, scale)
-        ).astype(BF16)
-        return carry
-
-    lax.fori_loop(0, planes, finish, 0)
-    tok_keep = pltpu.make_async_copy(moved.at[1, z], dtok_ref.at[z], loc_sems.at[8])
-    tok_keep.start()
-    sent += [out_sender.start(moved.at[1, p[1]], dtok_ref.at[z], p) for p in z_peers]
     for c in range(3):
         cols = slice(c * width, (c + 1) * width)
         dw[:, :, cols] = (
@@ -1255,7 +1724,7 @@
         )
     lanes = lax.broadcasted_iota(jnp.int32, (8, width), 0)
     table = jnp.zeros((8, width), F32)
-    for k in range(4):
+    for k in range(2, 4):
         table = jnp.where(lanes == k, jnp.sum(dnorm[k], axis=0, keepdims=True), table)
     table = jnp.concatenate([table, jnp.zeros((w_cols - 4 * width - 8, width), F32)], axis=0)
     dw[:, :, 4 * width :] = table.T.astype(BF16).reshape(groups, w_rows, w_cols - 4 * width)
@@ -1263,30 +1732,59 @@
     w_scatter = plane_scatter_steps(
         dw, w_own, w_theirs, w_deep, w_x, w_y, w_sender, loc_sems, z
     )
-    for _ in range(4):
+    next(w_scatter)
+    next(w_scatter)
+
+    def finish(c):
+        part = pl.ds(pl.multiple_of(c * chunk, chunk), chunk)
+        grad = dot_nt(dqkv[part, :], dense_ref[:, :, : 3 * width].reshape(width, 3 * width))
+        normal, scale = norm_parts(row_ref[c].astype(F32))
+        dnorm[0] += fold_rows(grad * normal)
+        dnorm[1] += fold_rows(grad)
+        moved[1, c] = (
+            dh[part, :] + norm_back_parts(grad * norm_ref[0:1, :], normal, scale)
+        ).astype(BF16)
+
+    for k, peer in enumerate(z_peers):
+        finish(peer[1])
+        sent.append(out_sender.start(moved.at[1, peer[1]], dtok_ref.at[z], peer))
         next(w_scatter)
+    finish(z)
+    tok_keep = pltpu.make_async_copy(moved.at[1, z], dtok_ref.at[z], loc_sems.at[8])
+    tok_keep.start()
+    for k in range(2):
+        total = jnp.sum(dnorm[k], axis=0, keepdims=True)
+        for q in range(width // 128):
+            row = k * (width // 128) + q
+            norm_part[row : row + 1] = total[:, q * 128 : (q + 1) * 128]
+    norm_sender = Sender(n_send, n_recv)
+    norm_z = [norm_sender.start(norm_part, norm_in.at[k], p) for k, p in enumerate(z_peers)]
     w_sum[...] = next(w_scatter).astype(BF16)
-    shard = shard_ref.shape[0]
+    shard = dqkv_out.shape[0]
     last = [
         out_sender.start(w_sum.at[pl.ds(p[1] * shard, shard)], w_in.at[k], p)
         for k, p in enumerate(z_peers)
     ]
+    for copy in norm_z:
+        copy.wait_recv()
+    norm_all[me] = norm_part[...] + jnp.sum(norm_in[...], axis=0)
+    norm_d = [norm_sender.start(norm_all.at[me], norm_all.at[me], p) for p in d_peers]
     total = w_sum[pl.ds(z * shard, shard)].astype(F32)
     for k, copy in enumerate(last):
         copy.wait_recv()
         total = total + w_in[k].astype(F32)
-    shard_ref[...] = total
-    for copy in sent + small_d:
+    dqkv_out[...] = total[:, : 3 * width]
+    dproj_out[...] = total[:, 3 * width : 4 * width]
+    ln_out[...] = total[:, 4 * width :]
+    for copy in norm_d:
         copy.wait_recv()
-    for i, copy in enumerate(unit_copies):
-        if i % 8 == 0:
-            copy.wait()
-        else:
-            copy.wait_recv()
-            copy.wait_send()
+    norm_out[...] = jnp.sum(norm_all[...], axis=0)
+    for copy in sent:
+        copy.wait_recv()
+    chain.finish()
     out_keep.wait()
     tok_keep.wait()
-    for sender in (small_sender, y_sender, w_sender, out_sender):
+    for sender in (small_sender, y_sender, w_sender, out_sender, norm_sender):
         sender.drain()
 
 
@@ -1299,7 +1797,9 @@
     ]
 
 
-def backward(row, norms, dense, qf, kf, qkv, o, lse, hres, g_all, zd, zy, gu, gd, small, heads):
+def backward(
+    row, norms, dense, qf, kf, qkv, o, lse, hres, g_all, zd, zy, gu, gd, small, gates, heads
+):
     planes, piece, width = row.shape
     groups = zd.shape[0]
     rows = planes * piece
@@ -1312,21 +1812,35 @@
         out_shape=(
             sd(row.shape, BF16),
             sd(row.shape, BF16),
-            sd((w_rows // planes, w_cols), F32),
-            sd((2, planes) + gu.shape[2:], BF16),
-            sd((2, planes) + gd.shape[2:], BF16),
-            sd((groups,) + small.shape, F32),
+            sd((w_rows // planes, 3 * width), F32),
+            sd((w_rows // planes, width), F32),
+            sd((w_rows // planes, 128), F32),
+            sd((2,) + gu.shape[2:], BF16),
+            sd((2,) + gd.shape[2:], BF16),
+            sd((groups, 128), F32),
+            sd((1, 2 * gu.shape[3] // planes), F32),
+            sd((1, width // planes), F32),
+            sd((2 * width // 128, 128), F32),
+            sd((5,) + gu.shape[1:], BF16),
+            sd((5,) + gd.shape[1:], BF16),
         ),
-        in_specs=[vmem_spec()] * 9 + [any_spec()] * 5 + [vmem_spec()],
-        out_specs=(any_spec(), any_spec(), vmem_spec(), any_spec(), any_spec(), vmem_spec()),
-        scratch_shapes=[
+        in_specs=[any_spec(), vmem_spec()] + [any_spec()] * 12 + [vmem_spec()] * 2,
+        out_specs=tuple(
+            [any_spec()] * 2
+            + [vmem_spec()] * 3
+            + [any_spec()] * 2
+            + [vmem_spec()] * 4
+            + [any_spec()] * 2
+        ),
+        scratch_shapes=[pltpu.VMEM(a.shape, a.dtype) for a in (row, dense, qf, kf, qkv, o, lse, hres)]
+        + [
             pltpu.VMEM(row.shape, BF16),
             pltpu.VMEM((2, rows, 2 * pair), BF16),
             pltpu.VMEM((2, rows, 2 * pair), BF16),
             pltpu.VMEM((rows, width), F32),
             pltpu.VMEM((rows, width), BF16),
             pltpu.VMEM((rows, width), BF16),
-            pltpu.VMEM((rows, width), F32),
+            pltpu.VMEM((rows, pair), F32),
             pltpu.VMEM((pair, rows), BF16),
             pltpu.VMEM((pair, rows), BF16),
             pltpu.VMEM((pair, rows), F32),
@@ -1346,6 +1860,12 @@
             pltpu.VMEM((w_rows, w_cols), BF16),
             pltpu.VMEM((planes - 1, w_rows // planes, w_cols), BF16),
             pltpu.VMEM((planes - 1,) + small.shape, F32),
+            pltpu.VMEM((groups,) + small.shape, F32),
+            pltpu.VMEM((2 * width // 128, 128), F32),
+            pltpu.VMEM((planes - 1, 2 * width // 128, 128), F32),
+            pltpu.VMEM((groups, 2 * width // 128, 128), F32),
+            dma((planes + groups,)),
+            dma((planes + groups,)),
             dma((planes + groups,)),
             dma((planes + groups,)),
             dma((PLANE_SCATTER_COPIES,)),
@@ -1356,9 +1876,16 @@
             dma((PLANE_SCATTER_COPIES,)),
             dma((3 * planes,)),
             dma((3 * planes,)),
-            dma((16,)),
-            dma((16,)),
+            pltpu.VMEM((3,) + gu.shape[1:], BF16),
+            pltpu.VMEM((3,) + gd.shape[1:], BF16),
+            pltpu.VMEM(gu.shape[1:], BF16),
+            pltpu.VMEM(gd.shape[1:], BF16),
+            dma((8,)),
+            dma((10,)),
+            dma((10,)),
+            dma((6,)),
             dma((9,)),
+            dma((8,)),
         ],
         compiler_params=pltpu.CompilerParams(
             collective_id=4, has_side_effects=True, vmem_limit_bytes=VMEM_MAX
@@ -1367,23 +1894,61 @@
             flops=80_000_000_000, bytes_accessed=20_000_000, transcendentals=8_000_000
         ),
         name="attention_backward",
-    )(row, norms, dense, qf, kf, qkv, o, lse, hres, g_all, zd, zy, gu, gd, small)
+    )(row, norms, dense, qf, kf, qkv, o, lse, hres, g_all, zd, zy, gu, gd, small, gates)
+
+
+def make_tile_list(marks, list_ref):
+    blocks, piece = marks.shape
+    per = piece // TILE
+    iota = functools.partial(lax.broadcasted_iota, jnp.int32)
+
+    def table(mask):
+        return jnp.where(mask, 1.0, 0.0).astype(BF16)
+
+    kept = table(marks >= 0.0)
+    folded = dot_nn(kept, table(iota((piece, 128), 0) // TILE == iota((piece, 128), 1)))
+    real = iota((blocks, 128), 1) < per
+    hit = jnp.where(folded > 0.0, 1.0, 0.0)
+    inside = dot_nn(hit.astype(BF16), table(iota((128, 128), 0) < iota((128, 128), 1)))
+    totals = jnp.broadcast_to(jnp.sum(hit, axis=1, keepdims=True), (blocks, 128))
+    above = dot_nn(table(iota((blocks, blocks), 1) < iota((blocks, blocks), 0)), totals.astype(BF16))
+    count = jnp.sum(hit)
+    rank = inside + above
+    index = iota((blocks, 128), 0) * per + iota((blocks, 128), 1)
+    place = jnp.where(hit > 0.0, rank, count + index.astype(F32) - rank)
+    place = jnp.where(real, place, 0.0).astype(jnp.int32)
+    tiles = blocks * per
+    row = iota((tiles, 128), 0)
+    spread = table(iota((tiles, blocks), 0) // per == iota((tiles, blocks), 1))
+    mine = lax.rem(row, per) == iota((tiles, 128), 1)
+    digits = []
+    for digit in (place // per, lax.rem(place, per)):
+        full = dot_nn(spread, digit.astype(F32).astype(BF16))
+        digits.append(jnp.sum(jnp.where(mine, full, 0.0), axis=1, keepdims=True).astype(jnp.int32))
+    to_row = table(digits[0] == iota((tiles, blocks), 1))
+    to_column = digits[1] == iota((tiles, 128), 1)
+    found = jnp.zeros((blocks, 128), F32)
+    for value, scale in ((row // per, per), (lax.rem(row, per), 1)):
+        part = jnp.where(to_column, value.astype(F32), 0.0).astype(BF16)
+        found = found + scale * dot_tn(to_row, part)
+    found = jnp.where(iota((blocks, 128), 1) == per, count, found)
+    list_ref[...] = found.astype(jnp.int32)
 
 
 def expert_kernel(
-    list_ref,
-    meta_ref,
+    marks_ref,
+    gates_ref,
+    codes_ref,
     own_ref,
     x_ref,
     g_ref,
     up_ref,
     down_ref,
-    bup_ref,
-    bdown_ref,
     zd_ref,
     zy_ref,
     gu_ref,
     gd_ref,
+    small_ref,
     dbup_ref,
     dbdown_ref,
     dgate_ref,
@@ -1403,7 +1968,15 @@
     dyt,
     yacc,
     xacc,
+    meta,
+    bup,
+    bdown,
+    list_vmem,
+    list_ref,
+    list_sem,
     sems,
+    upt,
+    downt,
 ):
     me = lax.axis_index("dp")
     groups, rows, width = x_ref.shape
@@ -1434,6 +2007,29 @@
     dbup_ref[...] = jnp.zeros_like(dbup_ref)
     dbdown_ref[...] = jnp.zeros_like(dbdown_ref)
     dgate_ref[...] = jnp.zeros_like(dgate_ref)
+    core = lax.rem(me, 2)
+    piece = marks_ref.shape[2]
+    blocks = marks_ref.shape[1]
+    lane = lax.broadcasted_iota(jnp.int32, (piece, 128), 1)
+    turned = [marks_ref[e].T for e in range(2)]
+    for k in range(blocks):
+        meta[k * piece : (k + 1) * piece, :] = jnp.where(
+            lane == 0, turned[0][:, k : k + 1], turned[1][:, k : k + 1]
+        )
+    for e in range(2):
+        for p in range(planes):
+            for q in range(2):
+                at = p * (hidden // planes) + q * 128
+                bup[e, :, at : at + 128] = codes_ref[
+                    me - core + e, p, pl.ds(BIAS_UP + 2 * core + q, 1), :
+                ]
+            bdown[e, :, p * 128 : (p + 1) * 128] = jnp.where(
+                core == 0, codes_ref[me - core + e, p, BIAS_DOWN : BIAS_DOWN + 1, :], 0.0
+            )
+        make_tile_list(marks_ref[e], list_vmem.at[e])
+    list_copy = pltpu.make_async_copy(list_vmem, list_ref, list_sem)
+    list_copy.start()
+    list_copy.wait()
     for copy in copies:
         copy.wait()
 
@@ -1452,20 +2048,25 @@
     def one_expert(e):
         acc_up[...] = jnp.zeros_like(acc_up)
         acc_down[...] = jnp.zeros_like(acc_down)
-        n_blocks = lax.div(list_ref[e, 0] + (tiles - 1), tiles)
+        upt[...] = up[e].T
+        downt[...] = down[e].T
+        n_blocks = lax.div(list_ref[e, 0, 16] + (tiles - 1), tiles)
+        gate_row = gates_ref[pl.ds(me - core + e, 1), :]
+        lane_b = lax.broadcasted_iota(jnp.int32, (BLOCK, 128), 1).astype(F32)
 
         def one_block(b, carry):
             def fetch(k, inner):
-                index = list_ref[e, 1 + b * tiles + k]
+                index = list_ref[e, b * (tiles // 16) + lax.div(k, 16), lax.rem(k, 16)]
                 src, part = lax.div(index, per_row), spot(lax.rem(index, per_row))
                 dst = spot(k)
                 xb[dst, :] = xs[src, part, :]
                 gb[dst, :] = gs[src, part, :]
-                mb[dst, :] = meta_ref[spot(index), :]
+                mb[dst, :] = meta[spot(index), :]
                 return inner
 
-            lax.fori_loop(0, tiles, fetch, 0, unroll=4)
-            gate = mb[:, 2 * e : 2 * e + 1]
+            lax.fori_loop(0, tiles, fetch, 0, unroll=True)
+            hot = lane_b == mb[:, e : e + 1]
+            gate = jnp.sum(jnp.where(hot, gate_row, 0.0), axis=1, keepdims=True)
             dyb_new = (gb[...].astype(F32) * gate).astype(BF16)
             dyb[...] = dyb_new
             xt[...] = xb[...].T
@@ -1474,7 +2075,7 @@
 
             def one_chunk(f, inner):
                 cols = pl.ds(pl.multiple_of(f * FCHUNK, FCHUNK), FCHUNK)
-                u = dot_nn(xb[...], up[e, :, cols]) + bup_ref[e, :, cols]
+                u = dot_nn(xb[...], up[e, :, cols]) + bup[e, :, cols]
                 sq = u * u
                 th = jnp.tanh(u * (0.7978845608028654 + 0.035677408136300125 * sq))
                 half = 0.5 + 0.5 * th
@@ -1482,9 +2083,9 @@
                     (0.5 - 0.5 * th * th) * (0.7978845608028654 + 0.10703222440890037 * sq)
                 )
                 a = (u * half).astype(BF16)
-                du = (dot_nt(dyb[...], down[e, cols, :]) * slope).astype(BF16)
+                du = (dot_nn(dyb[...], downt[:, cols]) * slope).astype(BF16)
                 y_new = dot_nn(a, down[e, cols, :])
-                x_new = dot_nt(du, up[e, :, cols])
+                x_new = dot_nn(du, upt[cols, :])
 
                 @pl.when(f == 0)
                 def _():
@@ -1502,15 +2103,14 @@
                 return inner
 
             lax.fori_loop(0, hidden // FCHUNK, one_chunk, 0)
-            y = yacc[...] + bdown_ref[e]
+            y = yacc[...] + bdown[e]
             inner_prod = jnp.sum(y * gb[...].astype(F32), axis=-1, keepdims=True)
-            lane = lax.broadcasted_iota(jnp.int32, (BLOCK, 128), 1).astype(F32)
-            dgate_ref[e] += fold_rows(jnp.where(lane == mb[:, 2 * e + 1 : 2 * e + 2], inner_prod, 0.0))
+            dgate_ref[e] += fold_rows(jnp.where(hot, inner_prod, 0.0))
             gb[...] = (y * gate).astype(BF16)
             xb[...] = xacc[...].astype(BF16)
 
             def store(k, inner):
-                dst = spot(list_ref[e, 1 + b * tiles + k])
+                dst = spot(list_ref[e, b * (tiles // 16) + lax.div(k, 16), lax.rem(k, 16)])
                 src = spot(k)
                 if e == 0:
                     zds[dst, :] = xb[src, :]
@@ -1520,7 +2120,7 @@
                     zys[dst, :] = (zys[dst, :].astype(F32) + gb[src, :].astype(F32)).astype(BF16)
                 return inner
 
-            lax.fori_loop(0, tiles, store, 0, unroll=4)
+            lax.fori_loop(0, tiles, store, 0, unroll=True)
             return carry
 
         lax.fori_loop(0, n_blocks, one_block, 0)
@@ -1537,11 +2137,22 @@
     one_expert(1)
     save(zds, zd_ref)
     save(zys, zy_ref)
+    small_ref[...] = jnp.zeros_like(small_ref)
+    up_rows, down_rows = hidden // 128, width // 128
+    for e in range(2):
+        small_ref[e : e + 1] = jnp.sum(dgate_ref[e], axis=0, keepdims=True)
+        for at, acc, count in (
+            (2 + e * up_rows, dbup_ref, up_rows),
+            (2 + 2 * up_rows + e * down_rows, dbdown_ref, down_rows),
+        ):
+            sums = jnp.sum(acc[e], axis=0, keepdims=True)
+            for k in range(count):
+                small_ref[at + k : at + k + 1] = sums[:, k * 128 : (k + 1) * 128]
     for copy in saves:
         copy.wait()
 
 
-def experts(tile_list, meta, x_own, x_all, g_all, up, down, b_up, b_down):
+def experts(marks, gates, codes, x_own, x_all, g_all, up, down):
     groups, rows, width = x_all.shape
     hidden = up.shape[2]
     planes = 4
@@ -1554,13 +2165,14 @@
             sd((total, width), BF16),
             sd((planes, 2, width // planes, hidden), BF16),
             sd((planes, 2, hidden // planes, width), BF16),
-            sd((2, 8, hidden), F32),
-            sd((2, 8, width), F32),
-            sd((2, 8, 128), F32),
+            sd((-(-(2 + 2 * (hidden + width) // 128) // 8) * 8, 128), F32),
         ),
-        in_specs=[smem_spec(), vmem_spec()] + [any_spec()] * 5 + [vmem_spec()] * 2,
-        out_specs=tuple([any_spec()] * 4 + [vmem_spec()] * 3),
+        in_specs=[vmem_spec()] * 3 + [any_spec()] * 5,
+        out_specs=tuple([any_spec()] * 4 + [vmem_spec()]),
         scratch_shapes=[
+            pltpu.VMEM((2, 8, hidden), F32),
+            pltpu.VMEM((2, 8, width), F32),
+            pltpu.VMEM((2, 8, 128), F32),
             pltpu.VMEM((groups, rows, width), BF16),
             pltpu.VMEM((groups, rows, width), BF16),
             pltpu.VMEM((total, width), BF16),
@@ -1577,14 +2189,22 @@
             pltpu.VMEM((width, BLOCK), BF16),
             pltpu.VMEM((BLOCK, width), F32),
             pltpu.VMEM((BLOCK, width), F32),
+            pltpu.VMEM((total, 128), F32),
+            pltpu.VMEM((2, 1, hidden), F32),
+            pltpu.VMEM((2, 1, width), F32),
+            pltpu.VMEM((2, marks.shape[1], 128), jnp.int32),
+            pltpu.SMEM((2, marks.shape[1], 128), jnp.int32),
+            pltpu.SemaphoreType.DMA,
             pltpu.SemaphoreType.DMA((40,)),
+            pltpu.VMEM((hidden, width), BF16),
+            pltpu.VMEM((width, hidden), BF16),
         ],
         compiler_params=pltpu.CompilerParams(vmem_limit_bytes=VMEM_MAX),
         cost_estimate=pl.CostEstimate(
             flops=60_000_000_000, bytes_accessed=40_000_000, transcendentals=8_000_000
         ),
         name="experts",
-    )(tile_list, meta, x_own, x_all, g_all, up, down, b_up, b_down)
+    )(marks, gates, codes, x_own, x_all, g_all, up, down)
 
 
 def fast_shards(
@@ -1618,138 +2238,70 @@
     capacity = 4 * row_count * piece // n_experts
     me, z = lax.axis_index("dp"), lax.axis_index("fsdp")
 
-    seg_hot = segment_ids[:, :, None] == jnp.arange(sent_task.shape[1])[None, None, :]
-    task_tok = jnp.sum(jnp.where(seg_hot, sent_task[:, None, :], 0), axis=-1)
-    code = (task_tok * 16 + segment_ids * 2 + key_mask).astype(F32)
-    logits_part = jnp.dot(task_embed.astype(F32), w_gate.astype(F32), precision=exact)
-    norm_part = jnp.stack([ln1_gain, ln1_bias, ln2_gain, ln2_bias]).astype(F32)
-    bias_part = jnp.concatenate([b_up[0], b_down[0]]).astype(F32)
-    parts = [code.reshape(-1), logits_part.reshape(-1), norm_part.reshape(-1), bias_part]
-    used = sum(p.shape[0] for p in parts)
-    pad_rows = -(-used // 1024) * 8
-    payload = jnp.concatenate(parts + [jnp.zeros((pad_rows * 128 - used,), F32)])
-    gathered = small_gather(payload.reshape(pad_rows, 128), planes, groups)
-    gathered = gathered.reshape(groups, planes, pad_rows * 128)
-    ends = []
-    at = 0
-    for p in parts:
-        ends.append((at, at + p.shape[0]))
-        at += p.shape[0]
-    codes = gathered[:, :, ends[0][0] : ends[0][1]].astype(jnp.int32)
-    codes = codes.reshape(groups, planes, row_count, piece)
-    logits_all = jnp.sum(gathered[:, :, ends[1][0] : ends[1][1]], axis=(0, 1))
-    logits_all = logits_all.reshape(tasks, n_experts)
-    norms = gathered[:, :, ends[2][0] : ends[2][1]].reshape(groups * planes, 4, -1)
-    norms = norms.transpose(1, 0, 2).reshape(4, width)
-    norms = jnp.concatenate([norms, jnp.zeros((4, width), F32)])
     core = me % 2
-    biases = lax.dynamic_slice_in_dim(
-        gathered[:, :, ends[3][0] : ends[3][1]], me - core, 2, 0
-    )
     half = hidden // 2
-    bias_up = biases[:, :, : b_up.shape[1]].reshape(2, planes, 2, half // planes)
-    bias_up = lax.dynamic_index_in_dim(bias_up, core, 2, keepdims=False).reshape(2, 1, half)
-    bias_down = biases[:, :, b_up.shape[1] :].reshape(2, 1, width)
-    bias_down = jnp.where(core == 0, bias_down, 0.0)
-
-    seg_first = codes[:, 0, :, 0] % 16 // 2
-    seg_last = codes[:, planes - 1, :, piece - 1] % 16 // 2
-    single = jnp.argmax((seg_first == seg_last).astype(jnp.int32), axis=1)
-    target = jnp.arange(groups) % planes
-    slots = jnp.arange(planes)[None, :]
-    order = jnp.where(
-        slots == target[:, None],
-        single[:, None],
-        jnp.where(slots == single[:, None], target[:, None], slots),
-    ).astype(jnp.int32)
-    my_order = lax.dynamic_index_in_dim(order, me, 0, keepdims=False)
-    row_of = lax.dynamic_index_in_dim(order, z, 1, keepdims=False)
-
-    tokens_out, grads_out = pick_rows(my_order, (tokens, out_grad), (BF16, BF16))
-    dense = jnp.concatenate([w_qkv, w_proj], axis=1)
-    my_codes = lax.dynamic_index_in_dim(codes, me, 0, keepdims=False)
-    my_code = lax.dynamic_index_in_dim(my_codes, row_of[me], 1, keepdims=False).reshape(length)
-    my_seg, my_key = my_code % 16 // 2, my_code % 2
-    pair = 2 * HD
-    feature = jnp.arange(pair)[None, :]
-    hot = my_seg[:, None] == feature
-    qf = hot.astype(BF16)
-    kf = jnp.where((feature < 8) & ~(hot & (my_key[:, None] == 1)), FAR, 0.0).astype(BF16)
-
-    up_halves = w_up[0].reshape(-1, planes, 2, half // planes).transpose(2, 0, 1, 3)
-    up_halves = up_halves.reshape(2, -1, half)
-    down_halves = w_down[0].reshape(2, -1, width)
-    (row, dense_full, qkv, o, lse, hres, xn2, x_all, g_all, up_all, down_all) = forward(
-        tokens_out, grads_out, dense, up_halves, down_halves, norms, qf, kf, HEADS, groups
-    )
-
-    choose = (task_experts[:, :, None] == jnp.arange(n_experts)[None, None, :]).astype(F32)
-
-    def gate_values(logits):
-        return jax.nn.softmax(jnp.sum(logits[:, None, :] * choose, axis=-1), axis=-1)
-
-    gates, gate_back = jax.vjp(gate_values, logits_all)
-    chip_experts = me - core + jnp.arange(2)
-    mine = task_experts[None] == chip_experts[:, None, None]
-    shifts = jnp.left_shift(1, jnp.arange(tasks, dtype=jnp.int32))
-    bits = jnp.sum(jnp.where(mine, shifts[None, :, None], 0), axis=1)
-    gate_of_task = jnp.sum(jnp.where(mine, gates[None], 0.0), axis=2)
-    task_all = codes // 16
-    hits = jnp.right_shift(bits[:, None, None, :, None, None], task_all[None, :, :, None]) & 1
-    hits = hits.astype(F32)
-    lower = (jnp.arange(piece)[:, None] < jnp.arange(piece)[None, :]).astype(BF16)
-    before = jnp.dot(
-        hits.reshape(-1, piece).astype(BF16), lower, preferred_element_type=F32
-    ).reshape(hits.shape)
-    counts = jnp.sum(hits, axis=-1).reshape(2, groups, planes, 2 * row_count)
-    ahead = (jnp.cumsum(counts, axis=-1) - counts).reshape(2, groups, planes, 2, row_count)
-    rank = before + ahead[..., None]
-    kept = jnp.sum(jnp.where(rank < capacity, hits, 0.0), axis=3)
-    here = (jnp.arange(row_count)[None, :] == row_of[:, None])[:, None, :, None]
-    kept_here = jnp.sum(jnp.where(here[None], kept, 0.0), axis=3).reshape(2, total)
-    task_here = jnp.sum(jnp.where(here, task_all, 0), axis=2).reshape(total)
-    task_hot = task_here[:, None] == jnp.arange(tasks)[None, :]
-    gate_here = jnp.sum(jnp.where(task_hot[None], gate_of_task[:, None, :], 0.0), axis=2)
-    gate_here = gate_here * kept_here
-    task_mark = jnp.where(kept_here > 0, task_here.astype(F32)[None], -1.0)
-    lane = jnp.arange(128)[None, :]
-    meta = jnp.zeros((total, 128), F32)
-    for k in range(2):
-        meta = jnp.where(lane == 2 * k, gate_here[k][:, None], meta)
-        meta = jnp.where(lane == 2 * k + 1, task_mark[k][:, None], meta)
-    n_tiles = total // TILE
-    tile_hit = jnp.max(kept_here.reshape(2, n_tiles, TILE), axis=2) > 0
-    hit_rank = jnp.cumsum(tile_hit.astype(jnp.int32), axis=1)
-    hit_count = hit_rank[:, -1:]
-    index = jnp.arange(n_tiles, dtype=jnp.int32)
-    place = jnp.where(tile_hit, hit_rank - 1, hit_count + index[None] - hit_rank)
-    tile_list = jnp.sum(
-        jnp.where(place[:, None, :] == index[None, :, None], index[None, None, :], 0),
-        axis=2,
-        dtype=jnp.int32,
-    )
-    tile_list = jnp.concatenate([hit_count, tile_list], axis=1)
-
-    zd, zy, gu, gd, dbup, dbdown, dgate = experts(
-        tile_list,
-        meta,
+    shard_norms = jnp.concatenate([ln1_gain, ln1_bias, ln2_gain, ln2_bias]).astype(F32)
+    shard_norms = jnp.pad(shard_norms, (0, 128 - shard_norms.shape[0])).reshape(1, 128)
+    logits_part = jnp.dot(task_embed, w_gate, preferred_element_type=F32)
+    routing = (segment_ids, key_mask, logits_part, shard_norms, b_up, b_down)
+    (
+        codes,
+        marks,
+        gates_rows,
+        order,
+        norms,
+        qf,
+        kf,
+        row,
+        dense_full,
+        qkv,
+        o,
+        lse,
+        hres,
+        xn2,
+        x_all,
+        g_all,
+        up_all,
+        down_all,
+    ) = forward(
+        sent_task,
+        task_experts,
+        routing,
+        tokens,
+        out_grad,
+        w_qkv,
+        w_proj,
+        w_up,
+        w_down,
+        HEADS,
+        groups,
+        capacity,
+    )
+    zd, zy, gu, gd, small = experts(
+        marks,
+        gates_rows,
+        codes,
         xn2.reshape(length, width),
         x_all.reshape(groups, length, width),
         g_all.reshape(groups, length, width),
         up_all.reshape(2, width, half),
         down_all.reshape(2, half, width),
-        bias_up,
-        bias_down,
-    )
-    small = jnp.concatenate(
-        [
-            jnp.sum(dgate, axis=1),
-            jnp.sum(dbup, axis=1).reshape(-1, 128),
-            jnp.sum(dbdown, axis=1).reshape(-1, 128),
-        ]
-    )
-    small = jnp.concatenate([small, jnp.zeros((-small.shape[0] % 8, 128), F32)])
-    out_pieces, tok_pieces, shard, gu_in, gd_in, small_all = backward(
+    )
+    (
+        out_pieces,
+        tok_pieces,
+        d_w_qkv,
+        d_w_proj,
+        d_ln2,
+        gu_in,
+        gd_in,
+        dlogits,
+        d_b_up,
+        d_b_down,
+        norm_sums,
+        _,
+        _,
+    ) = backward(
         row,
         norms,
         dense_full,
@@ -1765,47 +2317,37 @@
         gu,
         gd,
         small,
+        gates_rows,
         HEADS,
     )
-    d_w_up = jnp.sum(gu_in.astype(F32), axis=1).reshape(2, -1, planes, half // planes)
+    d_w_up = gu_in.astype(F32).reshape(2, -1, planes, half // planes)
     d_w_up = d_w_up.transpose(1, 2, 0, 3).reshape(-1, hidden)
-    d_w_down = jnp.sum(gd_in.astype(F32), axis=1).reshape(-1, width)
-    output, d_tokens = pick_rows(my_order, (out_pieces, tok_pieces), (BF16, F32))
-
-    chips = small_all.reshape(groups // 2, 2, -1, 128)
-    dgate_all = jnp.sum(chips[:, :, :2, :tasks], axis=1).reshape(n_experts, tasks).T
-    dgates = jnp.sum(dgate_all[:, None, :] * choose, axis=-1)
-    (dlogits,) = gate_back(dgates)
-    d_task_embed = jnp.dot(dlogits, w_gate.astype(F32).T, precision=exact)
-    d_w_gate = jnp.dot(task_embed.astype(F32).T, dlogits, precision=exact)
-    my_chip = lax.dynamic_index_in_dim(chips, me // 2, 0, keepdims=False)
-    cut = 2 + 2 * half // 128
-    d_b_up = lax.dynamic_index_in_dim(
-        my_chip[:, 2:cut].reshape(2, 2, planes, half // planes), core, 1, keepdims=False
-    )
-    d_b_up = lax.dynamic_index_in_dim(d_b_up, z, 1, keepdims=False).reshape(hidden // planes)
-    d_b_down = lax.dynamic_index_in_dim(
-        my_chip[0, cut : cut + 2 * width // 128].reshape(2, planes, width // planes),
-        core,
-        0,
-        keepdims=False,
-    )
-    d_b_down = lax.dynamic_index_in_dim(d_b_down, z, 0, keepdims=False)
+    d_w_down = gd_in.astype(F32).reshape(-1, width)
+    output, d_tokens = pick_rows(order, (out_pieces, tok_pieces), (BF16, F32))
+
+    features = width // (groups * planes)
+    d_ln1 = lax.dynamic_slice_in_dim(
+        norm_sums.reshape(2, width), (me * planes + z) * features, features, 1
+    )
+
+    dlogits = dlogits[:, :tasks]
+    d_task_embed = jnp.dot(dlogits.T, w_gate.astype(F32).T, precision=exact)
+    d_w_gate = jnp.dot(task_embed.astype(F32).T, dlogits.T, precision=exact)
     return (
         output,
         d_tokens,
-        shard[:, 4 * width],
-        shard[:, 4 * width + 1],
-        shard[:, : 3 * width],
-        shard[:, 3 * width : 4 * width],
-        shard[:, 4 * width + 2],
-        shard[:, 4 * width + 3],
+        d_ln1[0],
+        d_ln1[1],
+        d_w_qkv,
+        d_w_proj,
+        d_ln2[:, 2],
+        d_ln2[:, 3],
         d_task_embed,
         d_w_gate,
         d_w_up[None],
-        d_b_up[None],
+        d_b_up,
         d_w_down[None],
-        d_b_down[None],
+        d_b_down,
     )
 
 
@@ -1814,6 +2356,7 @@
     return (
         groups == 8
         and planes == 4
+        and tokens.shape[1] == planes * 256
         and tokens.shape[0] == groups * planes
         and w_gate.shape[1] == groups
         and tokens.shape[1] % (planes * QCHUNK) == 0

time: 501 us -> 406 us (0.81); the launches traced: 508 us -> 408 us
  Pallas kernels: 458 us -> 389 us
  other arithmetic: 26.7 us -> 2.39 us
  local copies, waits for them, and re-layouts: 16.9 us -> 10.7 us
    pallas_call x1, Pallas kernels: 99 us -> 40.7 us  [experts(): pl.pallas_call(expert_kernel, out_shape=(sd((total, width), BF16), sd((to...]
    pallas_call x2 -> x1, Pallas kernels: 158 us -> 141 us  [forward(): pl.pallas_call(functools.partial(forward_kernel, heads, planes, capacity)...]
    pallas_call x1, Pallas kernels: 192 us -> 204 us  [backward(): pl.pallas_call(functools.partial(backward_kernel, heads, planes, groups),...]
    reduce_sum x21 -> x0, other arithmetic: 9.56 us -> none  [the longest x1 1.33 us: fast_shards(): d_w_down = jnp.sum(gd_in.astype(F32), axis=1).reshape(-1, width)]
    select_n x7 -> x0, other arithmetic: 7.05 us -> none  [the longest x1 6.27 us: fast_shards(): meta = jnp.where(lane == 2 * k + 1, task_mark[k][:, None], meta)]
    pallas_call x2 -> x1, Pallas kernels: 9.04 us -> 3.3 us  [pick_rows(): pl.pallas_call(pick_rows_kernel, out_shape=tuple((jax.ShapeDtypeStruct(ar...]
where the time goes in v3:
time: 406 us; the launch traced here: 408 us
  Pallas kernels  389 us (96%)
  local copies, waits for them, and re-layouts  10.7 us (3%)
  matrix products  4.32 us (1%)
    pallas_call x1, Pallas kernels, backward(): pl.pallas_call(functools.partial(backward_kernel, heads, planes, groups),...  204 us
    pallas_call x1, Pallas kernels, forward(): pl.pallas_call(functools.partial(forward_kernel, heads, planes, capacity)...  141 us
    pallas_call x1, Pallas kernels, experts(): pl.pallas_call(expert_kernel, out_shape=(sd((total, width), BF16), sd((to...  40.7 us

profile of v3, /device:TPU:25, one launch (start us, length us, event | category | flops | bytes accessed | tf_op | source)
XLA Modules:
  0.0 407.7 jit_solution(1062641343285790009)
XLA Ops:
  0.6 0.0 copy-start
  0.7 1.4 copy.35.te_ref
  2.0 0.0 copy-done
  2.0 1.5 fusion.5.logit_ref
  3.5 1.3 fusion.4.shard_norms
  4.8 141.3 %attention_forward.1 = (f32[8,4,48,128]{3,2,1,0:T(8,128)}, f32[2,32,256]{2,1,0:T(8,128)}, f32[8,128]{1,0:T(8,128)}, s32[8,128]{1,0:T(8,128)}, f32[8,512]{1,0:T(8...) custom-call(s32[4,8]{1,0:T(4,128)} %sent_ref.1, ...), custom_call_target="tpu_custom_call" | custom-call | flops 40000000000 | bytes 10000000 | tf_op jit(solution)/shard_map/attention_forward/pallas_call | solution.py:1205
  146.1 40.7 %experts.1 = (bf16[8192,512]{1,0:T(8,128)(2,1)}, bf16[8192,512]{1,0:T(8,128)(2,1)}, bf16[4,2,128,1024]{3,2,1,0:T(8,128)(2,1)}, bf16[4,2,256,512]{3,2,1,0:T(8,128)(2,1)}, f32[32,128]{1,0:T(8,128)}) custom-call(f32[2,32,256]{2,1,0:T(8,128)} %get-tuple-element.61.marks_ref, f32[8,128]{1,0:T(8,128)} %get-tuple-element.62.gates_ref, ...), custom_call_target="tpu_custom_call" | custom-call | flops 60000002048 | bytes 40000000 | tf_op jit(solution)/shard_map/experts/pallas_call | solution.py:2161
  186.8 0.0 copy-start.5
  186.9 203.9 %attention_backward.1 = (bf16[4,256,512]{2,1,0:T(8,128)(2,1)}, bf16[4,256,512]{2,1,0:T(8,128)(2,1)}, f32[16,1536]{1,0:T(8,128)}, f32[16,512]{1,0:T(8,128)}, f32[...) custom-call(bf16[4,256,512]{2,1,0:T(8,128)(2,1)} %get-tuple-element., ...), custom_call_target="tpu_custom_call" | custom-call | flops 80000000000 | bytes 20000000 | tf_op jit(solution)/shard_map/attention_backward/pallas_call | solution.py:1810
  390.8 3.3 row_order.1
  394.1 0.7 reshape.74
  394.8 0.1 constant_dynamic-slice_fusion
  394.8 0.5 slice_bitcast_fusion
  395.4 1.5 slice_reduce_fusion
  396.8 0.0 copy-done.5
  396.8 1.5 fusion.1
  398.3 1.4 convolution_bitcast_fusion
  399.7 1.6 reshape.80
  401.3 0.0 copy-start.2
  401.3 0.0 copy-start.3
  401.3 0.0 copy-start.4
  401.3 0.0 copy-start.6
  401.3 0.8 copy.37
  402.1 1.8 reshape.78
  403.9 0.0 copy-done.1
  403.9 1.1 bitcast_convert_fusion
  405.0 0.0 copy-done.2
  405.0 0.6 copy.43
  405.7 0.0 copy-done.3
  405.7 0.6 copy.44
  406.3 0.6 copy.45
  406.9 0.5 copy.46
  (3 shorter events, 0.0 us)
Async XLA Ops:
  0.6 1.4 copy-start
  186.8 210.0 %copy-start.5 = (bf16[16,8]{0,1:T(8,128)(2,1)S(1)}, bf16[16,8]{0,1:T(8,128)(2,1)}, u32[]{:S(2)}) copy-start(bf16[16,8]{0,1:T(8,128)(2,1)} %param.31) | copy-start | bytes 772
  399.7 4.2 %copy-start.1 = (bf16[2,256,512]{2,1,0:T(8,128)(2,1)S(1)}, bf16[2,256,512]{2,1,0:T(8,128)(2,1)}, u32[]{:S(2)}) copy-start(bf16[2,256,512]{2,1,0:T(8,128)(2,1)} %get-tuple-element.84) | copy-start | bytes 1572868
  401.3 3.8 copy-start.2
  401.3 4.4 %copy-start.3 = (f32[16,512]{1,0:T(8,128)S(1)}, f32[16,512]{1,0:T(8,128)}, u32[]{:S(2)}) copy-start(f32[16,512]{1,0:T(8,128)} %get-tuple-element.109) | copy-start | bytes 98308
  401.3 5.0 %copy-start.4 = (f32[1,512]{1,0:T(1,128)S(1)}, f32[1,512]{1,0:T(1,128)}, u32[]{:S(2)}) copy-start(f32[1,512]{1,0:T(1,128)} %get-tuple-element.115) | copy-start | bytes 6148
  401.3 5.6 %copy-start.6 = (f32[1,128]{1,0:T(1,128)S(1)}, f32[1,128]{1,0:T(1,128)}, u32[]{:S(2)}) copy-start(f32[1,128]{1,0:T(1,128)} %get-tuple-element.117) | copy-start | bytes 1540
